TPU v7x, 32 devices: a whole 2x2x4 slice. The times are simulated.
32 devices in a mesh: runs: 2 (over y), gx: 4 (over z), gy: 4 (over x, core).
Axes of the slice: x: 2, y: 2, z: 4, core: 2. Of those that a mesh axis runs over, the one named last changes fastest.
Arguments:
- offsets: float32 [1024, 3, 128], P(('runs', 'gx', 'gy')), parts along dimension 0, may hold values from 0.5 to 1.5
- cell_index: int32 [1024, 128], P(('runs', 'gx', 'gy')), parts along dimension 0, may hold values from 0 to 23
- velocity: float32 [1024, 3, 128], P(('runs', 'gx', 'gy')), parts along dimension 0, may hold values from -6 to 6
- affine: float32 [1024, 9, 128], P(('runs', 'gx', 'gy')), parts along dimension 0, may hold values from -3 to 3
- strain: float32 [1024, 9, 128], P(('runs', 'gx', 'gy')), parts along dimension 0, may hold values from -0.1 to 0.1
- particle_mass: float32 [1024, 128], P(('runs', 'gx', 'gy')), parts along dimension 0, may hold values from 0.5 to 2
- owner_row: int32 [1024, 1], P(('runs', 'gx', 'gy')), parts along dimension 0, may hold values from 0 to 3; in each aligned block of 32 rows (0 to 31, 32 to 63, ...) at most 24 rows name the same one
- anchor_xy: int32 [1024, 2], P(('runs', 'gx', 'gy')), parts along dimension 0, may hold values from -2 to 14
- anchor_z: int32 [1024], P(('runs', 'gx', 'gy')), parts along dimension 0, may hold values from 0 to 120
Outputs:
- final_velocity: float32 [1024, 3, 128], P(('runs', 'gx', 'gy')), parts along dimension 0
- final_affine: float32 [1024, 9, 128], P(('runs', 'gx', 'gy')), parts along dimension 0
- final_deform: float32 [1024, 9, 128], P(('runs', 'gx', 'gy')), parts along dimension 0
There are 2 independent parts, one for each index of `runs`. A program takes and returns all parts, laid end to end along the dimension named above; each array names one. Nothing has to cross between parts.
Inputs may be any that keep to these rules, and one draw needn't show every extreme that they name: `owner_row`: among the 32 bins of one device, in aligned blocks of 32 bins, at most 24 name the same row.
All inputs are finite; a program needn't handle non-finite values.
Results may differ from a plain program's by a relative error of at most 0.0003.
Values sent between devices are 32-bit elements; how exact they have to be, the bound alone decides.
No kernel may reach another device: no remote copies, remote signals or barrier semaphores. Data moves between devices by JAX's collectives and lax.ppermute only.
A program may use at most 128 MiB of HBM per device.

v0:
```python
import jax
import jax.numpy as jnp
from jax import lax
from jax.sharding import PartitionSpec as P

TILE = 16
CZ = 128
SUBSTEPS = 4


time_step = 0.05
shear_coef = 2.0
bulk_coef = 2.0
gravity = 2.0
mass_floor = 0.25
highest_index = lax.Precision.HIGHEST


def padded(block, sides, width):
    for axis, dim in sides:
        count = lax.axis_size(axis)
        forward = [(i, i + 1) for i in range(count - 1)]
        backward = [(target, source) for source, target in forward]
        low = lax.ppermute(
            lax.slice_in_dim(block, block.shape[dim] - width, None, axis=dim), axis, forward
        )
        high = lax.ppermute(lax.slice_in_dim(block, 0, width, axis=dim), axis, backward)
        block = jnp.concatenate([low, block, high], axis=dim)
    return block


def node_grid():
    serial = jnp.arange(128, dtype=jnp.int32)
    return jnp.stack([serial // 32, serial // 8 % 4, serial % 8])


def axis_weights(fraction, base_cell, extent):
    offsets_of = jnp.arange(extent, dtype=jnp.int32)[None, None, :] - base_cell[:, :, None]
    lower = 0.5 * (1.5 - fraction) ** 2
    middle = 0.75 - (fraction - 1.0) ** 2
    upper = 0.5 * (fraction - 0.5) ** 2
    return (
        jnp.where(offsets_of == 0, lower[:, :, None], 0.0)
        + jnp.where(offsets_of == 1, middle[:, :, None], 0.0)
        + jnp.where(offsets_of == 2, upper[:, :, None], 0.0)
    )


def stencil(offsets, cell_index):
    base_cell = jnp.stack([cell_index // 12, cell_index // 6 % 2, cell_index % 6], axis=1)
    weight_x = axis_weights(offsets[:, 0], base_cell[:, 0], 4)
    weight_y = axis_weights(offsets[:, 1], base_cell[:, 1], 4)
    weight_z = axis_weights(offsets[:, 2], base_cell[:, 2], 8)
    kernel_weight = (
        weight_x[:, :, :, None, None]
        * weight_y[:, :, None, :, None]
        * weight_z[:, :, None, None, :]
    )
    kernel_weight = kernel_weight.reshape(offsets.shape[0], 128, 128)
    position = base_cell.astype(jnp.float32) + offsets
    return (kernel_weight, position)


def kirchhoff(deform):
    entries = [[deform[:, 3 * dim_out + dim_in] for dim_in in range(3)] for dim_out in range(3)]
    volume = (
        entries[0][0] * (entries[1][1] * entries[2][2] - entries[1][2] * entries[2][1])
        - entries[0][1] * (entries[1][0] * entries[2][2] - entries[1][2] * entries[2][0])
        + entries[0][2] * (entries[1][0] * entries[2][1] - entries[1][1] * entries[2][0])
    )
    log_volume = jnp.log(volume)
    stress = []
    for dim_out in range(3):
        for dim_in in range(3):
            product = (
                entries[dim_out][0] * entries[dim_in][0]
                + entries[dim_out][1] * entries[dim_in][1]
                + entries[dim_out][2] * entries[dim_in][2]
            )
            diagonal = 1.0 if dim_out == dim_in else 0.0
            stress.append(shear_coef * (product - diagonal) + bulk_coef * log_volume * diagonal)
    return stress


def deposit(kernel_weight, position, velocity, affine, deform, particle_mass):
    stress = kirchhoff(deform)
    blend = [particle_mass * affine[:, entry_at] - stress[entry_at] for entry_at in range(9)]
    pushed = [
        sum((blend[3 * dim_out + dim_in] * position[:, dim_in] for dim_in in range(3)))
        for dim_out in range(3)
    ]
    columns = (
        [particle_mass]
        + [particle_mass * velocity[:, dim_out] - pushed[dim_out] for dim_out in range(3)]
        + blend
    )
    source_rank = jnp.stack(columns, axis=1)
    moment_sums = jnp.einsum("axf,afg->xag", source_rank, kernel_weight, precision=highest_index)
    coords = node_grid().astype(jnp.float32)
    momentum = [
        moment_sums[1 + dim_out]
        + sum((moment_sums[4 + 3 * dim_out + dim_in] * coords[dim_in] for dim_in in range(3)))
        for dim_out in range(3)
    ]
    return jnp.stack([moment_sums[0]] + momentum, axis=0)


def collect(kernel_weight, position, offsets, deform, node_velocity):
    coords = node_grid().astype(jnp.float32)
    field_channels = [node_velocity[dim_out] for dim_out in range(3)] + [
        node_velocity[dim_out] * coords[dim_in] for dim_out in range(3) for dim_in in range(3)
    ]
    gathered_rows = jnp.einsum(
        "ejf,jvf->ejv", jnp.stack(field_channels, axis=0), kernel_weight, precision=highest_index
    )
    velocity = [gathered_rows[dim_out] for dim_out in range(3)]
    affine = [
        4.0 * (gathered_rows[3 + 3 * dim_out + dim_in] - velocity[dim_out] * position[:, dim_in])
        for dim_out in range(3)
        for dim_in in range(3)
    ]
    deform_next = [
        deform[:, 3 * dim_out + dim_in]
        + time_step
        * sum(
            (
                affine[3 * dim_out + dim_mid] * deform[:, 3 * dim_mid + dim_in]
                for dim_mid in range(3)
            )
        )
        for dim_out in range(3)
        for dim_in in range(3)
    ]
    offsets_next = offsets + time_step * jnp.stack(velocity, axis=1)
    return (
        jnp.stack(velocity, axis=1),
        jnp.stack(affine, axis=1),
        jnp.stack(deform_next, axis=1),
        offsets_next,
    )


def grid_velocity(node_sums, start_x, start_y, total_x, total_y):
    grid_shape = node_sums.shape[1:]
    coord_x = start_x + lax.broadcasted_iota(jnp.int32, grid_shape, 0)
    coord_y = start_y + lax.broadcasted_iota(jnp.int32, grid_shape, 1)
    coord_z = lax.broadcasted_iota(jnp.int32, grid_shape, 2)
    divisor = jnp.maximum(node_sums[0], mass_floor)
    inside_x = (coord_x >= 2) & (coord_x < total_x - 2)
    inside_y = (coord_y >= 2) & (coord_y < total_y - 2)
    inside_z = (coord_z >= 2) & (coord_z < grid_shape[2] - 2)
    velocity_x = jnp.where(inside_x, node_sums[1] / divisor, 0.0)
    velocity_y = jnp.where(inside_y, node_sums[2] / divisor, 0.0)
    velocity_z = jnp.where(inside_z, node_sums[3] / divisor - time_step * gravity, 0.0)
    return jnp.stack([velocity_x, velocity_y, velocity_z], axis=0)


def fold_ghosts(rimmed, axis_at):
    interior = rimmed.shape[axis_at] - 8
    inner_part = lax.slice_in_dim(rimmed, 4, interior + 4, axis=axis_at)
    lower_border = lax.slice_in_dim(rimmed, 0, 2, axis=axis_at)
    high_rim = lax.slice_in_dim(rimmed, interior + 6, interior + 8, axis=axis_at)
    low_spec = [(0, 0)] * rimmed.ndim
    high_spec = [(0, 0)] * rimmed.ndim
    low_spec[axis_at] = (0, interior - 2)
    high_spec[axis_at] = (interior - 2, 0)
    return inner_part + jnp.pad(lower_border, low_spec) + jnp.pad(high_rim, high_spec)


def shards(
    offsets, cell_index, velocity, affine, strain, particle_mass, owner_row, anchor_xy, anchor_z
):
    groups = lax.axis_size("gx")
    bins_here = offsets.shape[0]
    most_per = max(2, 3 * bins_here // groups)
    slot_total = groups * most_per
    start_x = lax.axis_index("gx") * TILE
    start_y = lax.axis_index("gy") * TILE
    total_x = TILE * groups
    total_y = TILE * lax.axis_size("gy")
    target = owner_row[:, 0]
    chosen = (target[:, None] == jnp.arange(groups, dtype=jnp.int32)[None, :]).astype(jnp.float32)
    earlier = jnp.tril(jnp.ones((bins_here, bins_here), jnp.float32), -1)
    ahead_of = jnp.dot(earlier, chosen, precision=highest_index)
    rank_in = jnp.sum(ahead_of * chosen, axis=1).astype(jnp.int32)
    slot_of = target * most_per + rank_in
    anchor = jnp.concatenate(
        [anchor_xy, anchor_z[:, None], jnp.ones((bins_here, 1), jnp.int32)], axis=1
    )
    identity = jnp.eye(3, dtype=jnp.float32).reshape(1, 9, 1)
    deform = strain + identity
    placed = lax.all_to_all(
        jnp.zeros((slot_total, 4), jnp.int32).at[slot_of].set(anchor),
        "gx",
        split_axis=0,
        concat_axis=0,
        tiled=True,
    )
    span = TILE + 4
    corner = jnp.arange(4, dtype=jnp.int32)
    span_line = jnp.arange(span, dtype=jnp.int32)
    along_x = (
        (placed[:, 0:1] + 2 + corner[None, :])[:, :, None] == span_line[None, None, :]
    ).astype(jnp.float32)
    along_y = (
        (placed[:, 1:2] + 2 + corner[None, :])[:, :, None] == span_line[None, None, :]
    ).astype(jnp.float32)
    depth = jnp.arange(8, dtype=jnp.int32)
    along_z = (
        (placed[:, 2:3] + depth[None, :])[:, :, None]
        == jnp.arange(CZ, dtype=jnp.int32)[None, None, :]
    ).astype(jnp.float32)
    selector = (along_x, along_y, along_z)
    for substep in range(SUBSTEPS):
        kernel_weight, position = stencil(offsets, cell_index)
        patches = deposit(kernel_weight, position, velocity, affine, deform, particle_mass)
        outgoing = jnp.zeros((4, slot_total, 128), jnp.float32).at[:, slot_of].set(patches)
        incoming = lax.all_to_all(outgoing, "gx", split_axis=1, concat_axis=1, tiled=True)
        grid_along_x, grid_along_y, grid_along_z = selector
        slots = incoming.shape[1]
        boxes = incoming.reshape(4, slots, 4, 4, 8)
        spread = jnp.einsum("csijk,skz->csijz", boxes, grid_along_z, precision=highest_index)
        spread = jnp.einsum("csijz,sjy->csiyz", spread, grid_along_y, precision=highest_index)
        extended = jnp.einsum("csiyz,six->cxyz", spread, grid_along_x, precision=highest_index)
        rimmed = padded(extended, (("gx", 1), ("gy", 2)), 2)
        node_sums = fold_ghosts(fold_ghosts(rimmed, 1), 2)
        node_velocity = grid_velocity(node_sums, start_x, start_y, total_x, total_y)
        framed = padded(node_velocity, (("gx", 1), ("gy", 2)), 2)
        picked = jnp.einsum("cxyz,six->csiyz", framed, grid_along_x, precision=highest_index)
        picked = jnp.einsum("csiyz,sjy->csijz", picked, grid_along_y, precision=highest_index)
        picked = jnp.einsum("csijz,skz->csijk", picked, grid_along_z, precision=highest_index)
        node_patch = picked.reshape(3, slots, 128)
        returned = lax.all_to_all(node_patch, "gx", split_axis=1, concat_axis=1, tiled=True)
        velocity, affine, deform, offsets = collect(
            kernel_weight, position, offsets, deform, returned[:, slot_of]
        )
    return (velocity, affine, deform)


def solution(mesh):
    in_specs = (
        P(("runs", "gx", "gy"), None, None),
        P(("runs", "gx", "gy"), None),
        P(("runs", "gx", "gy"), None, None),
        P(("runs", "gx", "gy"), None, None),
        P(("runs", "gx", "gy"), None, None),
        P(("runs", "gx", "gy"), None),
        P(("runs", "gx", "gy"), None),
        P(("runs", "gx", "gy"), None),
        P(("runs", "gx", "gy")),
    )
    out_specs = (
        P(("runs", "gx", "gy"), None, None),
        P(("runs", "gx", "gy"), None, None),
        P(("runs", "gx", "gy"), None, None),
    )
    return jax.shard_map(shards, mesh=mesh, in_specs=in_specs, out_specs=out_specs, check_vma=False)
```

profile of v0, /device:TPU:1, one launch (start us, length us, event | category | flops | bytes accessed | tf_op | source)
XLA Modules:
  0.0 534.6 jit_solution(17248274694388742843)
XLA Ops:
  4.6 5.4 %all-to-all-start = ((s32[4,24,4]{1,2,0:T(4,128)}), s32[4,24,4]{1,2,0:T(4,128)S(1)}, u32[]{:S(2)}, u32[]{:S(2)}) async-start(s32[4,24,4]{1,2,0:T(4,128)} %copy.175), calls=%async_computation | async-start | bytes 16384 | tf_op jit(solution)/shard_map/all_to_all | solution.py:192
  24.7 4.5 all-to-all-start.1
  29.5 4.9 all-to-all-done.1
  37.4 5.2 fusion.133
  42.6 10.2 %convolution_bitcast_fusion.3 = f32[4,96,4,20,128]{4,3,2,0,1:T(8,128)S(1)} fusion(f32[96,128,4,4,4]{1,4,3,2,0:T(4,128)S(1)} %fusion.133, s32[96,4]{1,0:T(8,128)S(1)} %iota_add_fusion), kind=kOutput, calls=%fused_computation.28 | convolution fusion | flops 188751360 | bytes 18875904 | tf_op jit(solution)/shard_map/csijz,sjy->csiyz/dot_general | solution.py:223
  52.8 14.4 %fusion.40 = f32[4,20,20,128]{3,1,2,0:T(8,128)S(1)} fusion(f32[4,96,4,20,128]{4,3,2,0,1:T(8,128)S(1)} %convolution_bitcast_fusion.3, s32[96,4]{0,1:T(4,128)S(1)} %iota_add_fusion.2), kind=kOutput, calls=%fused_computation.49 | convolution fusion | flops 943726080 | bytes 16549376 | tf_op jit(solution)/shard_map/csiyz,six->cxyz/dot_general | solution.py:224
  75.7 7.1 %collective-permute-start.2 = (f32[4,24,2,128]{3,1,2,0:T(8,128)S(1)}, f32[4,24,2,128]{3,1,2,0:T(8,128)S(1)}, u32[]{:S(2)}, u32[]{:S(2)}) collective-permute-start(f32[4,24,2,128]{3,1,2,0:T(8,128)S(1)} %get-tuple-element.170), channel_id=1, source_target_pairs={{0,1},{1,2},{2,3},{4,5},{5,6},{6,7},{8,9},{9,10},{10,11},{12,13},{... | collective-permute-start | bytes 294920 | tf_op jit(solution)/shard_map/ppermute | solution.py:24
  105.0 4.8 convolution_bitcast_fusion.7
  109.9 16.9 %fusion.14 = f32[96,4,3,4,128]{4,1,3,2,0:T(4,128)S(1)} fusion(f32[3,96,4,20,128]{4,1,3,0,2:T(8,128)S(1)} %convolution_bitcast_fusion.7, s32[96,4]{1,0:T(8,128)S(1)} %iota_add_fusion), kind=kOutput, calls=%fused_computation.23 | convolution fusion | flops 141565440 | bytes 14157312 | tf_op jit(solution)/shard_map/csiyz,sjy->csijz/dot_general | solution.py:230
  137.6 4.7 all-to-all-done.2
  154.6 9.6 %all_to_all.52 = f32[4,96,128]{2,0,1:T(4,128)} all-to-all(f32[4,96,128]{2,0,1:T(4,128)S(1)} %scatter_fusion.1), channel_id=1, replica_groups=mesh['runs'=2,'gx'=4,'gy'=4] {'gx'}, dimensions={1} | all-to-all | bytes 393216 | tf_op jit(solution)/shard_map/all_to_all | solution.py:218
  168.1 5.2 fusion.130
  173.3 10.2 %convolution_bitcast_fusion.2 = f32[4,96,4,20,128]{4,3,2,0,1:T(8,128)S(1)} fusion(f32[96,128,4,4,4]{1,4,3,2,0:T(4,128)S(1)} %fusion.130, s32[96,4]{1,0:T(8,128)S(1)} %iota_add_fusion), kind=kOutput, calls=%fused_computation.27 | convolution fusion | flops 188751360 | bytes 18875904 | tf_op jit(solution)/shard_map/csijz,sjy->csiyz/dot_general | solution.py:223
  183.5 14.4 %fusion.43 = f32[4,20,20,128]{3,1,2,0:T(8,128)S(1)} fusion(f32[4,96,4,20,128]{4,3,2,0,1:T(8,128)S(1)} %convolution_bitcast_fusion.2, s32[96,4]{0,1:T(4,128)S(1)} %iota_add_fusion.2), kind=kOutput, calls=%fused_computation.50 | convolution fusion | flops 943726080 | bytes 16549376 | tf_op jit(solution)/shard_map/csiyz,six->cxyz/dot_general | solution.py:224
  233.0 4.8 convolution_bitcast_fusion.6
  237.8 16.9 %fusion.12 = f32[96,4,3,4,128]{4,1,3,2,0:T(4,128)S(1)} fusion(f32[3,96,4,20,128]{4,1,3,0,2:T(8,128)S(1)} %convolution_bitcast_fusion.6, s32[96,4]{1,0:T(8,128)S(1)} %iota_add_fusion), kind=kOutput, calls=%fused_computation.21 | convolution fusion | flops 141565440 | bytes 14157312 | tf_op jit(solution)/shard_map/csiyz,sjy->csijz/dot_general | solution.py:230
  260.4 9.3 %all_to_all.53 = f32[3,96,128]{2,0,1:T(4,128)} all-to-all(f32[3,96,128]{2,0,1:T(4,128)S(1)} %copy.205), channel_id=1, replica_groups=mesh['runs'=2,'gx'=4,'gy'=4] {'gx'}, dimensions={1} | all-to-all | bytes 294912 | tf_op jit(solution)/shard_map/all_to_all | solution.py:233
  284.1 9.1 %all_to_all.54 = f32[4,96,128]{2,0,1:T(4,128)S(1)} all-to-all(f32[4,96,128]{2,0,1:T(4,128)S(1)} %scatter_fusion.2), channel_id=1, replica_groups=mesh['runs'=2,'gx'=4,'gy'=4] {'gx'}, dimensions={1} | all-to-all | bytes 393216 | tf_op jit(solution)/shard_map/all_to_all | solution.py:218
  294.1 4.2 copy.211
  298.3 5.2 fusion.127
  303.4 10.2 %convolution_bitcast_fusion.1 = f32[4,96,4,20,128]{4,3,2,0,1:T(8,128)S(1)} fusion(f32[96,128,4,4,4]{1,4,3,2,0:T(4,128)S(1)} %fusion.127, s32[96,4]{1,0:T(8,128)S(1)} %iota_add_fusion), kind=kOutput, calls=%fused_computation.26 | convolution fusion | flops 188751360 | bytes 18875904 | tf_op jit(solution)/shard_map/csijz,sjy->csiyz/dot_general | solution.py:223
  313.7 14.4 %fusion.46 = f32[4,20,20,128]{3,1,2,0:T(8,128)S(1)} fusion(f32[4,96,4,20,128]{4,3,2,0,1:T(8,128)S(1)} %convolution_bitcast_fusion.1, s32[96,4]{0,1:T(4,128)S(1)} %iota_add_fusion.2), kind=kOutput, calls=%fused_computation.51 | convolution fusion | flops 943726080 | bytes 16549376 | tf_op jit(solution)/shard_map/csiyz,six->cxyz/dot_general | solution.py:224
  363.2 4.8 convolution_bitcast_fusion.5
  368.0 16.9 %fusion.10 = f32[96,4,3,4,128]{4,1,3,2,0:T(4,128)S(1)} fusion(f32[3,96,4,20,128]{4,1,3,0,2:T(8,128)S(1)} %convolution_bitcast_fusion.5, s32[96,4]{1,0:T(8,128)S(1)} %iota_add_fusion), kind=kOutput, calls=%fused_computation.19 | convolution fusion | flops 141565440 | bytes 14157312 | tf_op jit(solution)/shard_map/csiyz,sjy->csijz/dot_general | solution.py:230
  390.5 8.5 %all_to_all.55 = f32[3,96,128]{2,0,1:T(4,128)S(1)} all-to-all(f32[3,96,128]{2,0,1:T(4,128)S(1)} %copy.215), channel_id=1, replica_groups=mesh['runs'=2,'gx'=4,'gy'=4] {'gx'}, dimensions={1} | all-to-all | bytes 294912 | tf_op jit(solution)/shard_map/all_to_all | solution.py:233
  412.2 9.8 %all_to_all.56 = f32[4,96,128]{2,0,1:T(4,128)} all-to-all(f32[4,96,128]{2,0,1:T(4,128)S(1)} %scatter_fusion.3), channel_id=1, replica_groups=mesh['runs'=2,'gx'=4,'gy'=4] {'gx'}, dimensions={1} | all-to-all | bytes 393216 | tf_op jit(solution)/shard_map/all_to_all | solution.py:218
  428.0 5.2 fusion.124
  433.1 10.2 %convolution_bitcast_fusion = f32[4,96,4,20,128]{4,3,2,0,1:T(8,128)S(1)} fusion(f32[96,128,4,4,4]{1,4,3,2,0:T(4,128)S(1)} %fusion.124, s32[96,4]{1,0:T(8,128)S(1)} %iota_add_fusion), kind=kOutput, calls=%fused_computation.25 | convolution fusion | flops 188751360 | bytes 18875904 | tf_op jit(solution)/shard_map/csijz,sjy->csiyz/dot_general | solution.py:223
  443.4 14.4 %fusion.49 = f32[4,20,20,128]{3,1,2,0:T(8,128)S(1)} fusion(f32[4,96,4,20,128]{4,3,2,0,1:T(8,128)S(1)} %convolution_bitcast_fusion, s32[96,4]{0,1:T(4,128)S(1)} %iota_add_fusion.2), kind=kOutput, calls=%fused_computation.52 | convolution fusion | flops 943726080 | bytes 16549376 | tf_op jit(solution)/shard_map/csiyz,six->cxyz/dot_general | solution.py:224
  492.8 4.8 convolution_bitcast_fusion.4
  497.7 16.9 %fusion.8 = f32[96,4,3,4,128]{4,1,3,2,0:T(4,128)S(1)} fusion(f32[3,96,4,20,128]{4,1,3,0,2:T(8,128)S(1)} %convolution_bitcast_fusion.4, s32[96,4]{1,0:T(8,128)S(1)} %iota_add_fusion), kind=kOutput, calls=%fused_computation.17 | convolution fusion | flops 141565440 | bytes 14157312 | tf_op jit(solution)/shard_map/csiyz,sjy->csijz/dot_general | solution.py:230
  524.8 5.4 %all-to-all-done.8 = f32[3,96,128]{2,0,1:T(4,128)S(1)} async-done(((f32[3,96,128]{2,0,1:T(4,128)}), f32[3,96,128]{2,0,1:T(4,128)S(1)}, u32[]{:S(2)}, u32[]{:S(2)}) %all-to-all-start.8) | async-done | bytes 147488 | tf_op jit(solution)/shard_map/all_to_all | solution.py:233
  (418 shorter events, 242.7 us)
Async XLA Ops:
  4.6 20.2 %all-to-all-start = ((s32[4,24,4]{1,2,0:T(4,128)}), s32[4,24,4]{1,2,0:T(4,128)S(1)}, u32[]{:S(2)}, u32[]{:S(2)}) async-start(s32[4,24,4]{1,2,0:T(4,128)} %copy.175), calls=%async_computation | async-start | bytes 16384 | tf_op jit(solution)/shard_map/all_to_all | solution.py:192
  24.7 9.7 %all-to-all-start.1 = ((f32[4,96,128]{2,0,1:T(4,128)}), f32[4,96,128]{2,0,1:T(4,128)S(1)}, u32[]{:S(2)}, u32[]{:S(2)}) async-start(f32[4,96,128]{2,0,1:T(4,128)} %scatter_fusion), calls=%async_computation.1 | async-start | bytes 393216 | tf_op jit(solution)/shard_map/all_to_all | solution.py:218
  67.3 4.6 collective-permute-start
  70.4 5.2 collective-permute-start.1
  75.7 9.1 %collective-permute-start.2 = (f32[4,24,2,128]{3,1,2,0:T(8,128)S(1)}, f32[4,24,2,128]{3,1,2,0:T(8,128)S(1)}, u32[]{:S(2)}, u32[]{:S(2)}) collective-permute-start(f32[4,24,2,128]{3,1,2,0:T(8,128)S(1)} %get-tuple-element.170), channel_id=1, source_target_pairs={{0,1},{1,2},{2,3},{4,5},{5,6},{6,7},{8,9},{9,10},{10,11},{12,13},{... | collective-permute-start | bytes 294920 | tf_op jit(solution)/shard_map/ppermute | solution.py:24
  82.8 5.9 %collective-permute-start.3 = (f32[4,24,2,128]{3,1,2,0:T(8,128)S(1)}, f32[4,24,2,128]{3,1,2,0:T(8,128)S(1)}, u32[]{:S(2)}, u32[]{:S(2)}) collective-permute-start(f32[4,24,2,128]{3,1,2,0:T(8,128)S(1)} %get-tuple-element.171), channel_id=1, source_target_pairs={{1,0},{2,1},{3,2},{5,4},{6,5},{7,6},{9,8},{10,9},{11,10},{13,12},{... | collective-permute-start | bytes 294920 | tf_op jit(solution)/shard_map/ppermute | solution.py:27
  91.2 4.8 collective-permute-start.5
  96.1 5.2 collective-permute-start.6
  99.4 5.7 %collective-permute-start.7 = (f32[3,20,2,128]{3,1,2,0:T(8,128)S(1)}, f32[3,20,2,128]{3,1,2,0:T(8,128)S(1)}, u32[]{:S(2)}, u32[]{:S(2)}) collective-permute-start(f32[3,20,2,128]{3,1,2,0:T(8,128)S(1)} %get-tuple-element.199), channel_id=1, source_target_pairs={{1,0},{2,1},{3,2},{5,4},{6,5},{7,6},{9,8},{10,9},{11,10},{13,12},{... | collective-permute-start | bytes 184328 | tf_op jit(solution)/shard_map/ppermute | solution.py:27
  133.1 9.3 %all-to-all-start.2 = ((f32[3,96,128]{2,0,1:T(4,128)}), f32[3,96,128]{2,0,1:T(4,128)S(1)}, u32[]{:S(2)}, u32[]{:S(2)}) async-start(f32[3,96,128]{2,0,1:T(4,128)} %copy.195), calls=%async_computation.2 | async-start | bytes 393216 | tf_op jit(solution)/shard_map/all_to_all | solution.py:233
  198.0 4.2 collective-permute-start.8
  200.1 6.2 %collective-permute-start.9 = (f32[4,2,20,128]{3,1,2,0:T(2,128)S(1)}, f32[4,2,20,128]{3,1,2,0:T(2,128)S(1)}, u32[]{:S(2)}, u32[]{:S(2)}) collective-permute-start(f32[4,2,20,128]{3,1,2,0:T(2,128)S(1)} %get-tuple-element.177), channel_id=1, source_target_pairs={{4,0},{8,4},{12,8},{5,1},{9,5},{13,9},{6,2},{10,6},{14,10},{7,3},{... | collective-permute-start | bytes 245768 | tf_op jit(solution)/shard_map/ppermute | solution.py:27
  206.3 5.8 %collective-permute-start.10 = (f32[4,24,2,128]{3,1,2,0:T(8,128)S(1)}, f32[4,24,2,128]{3,1,2,0:T(8,128)S(1)}, u32[]{:S(2)}, u32[]{:S(2)}) collective-permute-start(f32[4,24,2,128]{3,1,2,0:T(8,128)S(1)} %get-tuple-element.168), channel_id=1, source_target_pairs={{0,1},{1,2},{2,3},{4,5},{5,6},{6,7},{8,9},{9,10},{10,11},{12,13},{... | collective-permute-start | bytes 294920 | tf_op jit(solution)/shard_map/ppermute | solution.py:24
  210.2 5.9 %collective-permute-start.11 = (f32[4,24,2,128]{3,1,2,0:T(8,128)S(1)}, f32[4,24,2,128]{3,1,2,0:T(8,128)S(1)}, u32[]{:S(2)}, u32[]{:S(2)}) collective-permute-start(f32[4,24,2,128]{3,1,2,0:T(8,128)S(1)} %get-tuple-element.169), channel_id=1, source_target_pairs={{1,0},{2,1},{3,2},{5,4},{6,5},{7,6},{9,8},{10,9},{11,10},{13,12},{... | collective-permute-start | bytes 294920 | tf_op jit(solution)/shard_map/ppermute | solution.py:27
  219.2 4.8 collective-permute-start.13
  224.1 5.2 collective-permute-start.14
  227.3 5.7 %collective-permute-start.15 = (f32[3,20,2,128]{3,1,2,0:T(8,128)S(1)}, f32[3,20,2,128]{3,1,2,0:T(8,128)S(1)}, u32[]{:S(2)}, u32[]{:S(2)}) collective-permute-start(f32[3,20,2,128]{3,1,2,0:T(8,128)S(1)} %get-tuple-element.197), channel_id=1, source_target_pairs={{1,0},{2,1},{3,2},{5,4},{6,5},{7,6},{9,8},{10,9},{11,10},{13,12},{... | collective-permute-start | bytes 184328 | tf_op jit(solution)/shard_map/ppermute | solution.py:27
  328.2 4.1 collective-permute-start.16
  330.2 5.9 %collective-permute-start.17 = (f32[4,2,20,128]{3,1,2,0:T(2,128)S(1)}, f32[4,2,20,128]{3,1,2,0:T(2,128)S(1)}, u32[]{:S(2)}, u32[]{:S(2)}) collective-permute-start(f32[4,2,20,128]{3,1,2,0:T(2,128)S(1)} %get-tuple-element.175), channel_id=1, source_target_pairs={{4,0},{8,4},{12,8},{5,1},{9,5},{13,9},{6,2},{10,6},{14,10},{7,3},{... | collective-permute-start | bytes 245768 | tf_op jit(solution)/shard_map/ppermute | solution.py:27
  336.2 6.1 %collective-permute-start.18 = (f32[4,24,2,128]{3,1,2,0:T(8,128)S(1)}, f32[4,24,2,128]{3,1,2,0:T(8,128)S(1)}, u32[]{:S(2)}, u32[]{:S(2)}) collective-permute-start(f32[4,24,2,128]{3,1,2,0:T(8,128)S(1)} %get-tuple-element.166), channel_id=1, source_target_pairs={{0,1},{1,2},{2,3},{4,5},{5,6},{6,7},{8,9},{9,10},{10,11},{12,13},{... | collective-permute-start | bytes 294920 | tf_op jit(solution)/shard_map/ppermute | solution.py:24
  340.4 5.9 %collective-permute-start.19 = (f32[4,24,2,128]{3,1,2,0:T(8,128)S(1)}, f32[4,24,2,128]{3,1,2,0:T(8,128)S(1)}, u32[]{:S(2)}, u32[]{:S(2)}) collective-permute-start(f32[4,24,2,128]{3,1,2,0:T(8,128)S(1)} %get-tuple-element.167), channel_id=1, source_target_pairs={{1,0},{2,1},{3,2},{5,4},{6,5},{7,6},{9,8},{10,9},{11,10},{13,12},{... | collective-permute-start | bytes 294920 | tf_op jit(solution)/shard_map/ppermute | solution.py:27
  349.4 4.8 collective-permute-start.21
  354.2 5.2 collective-permute-start.22
  357.5 5.7 %collective-permute-start.23 = (f32[3,20,2,128]{3,1,2,0:T(8,128)S(1)}, f32[3,20,2,128]{3,1,2,0:T(8,128)S(1)}, u32[]{:S(2)}, u32[]{:S(2)}) collective-permute-start(f32[3,20,2,128]{3,1,2,0:T(8,128)S(1)} %get-tuple-element.195), channel_id=1, source_target_pairs={{1,0},{2,1},{3,2},{5,4},{6,5},{7,6},{9,8},{10,9},{11,10},{13,12},{... | collective-permute-start | bytes 184328 | tf_op jit(solution)/shard_map/ppermute | solution.py:27
  457.9 4.1 collective-permute-start.24
  459.9 5.9 %collective-permute-start.25 = (f32[4,2,20,128]{3,1,2,0:T(2,128)S(1)}, f32[4,2,20,128]{3,1,2,0:T(2,128)S(1)}, u32[]{:S(2)}, u32[]{:S(2)}) collective-permute-start(f32[4,2,20,128]{3,1,2,0:T(2,128)S(1)} %get-tuple-element.173), channel_id=1, source_target_pairs={{4,0},{8,4},{12,8},{5,1},{9,5},{13,9},{6,2},{10,6},{14,10},{7,3},{... | collective-permute-start | bytes 245768 | tf_op jit(solution)/shard_map/ppermute | solution.py:27
  465.9 6.7 %collective-permute-start.26 = (f32[4,24,2,128]{3,1,2,0:T(8,128)S(1)}, f32[4,24,2,128]{3,1,2,0:T(8,128)S(1)}, u32[]{:S(2)}, u32[]{:S(2)}) collective-permute-start(f32[4,24,2,128]{3,1,2,0:T(8,128)S(1)} %get-tuple-element.164), channel_id=1, source_target_pairs={{0,1},{1,2},{2,3},{4,5},{5,6},{6,7},{8,9},{9,10},{10,11},{12,13},{... | collective-permute-start | bytes 294920 | tf_op jit(solution)/shard_map/ppermute | solution.py:24
  470.1 5.9 %collective-permute-start.27 = (f32[4,24,2,128]{3,1,2,0:T(8,128)S(1)}, f32[4,24,2,128]{3,1,2,0:T(8,128)S(1)}, u32[]{:S(2)}, u32[]{:S(2)}) collective-permute-start(f32[4,24,2,128]{3,1,2,0:T(8,128)S(1)} %get-tuple-element.165), channel_id=1, source_target_pairs={{1,0},{2,1},{3,2},{5,4},{6,5},{7,6},{9,8},{10,9},{11,10},{13,12},{... | collective-permute-start | bytes 294920 | tf_op jit(solution)/shard_map/ppermute | solution.py:27
  479.0 4.8 collective-permute-start.29
  483.9 5.8 %collective-permute-start.30 = (f32[3,20,2,128]{3,1,2,0:T(8,128)S(1)}, f32[3,20,2,128]{3,1,2,0:T(8,128)S(1)}, u32[]{:S(2)}, u32[]{:S(2)}) collective-permute-start(f32[3,20,2,128]{3,1,2,0:T(8,128)S(1)} %get-tuple-element.192), channel_id=1, source_target_pairs={{0,1},{1,2},{2,3},{4,5},{5,6},{6,7},{8,9},{9,10},{10,11},{12,13},{... | collective-permute-start | bytes 184328 | tf_op jit(solution)/shard_map/ppermute | solution.py:24
  487.2 5.7 %collective-permute-start.31 = (f32[3,20,2,128]{3,1,2,0:T(8,128)S(1)}, f32[3,20,2,128]{3,1,2,0:T(8,128)S(1)}, u32[]{:S(2)}, u32[]{:S(2)}) collective-permute-start(f32[3,20,2,128]{3,1,2,0:T(8,128)S(1)} %get-tuple-element.193), channel_id=1, source_target_pairs={{1,0},{2,1},{3,2},{5,4},{6,5},{7,6},{9,8},{10,9},{11,10},{13,12},{... | collective-permute-start | bytes 184328 | tf_op jit(solution)/shard_map/ppermute | solution.py:27
  521.0 9.2 %all-to-all-start.8 = ((f32[3,96,128]{2,0,1:T(4,128)}), f32[3,96,128]{2,0,1:T(4,128)S(1)}, u32[]{:S(2)}, u32[]{:S(2)}) async-start(f32[3,96,128]{2,0,1:T(4,128)} %copy.225), calls=%async_computation.8 | async-start | bytes 393216 | tf_op jit(solution)/shard_map/all_to_all | solution.py:233
  (72 other events, 967.8 us)
where the time goes:
time: 543 us; the launch traced here: 535 us
  matrix products  244 us (45%)
  starting transfers between devices  93 us (17%)
  waiting for transfers between devices  75.4 us (14%)
  local copies, waits for them, and re-layouts  50.4 us (9%)
  blocking collectives  46.3 us (9%)
  other arithmetic  22.1 us (4%)
    dot_general x4, matrix products, shards(): jnp.einsum('csiyz,sjy->csijz', picked, grid_along_y, precision=highest_in...  67.4 us
    ppermute x16, waiting for transfers between devices, padded(): lax.ppermute(lax.slice_in_dim(block, 0, width, axis=dim), axis, backward)  58.6 us
    dot_general x4, matrix products, shards(): jnp.einsum('csiyz,six->cxyz', spread, grid_along_x, precision=highest_index)  57.8 us
    ppermute x16, starting transfers between devices, padded(): lax.ppermute(lax.slice_in_dim(block, block.shape[dim] - width, None, axis...  49.2 us
    dot_general x4, matrix products, shards(): jnp.einsum('csijz,sjy->csiyz', spread, grid_along_y, precision=highest_in...  40.8 us
    all_to_all x3, blocking collectives, shards(): lax.all_to_all(outgoing, 'gx', split_axis=1, concat_axis=1, tiled=True)  28.5 us
    ppermute x16, starting transfers between devices, padded(): lax.ppermute(lax.slice_in_dim(block, 0, width, axis=dim), axis, backward)  26.4 us
    dot_general x4, matrix products, shards(): jnp.einsum('csijk,skz->csijz', boxes, grid_along_z, precision=highest_index)  20.7 us
  transfers between devices with their start and end apart: 36, of which 22 were waited for; matrix products, arithmetic and copies ran while one was open for 3% of the time, Pallas kernels for 0%

commit v1 on v0

v1 whole, which is shorter than its diff:
```python
import functools

import jax
import jax.numpy as jnp
from jax import lax
from jax.experimental import pallas as pl
from jax.experimental.pallas import tpu as pltpu
from jax.sharding import PartitionSpec as P

TILE = 16
CZ = 128
SUBSTEPS = 4
SPAN_Y = 26
LOW_Y = 5
ROWS_X = 4 * SPAN_Y

time_step = 0.05
shear_coef = 2.0
bulk_coef = 2.0
gravity = 2.0
mass_floor = 0.25

F32 = jnp.float32
BF16 = jnp.bfloat16


def split(value):
    high = value.astype(BF16)
    low = (value - high.astype(F32)).astype(BF16)
    return high, low


def quadratic(f):
    lower = 0.5 * (1.5 - f) ** 2
    middle = 0.75 - (f - 1.0) ** 2
    upper = 0.5 * (f - 0.5) ** 2
    return lower, middle, upper


def row_of(ref, at):
    return jnp.broadcast_to(ref[pl.ds(at, 1), :], (8, 128))


def stencil_rows(group, fractions, bases, params):
    def put(row, value):
        params[pl.ds(group * 128 + row, 8, stride=16), :] = value

    for axis in range(2):
        lower, middle, upper = quadratic(fractions[axis])
        first = bases[axis] < 0.5
        put(4 * axis, jnp.where(first, lower, 0.0))
        put(4 * axis + 1, jnp.where(first, middle, lower))
        put(4 * axis + 2, jnp.where(first, upper, middle))
        put(4 * axis + 3, jnp.where(first, 0.0, upper))
        put(8 + axis, bases[axis] + fractions[axis])
    put(10, fractions[2])
    put(11, bases[2])
    for at, value in enumerate(quadratic(fractions[2])):
        put(12 + at, value)


def depth_weights(bins, params, depth):
    serial = lax.broadcasted_iota(jnp.int32, (8, 128), 0).astype(F32)

    def one(at):
        base = at * 16
        t = serial - row_of(params, base + 11)
        w = jnp.where(
            t == 0.0,
            row_of(params, base + 12),
            jnp.where(
                t == 1.0,
                row_of(params, base + 13),
                jnp.where(t == 2.0, row_of(params, base + 14), 0.0),
            ),
        )
        return jnp.concatenate([w, (t - row_of(params, base + 10)) * w], axis=1)

    def pair(at, _):
        value = jnp.concatenate([one(2 * at), one(2 * at + 1)], axis=0)
        high, low = split(value)
        group = at // 8
        row = pl.multiple_of((at % 8) * 16, 16)
        depth[group, pl.ds(row, 16), :] = high
        depth[group, pl.ds(row + 128, 16), :] = high
        depth[group, pl.ds(row + 256, 16), :] = low
        return _

    lax.fori_loop(0, bins // 2, pair, 0, unroll=4)


def y_patterns(params, base, sub):
    upper_half = sub >= 4
    x1 = row_of(params, base + 9)
    weights = []
    moments = []
    for half in range(2):
        w = jnp.where(
            upper_half, row_of(params, base + 5 + 2 * half), row_of(params, base + 4 + 2 * half)
        )
        j = jnp.where(upper_half, 1.0 + 2 * half, 0.0 + 2 * half)
        weights.append(w)
        moments.append(w * (j - x1))
    return weights, moments


def deposit_rows(group, velocity, affine, deform, mass, blends):
    entries = [[deform[3 * a + b] for b in range(3)] for a in range(3)]
    volume = (
        entries[0][0] * (entries[1][1] * entries[2][2] - entries[1][2] * entries[2][1])
        - entries[0][1] * (entries[1][0] * entries[2][2] - entries[1][2] * entries[2][0])
        + entries[0][2] * (entries[1][0] * entries[2][1] - entries[1][1] * entries[2][0])
    )
    log_volume = jnp.log(volume)

    def put(kind, channel, value):
        for half in range(2):
            blends[pl.ds(group * 256 + kind * 8 + half * 4 + channel, 8, stride=32), :] = value

    zero = jnp.zeros_like(mass)
    put(0, 0, mass)
    for b in range(3):
        put(1 + b, 0, zero)
    for a in range(3):
        put(0, 1 + a, mass * velocity[a])
        for b in range(3):
            product = sum(entries[a][c] * entries[b][c] for c in range(3))
            diagonal = 1.0 if a == b else 0.0
            stress = shear_coef * (product - diagonal) + bulk_coef * log_volume * diagonal
            put(1 + b, 1 + a, mass * affine[3 * a + b] - stress)


def scatter_bins(tabs, own_count, lane, sets, sums):
    at_base = own_count
    total = tabs.shape[0] // 2
    for column, patch_ref in enumerate(sets):
        devices = patch_ref.shape[0]
        groups = own_count // 16

        def block(at, _, patch_ref=patch_ref, at_base=at_base, column=column):
            dev = at // groups
            start = pl.multiple_of((at % groups) * 64, 64)
            first = at_base + at * 16
            for slot in range(16):
                row = tabs[first + slot]
                z = tabs[total + first + slot]

                def add(row=row, z=z, slot=slot):
                    patch = patch_ref[dev, pl.ds(start, 64), :]
                    moved = pltpu.roll(patch, (z + (128 - 8 * slot)) & 127, 1)
                    inside = (lane >= z) & (lane < z + 8)
                    moved = jnp.where(inside, moved, 0.0)
                    for i in range(4):
                        place = pl.ds(row + i * ROWS_X, 16)
                        sums[place, :] = sums[place, :] + moved[16 * i : 16 * i + 16]

                if column == 0:
                    add()
                else:
                    pl.when(row >= 0)(add)
            return _

        lax.fori_loop(0, devices * groups, block, 0)
        at_base = at_base + devices * own_count


def fill(blocks):
    return jnp.concatenate(blocks, axis=0)


def kernel(first, last, total_count, *refs):
    refs = list(refs)
    take = lambda n: [refs.pop(0) for _ in range(n)]
    if first:
        offsets_in, cell, velocity_in, affine_in, strain, mass_in = take(6)
        bins = mass_in.shape[0]
    else:
        tabs, patch_own, patch_a, patch_b, inside_ref, state_in = take(6)
        bins = state_in.shape[1]
    if last:
        velocity_out, affine_out, deform_out = take(3)
    else:
        patch_out, state_out = take(2)
    params, depth, wide, wide_low, products = take(5)
    if not first:
        sums, results = take(2)
    if not last:
        blends, products_low = take(2)
    groups = bins // 16
    sub = lax.broadcasted_iota(jnp.int32, (8, 128), 0)
    lane = lax.broadcasted_iota(jnp.int32, (64, 128), 1)
    lane_row = lax.broadcasted_iota(jnp.int32, (1, 128), 1)

    def load8(g8):
        span = pl.ds(g8 * 8, 8)
        if first:
            fractions = [offsets_in[a, span, :] for a in range(3)]
            c = cell[span, :]
            bx = (c >= 12).astype(jnp.int32)
            c = c - 12 * bx
            by = (c >= 6).astype(jnp.int32)
            bases = [bx.astype(F32), by.astype(F32), (c - 6 * by).astype(F32)]
            deform = [
                strain[e, span, :] + (1.0 if e % 4 == 0 else 0.0) for e in range(9)
            ]
            return fractions, bases, deform, mass_in[span, :]
        fractions = [state_in[a, span, :] for a in range(3)]
        bases = [state_in[3 + a, span, :] for a in range(3)]
        deform = [state_in[7 + e, span, :] for e in range(9)]
        return fractions, bases, deform, state_in[6, span, :]

    def store8(g8, fractions, bases, deform, mass):
        span = pl.ds(g8 * 8, 8)
        for a in range(3):
            state_out[a, span, :] = fractions[a]
            state_out[3 + a, span, :] = bases[a]
        state_out[6, span, :] = mass
        for e in range(9):
            state_out[7 + e, span, :] = deform[e]

    if first:
        for g8 in range(bins // 8):
            span = pl.ds(g8 * 8, 8)
            fractions, bases, deform, mass = load8(g8)
            store8(g8, fractions, bases, deform, mass)
            stencil_rows(g8, fractions, bases, params)
            velocity = [velocity_in[a, span, :] for a in range(3)]
            affine = [affine_in[e, span, :] for e in range(9)]
            deposit_rows(g8, velocity, affine, deform, mass, blends)
    else:
        total = tabs.shape[0] // 2
        for g8 in range(bins // 8):
            fractions, bases, _, _ = load8(g8)
            stencil_rows(g8, fractions, bases, params)
        depth_weights(bins, params, depth)

        def clear(at, _):
            for i in range(4):
                sums[pl.ds(tabs[at] + i * ROWS_X, 16), :] = jnp.zeros((16, 128), F32)
            return _

        lax.fori_loop(0, bins, clear, 0, unroll=4)
        scatter_bins(tabs, bins, lane, [patch_own, patch_a, patch_b], sums)
        for g in range(groups):
            compact = jnp.zeros((64, 128), F32)
            for slot in range(16):
                row = tabs[g * 16 + slot]
                z = tabs[total + g * 16 + slot]
                node = fill([sums[pl.ds(row + i * ROWS_X, 16), :] for i in range(4)])
                moved = pltpu.roll(node, (8 * slot + 128 - z) & 127, 1)
                compact = jnp.where(lane // 8 == slot, moved, compact)
            channel = lax.broadcasted_iota(jnp.int32, (64, 128), 0) & 3
            mass = jnp.where(channel == 0, compact, 0.0)
            mass = mass + pltpu.roll(mass, 1, 0)
            mass = mass + pltpu.roll(mass, 2, 0)
            node = compact / jnp.maximum(mass, mass_floor)
            node = node - jnp.where(channel == 3, time_step * gravity, 0.0)
            node = jnp.where(inside_ref[g] > 0.5, node, 0.0)
            high, low = split(node)
            both = jnp.concatenate([high, low], axis=1)
            for slot in range(16):
                keep = (lane_row // 8 == slot).astype(BF16)
                keep = jnp.concatenate([keep, keep], axis=1)
                wide[64 * slot : 64 * slot + 64, :] = both * keep
            products[...] = jnp.dot(
                wide[...], depth[g, 0:256, :], preferred_element_type=F32
            ) + jnp.dot(wide[:, 0:128], depth[g, 256:384, :], preferred_element_type=F32)

            def finish(slot, _, g=g):
                base = (g * 16 + slot) * 16
                weights, moments = y_patterns(params, base, sub)
                x0 = row_of(params, base + 8)
                at = pl.multiple_of(slot * 64, 64)
                plain = [None, None]
                along = [None, None]
                deep = [None, None]
                for i in range(4):
                    wx = row_of(params, base + i)
                    wxi = wx * (i - x0)
                    for half in range(2):
                        place = pl.ds(at + 16 * i + 8 * half, 8)
                        one = products[place, 0:128]
                        two = products[place, 128:256]
                        terms = (wx * one, wxi * one, wx * two)
                        for kept, term in zip((plain, along, deep), terms):
                            kept[half] = term if i == 0 else kept[half] + term
                found = (
                    weights[0] * plain[0] + weights[1] * plain[1],
                    weights[0] * along[0] + weights[1] * along[1],
                    moments[0] * plain[0] + moments[1] * plain[1],
                    weights[0] * deep[0] + weights[1] * deep[1],
                )
                place = pl.multiple_of((g * 16 + slot) * 32, 32)
                for kind, value in enumerate(found):
                    results[pl.ds(place + 8 * kind, 8), :] = value + pltpu.roll(value, 4, 0)
                return _

            lax.fori_loop(0, 16, finish, 0, unroll=4)

        for g8 in range(bins // 8):
            span = pl.ds(g8 * 8, 8)
            fractions, bases, deform, mass = load8(g8)

            def get(kind, a, g8=g8):
                return results[pl.ds(g8 * 256 + kind * 8 + 1 + a, 8, stride=32), :]

            velocity = [get(0, a) for a in range(3)]
            affine = [4.0 * get(1 + b, a) for a in range(3) for b in range(3)]
            deform = [
                deform[3 * a + b]
                + time_step * sum(affine[3 * a + c] * deform[3 * c + b] for c in range(3))
                for a in range(3)
                for b in range(3)
            ]
            if last:
                for a in range(3):
                    velocity_out[a, span, :] = velocity[a]
                for e in range(9):
                    affine_out[e, span, :] = affine[e]
                    deform_out[e, span, :] = deform[e]
            else:
                fractions = [fractions[a] + time_step * velocity[a] for a in range(3)]
                store8(g8, fractions, bases, deform, mass)
                stencil_rows(g8, fractions, bases, params)
                deposit_rows(g8, velocity, affine, deform, mass, blends)

    if not last:
        depth_weights(bins, params, depth)
        for g in range(groups):

            def build(slot, _, g=g):
                base = (g * 16 + slot) * 16
                place = pl.multiple_of((g * 16 + slot) * 32, 32)
                weights, moments = y_patterns(params, base, sub)
                x0 = row_of(params, base + 8)
                pushed, b0, b1, b2 = [blends[pl.ds(place + 8 * k, 8), :] for k in range(4)]
                plain = []
                deep = []
                for i in range(4):
                    wx = row_of(params, base + i)
                    along = (pushed + b0 * (i - x0)) * wx
                    across = b1 * wx
                    depthwise = b2 * wx
                    for half in range(2):
                        plain.append(along * weights[half] + across * moments[half])
                        deep.append(depthwise * weights[half])
                value = jnp.concatenate([fill(plain), fill(deep)], axis=1)
                high, low = split(value)
                at = pl.ds(pl.multiple_of(slot * 64, 64), 64)
                wide[at, :] = high
                wide_low[at, :] = low
                return _

            lax.fori_loop(0, 16, build, 0, unroll=2)
            turned = (((1,), (1,)), ((), ()))
            products[...] = lax.dot_general(
                wide[...], depth[g, 128:384, :], turned, preferred_element_type=F32
            )
            products_low[...] = lax.dot_general(
                wide_low[...], depth[g, 128:256, :], turned, preferred_element_type=F32
            )
            compact = jnp.zeros((64, 128), F32)
            for slot in range(16):
                at = slice(64 * slot, 64 * slot + 64)
                value = products[at, 0:128] + products[at, 128:256] + products_low[at, :]
                compact = jnp.where(lane // 8 == slot, value, compact)
            patch_out[64 * g : 64 * g + 64, :] = compact


def run_kernel(first, last, total_x, bins, operands):
    vmem = pl.BlockSpec(memory_space=pltpu.VMEM)
    smem = pl.BlockSpec(memory_space=pltpu.SMEM)
    shape = lambda *dims: jax.ShapeDtypeStruct(dims, F32)
    if last:
        outs = [shape(3, bins, 128), shape(9, bins, 128), shape(9, bins, 128)]
    else:
        outs = [shape(4 * bins, 128), shape(16, bins, 128)]
    groups = bins // 16
    scratch = [
        pltpu.VMEM((16 * bins, 128), F32),
        pltpu.VMEM((groups, 384, 256), BF16),
        pltpu.VMEM((1024, 256), BF16),
        pltpu.VMEM((1024, 256), BF16),
        pltpu.VMEM((1024, 256), F32),
    ]
    grid_rows = (total_x + 4) * ROWS_X
    if not first:
        scratch += [pltpu.VMEM((grid_rows, 128), F32), pltpu.VMEM((32 * bins, 128), F32)]
    if not last:
        scratch += [pltpu.VMEM((32 * bins, 128), F32), pltpu.VMEM((1024, 128), F32)]
    in_specs = [vmem] * len(operands)
    if not first:
        in_specs[0] = smem
    held = sum(4 * op.size for op in operands) + 512 * grid_rows
    return pl.pallas_call(
        functools.partial(kernel, first, last, bins),
        out_shape=outs,
        in_specs=in_specs,
        out_specs=[vmem] * len(outs),
        scratch_shapes=scratch,
        compiler_params=pltpu.CompilerParams(vmem_limit_bytes=held + (16 << 20)),
    )(*operands)


def column_of(payload):
    count = lax.axis_size("gx")
    if count > 8:
        return lax.all_gather(payload, "gx")
    pieces = [payload]
    for shift in range(1, count):
        pairs = [(i, (i + shift) % count) for i in range(count)]
        pieces.append(lax.ppermute(payload, "gx", pairs))
    return jnp.stack(pieces)


def neighbours_of(column):
    count = lax.axis_size("gy")
    got = []
    for start in range(2):
        pairs = []
        for low in range(start, count - 1, 2):
            pairs += [(low, low + 1), (low + 1, low)]
        got.append(lax.ppermute(column, "gy", pairs) if pairs else jnp.zeros_like(column))
    return got


def shards(
    offsets, cell_index, velocity, affine, strain, particle_mass, owner_row, anchor_xy, anchor_z
):
    bins = offsets.shape[0]
    total_x = TILE * lax.axis_size("gx")
    total_y = TILE * lax.axis_size("gy")
    place_y = lax.axis_index("gy")
    turn = lambda array: jnp.transpose(array, (1, 0, 2))
    corner_x = owner_row[:, 0] * TILE + anchor_xy[:, 0]
    own_row = (corner_x + 2) * ROWS_X + 4 * (anchor_xy[:, 1] + LOW_Y)

    serial = jnp.arange(64, dtype=jnp.int32)[None, :, None]
    group = bins // 16
    spread = lambda values: jnp.repeat(values.reshape(group, 16), 8, axis=1)[:, None, :]
    at_x = spread(corner_x) + serial // 16
    at_y = spread(place_y * TILE + anchor_xy[:, 1]) + serial // 4 % 4
    at_z = spread(anchor_z) + (jnp.arange(128, dtype=jnp.int32) % 8)[None, None, :]
    channel = serial % 4
    at = jnp.where(channel == 1, at_x, jnp.where(channel == 2, at_y, at_z))
    limit = jnp.where(channel == 1, total_x, jnp.where(channel == 2, total_y, CZ))
    in_grid = (at_x >= 0) & (at_x < total_x) & (at_y >= 0) & (at_y < total_y)
    inside = ((at >= 2) & (at < limit - 2) & (channel > 0) & in_grid).astype(F32)

    patch, state = run_kernel(
        True,
        False,
        total_x,
        bins,
        [
            turn(offsets),
            cell_index,
            turn(velocity),
            turn(affine),
            turn(strain),
            particle_mass,
        ],
    )
    facts = jnp.stack(
        [corner_x + 2, anchor_xy[:, 1], anchor_z, jnp.ones((bins,), jnp.int32)]
    ).astype(F32)
    facts = jnp.pad(facts, ((0, 4), (0, 128 - bins)))
    payload = jnp.concatenate([patch, facts], axis=0)
    tabs = None
    for substep in range(SUBSTEPS):
        column = column_of(payload)
        beside = neighbours_of(column)
        if substep == 0:
            even = place_y % 2 == 0
            rows = []
            depths = []
            for at, block in enumerate([column] + beside):
                known = block[:, 4 * bins : 4 * bins + 4, 0:bins].astype(jnp.int32)
                move = (0, jnp.where(even, TILE, -TILE), jnp.where(even, -TILE, TILE))[at]
                y = known[:, 1] + LOW_Y + move
                row = known[:, 0] * ROWS_X + 4 * y
                good = (known[:, 3] > 0) & (y >= 0) & (y <= LOW_Y + TILE + 1)
                rows.append(jnp.where(good, row, -1).reshape(-1))
                depths.append(known[:, 2].reshape(-1))
            tabs = jnp.concatenate([own_row] + rows + [anchor_z] + depths)
        last = substep == SUBSTEPS - 1
        results = run_kernel(
            False, last, total_x, bins, [tabs, column] + beside + [inside, state]
        )
        if not last:
            payload, state = results
    return tuple(turn(array) for array in results)


def solution(mesh):
    wide = P(("runs", "gx", "gy"), None, None)
    flat = P(("runs", "gx", "gy"), None)
    return jax.shard_map(
        shards,
        mesh=mesh,
        in_specs=(wide, flat, wide, wide, wide, flat, flat, flat, P(("runs", "gx", "gy"))),
        out_specs=(wide, wide, wide),
        check_vma=False,
    )
```

time: 543 us -> 123 us (0.23); the launches traced: 535 us -> 123 us
  matrix products: 244 us -> 0 us
  starting transfers between devices: 93 us -> 35.8 us
  Pallas kernels: 0 us -> 49.7 us
  blocking collectives: 46.3 us -> 0 us
  waiting for transfers between devices: 75.4 us -> 29.8 us
  local copies, waits for them, and re-layouts: 50.4 us -> 5.37 us
  other arithmetic: 22.1 us -> 1.1 us
    dot_general x33 -> x0, matrix products: 244 us -> none  [the longest x4 67.4 us: shards(): jnp.einsum('csiyz,sjy->csijz', picked, grid_along_y, precision=highest_in...]
    pallas_call x0 -> x5, Pallas kernels: none -> 49.7 us  [run_kernel(): pl.pallas_call(functools.partial(kernel, first, last, bins), out_shape=ou...]
    all_to_all x5 -> x0, blocking collectives: 46.3 us -> none  [the longest x3 28.5 us: shards(): lax.all_to_all(outgoing, 'gx', split_axis=1, concat_axis=1, tiled=True)]
    ppermute x32 -> x20, starting transfers between devices: 75.6 us -> 35.8 us  [the longest x8 21.3 us: neighbours_of(): lax.ppermute(column, 'gy', pairs)]
    ppermute x32 -> x20, waiting for transfers between devices: 60.4 us -> 29.8 us  [the longest x8 15.6 us: neighbours_of(): lax.ppermute(column, 'gy', pairs)]
    all_to_all x4 -> x0, starting transfers between devices: 17.4 us -> none  [the longest x2 7.48 us: shards(): lax.all_to_all(node_patch, 'gx', split_axis=1, concat_axis=1, tiled=True)]
    reshape x8 -> x1, local copies, waits for them, and re-layouts: 16 us -> 0.08 us  [shards(): values.reshape(group, 16)]
    all_to_all x4 -> x0, waiting for transfers between devices: 15 us -> none  [the longest x2 10.1 us: shards(): lax.all_to_all(node_patch, 'gx', split_axis=1, concat_axis=1, tiled=True)]
  transfers between devices with their start and end apart: 36 -> 20, of which waited for: 22 -> 13; matrix products, arithmetic and copies ran while one was open for 3% -> 1% of each run, Pallas kernels for 0% -> 0%
where the time goes in v1:
time: 123 us
  Pallas kernels  49.7 us (40%)
  starting transfers between devices  35.8 us (29%)
  waiting for transfers between devices  29.8 us (24%)
  local copies, waits for them, and re-layouts  5.37 us (4%)
    pallas_call x5, Pallas kernels, run_kernel(): pl.pallas_call(functools.partial(kernel, first, last, bins), out_shape=ou...  49.7 us
    ppermute x8, starting transfers between devices, neighbours_of(): lax.ppermute(column, 'gy', pairs)  21.3 us
    ppermute x8, waiting for transfers between devices, neighbours_of(): lax.ppermute(column, 'gy', pairs)  15.6 us
    ppermute x12, starting transfers between devices, column_of(): pieces.append(lax.ppermute(payload, 'gx', pairs))  14.5 us
    ppermute x12, waiting for transfers between devices, column_of(): pieces.append(lax.ppermute(payload, 'gx', pairs))  14.2 us
    unnamed x18, local copies, waits for them, and re-layouts  3.48 us
  transfers between devices with their start and end apart: 20, of which 13 were waited for; matrix products, arithmetic and copies ran while one was open for 1% of the time, Pallas kernels for 0%

profile of v1, /device:TPU:1, one launch (start us, length us, event | category | flops | bytes accessed | tf_op | source)
XLA Modules:
  0.0 122.8 jit_solution(9799366575221099927)
XLA Ops:
  2.1 0.9 copy-done
  3.0 0.9 copy-done.1
  3.9 0.8 copy-done.2
  4.7 0.8 copy-done.3
  5.5 2.1 %shard_map.112 = (f32[128,128]{1,0:T(8,128)S(1)}, f32[16,32,128]{2,1,0:T(8,128)S(1)}) custom-call(f32[3,32,128]{2,1,0:T(8,128)S(1)} %bitcast.38, s32[32,128]{1,0:T(8,128)S(1)} %copy-done.4, f32[3,32,128]{2,1,0:T(8,128)S(1)} %bitcast.39, f32[9,32,128]{2,1,0:T(8,128)S(1)} %bitcast.33, f32[9,32,128]{2,1,0:T(8,128)S(1)} %bitcast.34, f32[32,128]{1,0:T(8,128)S(1)} %copy-done.5), custom_call_target="tpu_custom_call" | custom-call | tf_op jit(solution)/shard_map/pallas_call | solution.py:395
  7.7 3.2 %collective-permute-start.1 = (f32[136,128]{1,0:T(8,128)S(1)}, f32[136,128]{1,0:T(8,128)S(1)}, u32[]{:S(2)}, u32[]{:S(2)}) collective-permute-start(f32[136,128]{1,0:T(8,128)S(1)} %get-tuple-element.34), channel_id=1, source_target_pairs={{0,8},{4,12},{8,0},{12,4},{1,9},{5,13},{9,1},{13,5},{2,10},{6,14},... | collective-permute-start | bytes 208904 | tf_op jit(solution)/shard_map/ppermute | solution.py:412
  10.9 1.3 %collective-permute-start = (f32[136,128]{1,0:T(8,128)S(1)}, f32[136,128]{1,0:T(8,128)S(1)}, u32[]{:S(2)}, u32[]{:S(2)}) collective-permute-start(f32[136,128]{1,0:T(8,128)S(1)} %get-tuple-element.34), channel_id=1, source_target_pairs={{0,4},{4,8},{8,12},{12,0},{1,5},{5,9},{9,13},{13,1},{2,6},{6,10},{... | collective-permute-start | bytes 208904 | tf_op jit(solution)/shard_map/ppermute | solution.py:412
  12.2 2.0 %collective-permute-start.2 = (f32[136,128]{1,0:T(8,128)S(1)}, f32[136,128]{1,0:T(8,128)S(1)}, u32[]{:S(2)}, u32[]{:S(2)}) collective-permute-start(f32[136,128]{1,0:T(8,128)S(1)} %get-tuple-element.34), channel_id=1, source_target_pairs={{0,12},{4,0},{8,4},{12,8},{1,13},{5,1},{9,5},{13,9},{2,14},{6,2},{... | collective-permute-start | bytes 208904 | tf_op jit(solution)/shard_map/ppermute | solution.py:412
  15.1 0.8 collective-permute-done
  16.2 5.4 %collective-permute-start.4 = (f32[4,136,128]{2,1,0:T(8,128)S(1)}, f32[4,136,128]{2,1,0:T(8,128)S(1)}, u32[]{:S(2)}, u32[]{:S(2)}) collective-permute-start(f32[4,136,128]{2,1,0:T(8,128)S(1)} %pad_maximum_fusion.refs_1_), channel_id=1, source_target_pairs={{1,2},{2,1},{5,6},{6,5},{9,10},{10,9},{13,14},{14,13},{17,18},{18,... | collective-permute-start | bytes 835592 | tf_op jit(solution)/shard_map/ppermute | solution.py:423
  21.9 3.9 %collective-permute-done.4.refs_3_ = f32[4,136,128]{2,1,0:T(8,128)S(1)} collective-permute-done((f32[4,136,128]{2,1,0:T(8,128)S(1)}, f32[4,136,128]{2,1,0:T(8,128)S(1)}, u32[]{:S(2)}, u32[]{:S(2)}) %collective-permute-start.4) | collective-permute-done | bytes 278560 | tf_op jit(solution)/shard_map/ppermute | solution.py:423
  26.4 12.3 %shard_map.113 = (f32[128,128]{1,0:T(8,128)S(1)}, f32[16,32,128]{2,1,0:T(8,128)S(1)}) custom-call(s32[832]{0:T(1024)S(1)} %concatenate.7.refs_0_, f32[4,136,128]{2,1,0:T(8,128)S(1)} %pad_maximum_fusion.refs_1_, f32[4,136,128]{2,1,0:T(8,128)S(1)} %collective-permute-done.3.refs_2_, f32[4,136,128]{2,1,0:T(8,128)S(1)} %collective-permute-done.4.refs_3_, ...), custom_call_target="tpu_custom_call" | custom-call | tf_op jit(solution)/shard_map/pallas_call | solution.py:395
  38.6 3.0 %collective-permute-start.7 = (f32[128,128]{1,0:T(8,128)S(1)}, f32[128,128]{1,0:T(8,128)S(1)}, u32[]{:S(2)}, u32[]{:S(2)}) collective-permute-start(f32[128,128]{1,0:T(8,128)S(1)} %get-tuple-element.16), channel_id=1, source_target_pairs={{0,12},{4,0},{8,4},{12,8},{1,13},{5,1},{9,5},{13,9},{2,14},{6,2},{... | collective-permute-start | bytes 196616 | tf_op jit(solution)/shard_map/ppermute | solution.py:412
  41.6 0.8 collective-permute-start.5
  42.9 2.9 %collective-permute-done.6 = f32[128,128]{1,0:T(8,128)S(1)} collective-permute-done((f32[128,128]{1,0:T(8,128)S(1)}, f32[128,128]{1,0:T(8,128)S(1)}, u32[]{:S(2)}, u32[]{:S(2)}) %collective-permute-start.6) | collective-permute-done | bytes 65568 | tf_op jit(solution)/shard_map/ppermute | solution.py:412
  46.6 5.2 %collective-permute-start.9 = (f32[4,128,128]{2,1,0:T(8,128)S(1)}, f32[4,128,128]{2,1,0:T(8,128)S(1)}, u32[]{:S(2)}, u32[]{:S(2)}) collective-permute-start(f32[4,128,128]{2,1,0:T(8,128)S(1)} %pad_maximum_fusion.1.refs_1_), channel_id=1, source_target_pairs={{1,2},{2,1},{5,6},{6,5},{9,10},{10,9},{13,14},{14,13},{17,18},{18,... | collective-permute-start | bytes 786440 | tf_op jit(solution)/shard_map/ppermute | solution.py:423
  51.9 4.0 %collective-permute-done.9.refs_3_ = f32[4,128,128]{2,1,0:T(8,128)S(1)} collective-permute-done((f32[4,128,128]{2,1,0:T(8,128)S(1)}, f32[4,128,128]{2,1,0:T(8,128)S(1)}, u32[]{:S(2)}, u32[]{:S(2)}) %collective-permute-start.9) | collective-permute-done | bytes 262176 | tf_op jit(solution)/shard_map/ppermute | solution.py:423
  55.9 12.2 %shard_map.114 = (f32[128,128]{1,0:T(8,128)S(1)}, f32[16,32,128]{2,1,0:T(8,128)S(1)}) custom-call(s32[832]{0:T(1024)S(1)} %concatenate.7.refs_0_, f32[4,128,128]{2,1,0:T(8,128)S(1)} %pad_maximum_fusion.1.refs_1_, f32[4,128,128]{2,1,0:T(8,128)S(1)} %collective-permute-done.8.refs_2_, f32[4,128,128]{2,1,0:T(8,128)S(1)} %collective-permute-done.9.refs_3_, ...), custom_call_target="tpu_custom_call" | custom-call | tf_op jit(solution)/shard_map/pallas_call | solution.py:395
  68.1 0.9 collective-permute-start.12
  69.1 1.4 %collective-permute-start.10 = (f32[128,128]{1,0:T(8,128)S(1)}, f32[128,128]{1,0:T(8,128)S(1)}, u32[]{:S(2)}, u32[]{:S(2)}) collective-permute-start(f32[128,128]{1,0:T(8,128)S(1)} %get-tuple-element.18), channel_id=1, source_target_pairs={{0,4},{4,8},{8,12},{12,0},{1,5},{5,9},{9,13},{13,1},{2,6},{6,10},{... | collective-permute-start | bytes 196616 | tf_op jit(solution)/shard_map/ppermute | solution.py:412
  70.5 2.2 %collective-permute-done.12 = f32[128,128]{1,0:T(8,128)S(1)} collective-permute-done((f32[128,128]{1,0:T(8,128)S(1)}, f32[128,128]{1,0:T(8,128)S(1)}, u32[]{:S(2)}, u32[]{:S(2)}) %collective-permute-start.12) | collective-permute-done | bytes 65568 | tf_op jit(solution)/shard_map/ppermute | solution.py:412
  72.6 2.1 %collective-permute-done.11 = f32[128,128]{1,0:T(8,128)S(1)} collective-permute-done((f32[128,128]{1,0:T(8,128)S(1)}, f32[128,128]{1,0:T(8,128)S(1)}, u32[]{:S(2)}, u32[]{:S(2)}) %collective-permute-start.11) | collective-permute-done | bytes 65568 | tf_op jit(solution)/shard_map/ppermute | solution.py:412
  74.7 5.2 %collective-permute-start.14 = (f32[4,128,128]{2,1,0:T(8,128)S(1)}, f32[4,128,128]{2,1,0:T(8,128)S(1)}, u32[]{:S(2)}, u32[]{:S(2)}) collective-permute-start(f32[4,128,128]{2,1,0:T(8,128)S(1)} %pad_maximum_fusion.2.refs_1_), channel_id=1, source_target_pairs={{1,2},{2,1},{5,6},{6,5},{9,10},{10,9},{13,14},{14,13},{17,18},{18,... | collective-permute-start | bytes 786440 | tf_op jit(solution)/shard_map/ppermute | solution.py:423
  80.0 3.8 %collective-permute-done.14.refs_3_ = f32[4,128,128]{2,1,0:T(8,128)S(1)} collective-permute-done((f32[4,128,128]{2,1,0:T(8,128)S(1)}, f32[4,128,128]{2,1,0:T(8,128)S(1)}, u32[]{:S(2)}, u32[]{:S(2)}) %collective-permute-start.14) | collective-permute-done | bytes 262176 | tf_op jit(solution)/shard_map/ppermute | solution.py:423
  83.8 12.2 %shard_map.115 = (f32[128,128]{1,0:T(8,128)S(1)}, f32[16,32,128]{2,1,0:T(8,128)S(1)}) custom-call(s32[832]{0:T(1024)S(1)} %concatenate.7.refs_0_, f32[4,128,128]{2,1,0:T(8,128)S(1)} %pad_maximum_fusion.2.refs_1_, f32[4,128,128]{2,1,0:T(8,128)S(1)} %collective-permute-done.13.refs_2_, f32[4,128,128]{2,1,0:T(8,128)S(1)} %collective-permute-done.14.refs_3_, ...), custom_call_target="tpu_custom_call" | custom-call | tf_op jit(solution)/shard_map/pallas_call | solution.py:395
  96.0 1.2 collective-permute-start.17
  97.2 0.8 collective-permute-start.15
  98.0 2.7 %collective-permute-done.17 = f32[128,128]{1,0:T(8,128)S(1)} collective-permute-done((f32[128,128]{1,0:T(8,128)S(1)}, f32[128,128]{1,0:T(8,128)S(1)}, u32[]{:S(2)}, u32[]{:S(2)}) %collective-permute-start.17) | collective-permute-done | bytes 65568 | tf_op jit(solution)/shard_map/ppermute | solution.py:412
  100.7 1.9 %collective-permute-done.16 = f32[128,128]{1,0:T(8,128)S(1)} collective-permute-done((f32[128,128]{1,0:T(8,128)S(1)}, f32[128,128]{1,0:T(8,128)S(1)}, u32[]{:S(2)}, u32[]{:S(2)}) %collective-permute-start.16) | collective-permute-done | bytes 65568 | tf_op jit(solution)/shard_map/ppermute | solution.py:412
  102.7 5.2 %collective-permute-start.19 = (f32[4,128,128]{2,1,0:T(8,128)S(1)}, f32[4,128,128]{2,1,0:T(8,128)S(1)}, u32[]{:S(2)}, u32[]{:S(2)}) collective-permute-start(f32[4,128,128]{2,1,0:T(8,128)S(1)} %pad_maximum_fusion.3.refs_1_), channel_id=1, source_target_pairs={{1,2},{2,1},{5,6},{6,5},{9,10},{10,9},{13,14},{14,13},{17,18},{18,... | collective-permute-start | bytes 786440 | tf_op jit(solution)/shard_map/ppermute | solution.py:423
  108.0 4.0 %collective-permute-done.19.refs_3_ = f32[4,128,128]{2,1,0:T(8,128)S(1)} collective-permute-done((f32[4,128,128]{2,1,0:T(8,128)S(1)}, f32[4,128,128]{2,1,0:T(8,128)S(1)}, u32[]{:S(2)}, u32[]{:S(2)}) %collective-permute-start.19) | collective-permute-done | bytes 262176 | tf_op jit(solution)/shard_map/ppermute | solution.py:423
  111.9 10.8 %shard_map.116 = (f32[3,32,128]{2,1,0:T(8,128)}, f32[9,32,128]{2,1,0:T(8,128)}, f32[9,32,128]{2,1,0:T(8,128)}) custom-call(s32[832]{0:T(1024)S(1)} %concatenate.7.refs_0_, f32[4,128,128]{2,1,0:T(8,128)S(1)} %pad_maximum_fusion.3.refs_1_, f32[4,128,128]{2,1,0:T(8,128)S(1)} %collective-permute-done.18.refs_2_, ...), custom_call_target="tpu_custom_call" | custom-call | tf_op jit(solution)/shard_map/pallas_call | solution.py:395
  (69 shorter events, 5.0 us)
Async XLA Ops:
  0.6 0.7 copy-start.7
  0.6 0.7 copy-start.8
  0.7 1.4 %copy-start.6 = (s32[32]{0:T(128)S(1)}, s32[32]{0:T(128)}, u32[]{:S(2)}) copy-start(s32[32]{0:T(128)} %param.17) | copy-start | bytes 388
  0.7 1.4 %copy-start.4 = (s32[32,128]{1,0:T(8,128)S(1)}, s32[32,128]{1,0:T(8,128)}, u32[]{:S(2)}) copy-start(s32[32,128]{1,0:T(8,128)} %refs_1_.1) | copy-start | bytes 49156
  0.7 1.4 %copy-start.5 = (f32[32,128]{1,0:T(8,128)S(1)}, f32[32,128]{1,0:T(8,128)}, u32[]{:S(2)}) copy-start(f32[32,128]{1,0:T(8,128)} %refs_5_.1) | copy-start | bytes 49156
  2.1 0.9 copy-start
  3.0 0.9 copy-start.1
  3.9 0.8 copy-start.2
  4.7 0.8 copy-start.3
  7.7 7.4 %collective-permute-start.1 = (f32[136,128]{1,0:T(8,128)S(1)}, f32[136,128]{1,0:T(8,128)S(1)}, u32[]{:S(2)}, u32[]{:S(2)}) collective-permute-start(f32[136,128]{1,0:T(8,128)S(1)} %get-tuple-element.34), channel_id=1, source_target_pairs={{0,8},{4,12},{8,0},{12,4},{1,9},{5,13},{9,1},{13,5},{2,10},{6,14},... | collective-permute-start | bytes 208904 | tf_op jit(solution)/shard_map/ppermute | solution.py:412
  10.9 5.0 %collective-permute-start = (f32[136,128]{1,0:T(8,128)S(1)}, f32[136,128]{1,0:T(8,128)S(1)}, u32[]{:S(2)}, u32[]{:S(2)}) collective-permute-start(f32[136,128]{1,0:T(8,128)S(1)} %get-tuple-element.34), channel_id=1, source_target_pairs={{0,4},{4,8},{8,12},{12,0},{1,5},{5,9},{9,13},{13,1},{2,6},{6,10},{... | collective-permute-start | bytes 208904 | tf_op jit(solution)/shard_map/ppermute | solution.py:412
  12.2 4.1 %collective-permute-start.2 = (f32[136,128]{1,0:T(8,128)S(1)}, f32[136,128]{1,0:T(8,128)S(1)}, u32[]{:S(2)}, u32[]{:S(2)}) collective-permute-start(f32[136,128]{1,0:T(8,128)S(1)} %get-tuple-element.34), channel_id=1, source_target_pairs={{0,12},{4,0},{8,4},{12,8},{1,13},{5,1},{9,5},{13,9},{2,14},{6,2},{... | collective-permute-start | bytes 208904 | tf_op jit(solution)/shard_map/ppermute | solution.py:412
  16.2 9.6 %collective-permute-start.4 = (f32[4,136,128]{2,1,0:T(8,128)S(1)}, f32[4,136,128]{2,1,0:T(8,128)S(1)}, u32[]{:S(2)}, u32[]{:S(2)}) collective-permute-start(f32[4,136,128]{2,1,0:T(8,128)S(1)} %pad_maximum_fusion.refs_1_), channel_id=1, source_target_pairs={{1,2},{2,1},{5,6},{6,5},{9,10},{10,9},{13,14},{14,13},{17,18},{18,... | collective-permute-start | bytes 835592 | tf_op jit(solution)/shard_map/ppermute | solution.py:423
  21.6 4.2 %collective-permute-start.3 = (f32[4,136,128]{2,1,0:T(8,128)S(1)}, f32[4,136,128]{2,1,0:T(8,128)S(1)}, u32[]{:S(2)}, u32[]{:S(2)}) collective-permute-start(f32[4,136,128]{2,1,0:T(8,128)S(1)} %pad_maximum_fusion.refs_1_), channel_id=1, source_target_pairs={{0,1},{1,0},{2,3},{3,2},{4,5},{5,4},{6,7},{7,6},{8,9},{9,8},{10,11... | collective-permute-start | bytes 835592 | tf_op jit(solution)/shard_map/ppermute | solution.py:423
  38.6 4.3 %collective-permute-start.7 = (f32[128,128]{1,0:T(8,128)S(1)}, f32[128,128]{1,0:T(8,128)S(1)}, u32[]{:S(2)}, u32[]{:S(2)}) collective-permute-start(f32[128,128]{1,0:T(8,128)S(1)} %get-tuple-element.16), channel_id=1, source_target_pairs={{0,12},{4,0},{8,4},{12,8},{1,13},{5,1},{9,5},{13,9},{2,14},{6,2},{... | collective-permute-start | bytes 196616 | tf_op jit(solution)/shard_map/ppermute | solution.py:412
  41.6 4.3 %collective-permute-start.6 = (f32[128,128]{1,0:T(8,128)S(1)}, f32[128,128]{1,0:T(8,128)S(1)}, u32[]{:S(2)}, u32[]{:S(2)}) collective-permute-start(f32[128,128]{1,0:T(8,128)S(1)} %get-tuple-element.16), channel_id=1, source_target_pairs={{0,8},{4,12},{8,0},{12,4},{1,9},{5,13},{9,1},{13,5},{2,10},{6,14},... | collective-permute-start | bytes 196616 | tf_op jit(solution)/shard_map/ppermute | solution.py:412
  41.6 5.0 %collective-permute-start.5 = (f32[128,128]{1,0:T(8,128)S(1)}, f32[128,128]{1,0:T(8,128)S(1)}, u32[]{:S(2)}, u32[]{:S(2)}) collective-permute-start(f32[128,128]{1,0:T(8,128)S(1)} %get-tuple-element.16), channel_id=1, source_target_pairs={{0,4},{4,8},{8,12},{12,0},{1,5},{5,9},{9,13},{13,1},{2,6},{6,10},{... | collective-permute-start | bytes 196616 | tf_op jit(solution)/shard_map/ppermute | solution.py:412
  46.6 9.3 %collective-permute-start.9 = (f32[4,128,128]{2,1,0:T(8,128)S(1)}, f32[4,128,128]{2,1,0:T(8,128)S(1)}, u32[]{:S(2)}, u32[]{:S(2)}) collective-permute-start(f32[4,128,128]{2,1,0:T(8,128)S(1)} %pad_maximum_fusion.1.refs_1_), channel_id=1, source_target_pairs={{1,2},{2,1},{5,6},{6,5},{9,10},{10,9},{13,14},{14,13},{17,18},{18,... | collective-permute-start | bytes 786440 | tf_op jit(solution)/shard_map/ppermute | solution.py:423
  51.8 4.0 %collective-permute-start.8 = (f32[4,128,128]{2,1,0:T(8,128)S(1)}, f32[4,128,128]{2,1,0:T(8,128)S(1)}, u32[]{:S(2)}, u32[]{:S(2)}) collective-permute-start(f32[4,128,128]{2,1,0:T(8,128)S(1)} %pad_maximum_fusion.1.refs_1_), channel_id=1, source_target_pairs={{0,1},{1,0},{2,3},{3,2},{4,5},{5,4},{6,7},{7,6},{8,9},{9,8},{10,11... | collective-permute-start | bytes 786440 | tf_op jit(solution)/shard_map/ppermute | solution.py:423
  68.1 4.5 %collective-permute-start.12 = (f32[128,128]{1,0:T(8,128)S(1)}, f32[128,128]{1,0:T(8,128)S(1)}, u32[]{:S(2)}, u32[]{:S(2)}) collective-permute-start(f32[128,128]{1,0:T(8,128)S(1)} %get-tuple-element.18), channel_id=1, source_target_pairs={{0,12},{4,0},{8,4},{12,8},{1,13},{5,1},{9,5},{13,9},{2,14},{6,2},{... | collective-permute-start | bytes 196616 | tf_op jit(solution)/shard_map/ppermute | solution.py:412
  69.0 5.7 %collective-permute-start.11 = (f32[128,128]{1,0:T(8,128)S(1)}, f32[128,128]{1,0:T(8,128)S(1)}, u32[]{:S(2)}, u32[]{:S(2)}) collective-permute-start(f32[128,128]{1,0:T(8,128)S(1)} %get-tuple-element.18), channel_id=1, source_target_pairs={{0,8},{4,12},{8,0},{12,4},{1,9},{5,13},{9,1},{13,5},{2,10},{6,14},... | collective-permute-start | bytes 196616 | tf_op jit(solution)/shard_map/ppermute | solution.py:412
  69.1 5.6 %collective-permute-start.10 = (f32[128,128]{1,0:T(8,128)S(1)}, f32[128,128]{1,0:T(8,128)S(1)}, u32[]{:S(2)}, u32[]{:S(2)}) collective-permute-start(f32[128,128]{1,0:T(8,128)S(1)} %get-tuple-element.18), channel_id=1, source_target_pairs={{0,4},{4,8},{8,12},{12,0},{1,5},{5,9},{9,13},{13,1},{2,6},{6,10},{... | collective-permute-start | bytes 196616 | tf_op jit(solution)/shard_map/ppermute | solution.py:412
  74.7 9.0 %collective-permute-start.14 = (f32[4,128,128]{2,1,0:T(8,128)S(1)}, f32[4,128,128]{2,1,0:T(8,128)S(1)}, u32[]{:S(2)}, u32[]{:S(2)}) collective-permute-start(f32[4,128,128]{2,1,0:T(8,128)S(1)} %pad_maximum_fusion.2.refs_1_), channel_id=1, source_target_pairs={{1,2},{2,1},{5,6},{6,5},{9,10},{10,9},{13,14},{14,13},{17,18},{18,... | collective-permute-start | bytes 786440 | tf_op jit(solution)/shard_map/ppermute | solution.py:423
  79.9 3.9 %collective-permute-start.13 = (f32[4,128,128]{2,1,0:T(8,128)S(1)}, f32[4,128,128]{2,1,0:T(8,128)S(1)}, u32[]{:S(2)}, u32[]{:S(2)}) collective-permute-start(f32[4,128,128]{2,1,0:T(8,128)S(1)} %pad_maximum_fusion.2.refs_1_), channel_id=1, source_target_pairs={{0,1},{1,0},{2,3},{3,2},{4,5},{5,4},{6,7},{7,6},{8,9},{9,8},{10,11... | collective-permute-start | bytes 786440 | tf_op jit(solution)/shard_map/ppermute | solution.py:423
  96.0 4.7 %collective-permute-start.17 = (f32[128,128]{1,0:T(8,128)S(1)}, f32[128,128]{1,0:T(8,128)S(1)}, u32[]{:S(2)}, u32[]{:S(2)}) collective-permute-start(f32[128,128]{1,0:T(8,128)S(1)} %get-tuple-element.20), channel_id=1, source_target_pairs={{0,12},{4,0},{8,4},{12,8},{1,13},{5,1},{9,5},{13,9},{2,14},{6,2},{... | collective-permute-start | bytes 196616 | tf_op jit(solution)/shard_map/ppermute | solution.py:412
  97.2 5.4 %collective-permute-start.16 = (f32[128,128]{1,0:T(8,128)S(1)}, f32[128,128]{1,0:T(8,128)S(1)}, u32[]{:S(2)}, u32[]{:S(2)}) collective-permute-start(f32[128,128]{1,0:T(8,128)S(1)} %get-tuple-element.20), channel_id=1, source_target_pairs={{0,8},{4,12},{8,0},{12,4},{1,9},{5,13},{9,1},{13,5},{2,10},{6,14},... | collective-permute-start | bytes 196616 | tf_op jit(solution)/shard_map/ppermute | solution.py:412
  97.2 5.4 %collective-permute-start.15 = (f32[128,128]{1,0:T(8,128)S(1)}, f32[128,128]{1,0:T(8,128)S(1)}, u32[]{:S(2)}, u32[]{:S(2)}) collective-permute-start(f32[128,128]{1,0:T(8,128)S(1)} %get-tuple-element.20), channel_id=1, source_target_pairs={{0,4},{4,8},{8,12},{12,0},{1,5},{5,9},{9,13},{13,1},{2,6},{6,10},{... | collective-permute-start | bytes 196616 | tf_op jit(solution)/shard_map/ppermute | solution.py:412
  102.7 9.3 %collective-permute-start.19 = (f32[4,128,128]{2,1,0:T(8,128)S(1)}, f32[4,128,128]{2,1,0:T(8,128)S(1)}, u32[]{:S(2)}, u32[]{:S(2)}) collective-permute-start(f32[4,128,128]{2,1,0:T(8,128)S(1)} %pad_maximum_fusion.3.refs_1_), channel_id=1, source_target_pairs={{1,2},{2,1},{5,6},{6,5},{9,10},{10,9},{13,14},{14,13},{17,18},{18,... | collective-permute-start | bytes 786440 | tf_op jit(solution)/shard_map/ppermute | solution.py:423
  107.9 4.0 %collective-permute-start.18 = (f32[4,128,128]{2,1,0:T(8,128)S(1)}, f32[4,128,128]{2,1,0:T(8,128)S(1)}, u32[]{:S(2)}, u32[]{:S(2)}) collective-permute-start(f32[4,128,128]{2,1,0:T(8,128)S(1)} %pad_maximum_fusion.3.refs_1_), channel_id=1, source_target_pairs={{0,1},{1,0},{2,3},{3,2},{4,5},{5,4},{6,7},{7,6},{8,9},{9,8},{10,11... | collective-permute-start | bytes 786440 | tf_op jit(solution)/shard_map/ppermute | solution.py:423

commit v2 on v1

--- a/solution.py
+++ b/solution.py
@@ -130,62 +130,129 @@
             put(1 + b, 1 + a, mass * affine[3 * a + b] - stress)
 
 
-def scatter_bins(tabs, own_count, lane, sets, sums):
-    at_base = own_count
+def add_patch(sums, row, patch, shift, z, lane):
+    moved = pltpu.roll(patch, shift & 127, 1)
+    moved = jnp.where((lane >= z) & (lane < z + 8), moved, 0.0)
+    for i in range(4):
+        place = pl.ds(row + i * ROWS_X, 16)
+        sums[place, :] = sums[place, :] + moved[16 * i : 16 * i + 16]
+
+
+def clear_own(tabs, bins, sums):
+    def clear(at, _):
+        for i in range(4):
+            sums[pl.ds(tabs[at] + i * ROWS_X, 16), :] = jnp.zeros((16, 128), F32)
+        return _
+
+    lax.fori_loop(0, bins, clear, 0, unroll=4)
+
+
+def gather_group(tabs, group, sums, lane):
     total = tabs.shape[0] // 2
-    for column, patch_ref in enumerate(sets):
-        devices = patch_ref.shape[0]
-        groups = own_count // 16
-
-        def block(at, _, patch_ref=patch_ref, at_base=at_base, column=column):
-            dev = at // groups
-            start = pl.multiple_of((at % groups) * 64, 64)
-            first = at_base + at * 16
-            for slot in range(16):
-                row = tabs[first + slot]
-                z = tabs[total + first + slot]
-
-                def add(row=row, z=z, slot=slot):
-                    patch = patch_ref[dev, pl.ds(start, 64), :]
-                    moved = pltpu.roll(patch, (z + (128 - 8 * slot)) & 127, 1)
-                    inside = (lane >= z) & (lane < z + 8)
-                    moved = jnp.where(inside, moved, 0.0)
-                    for i in range(4):
-                        place = pl.ds(row + i * ROWS_X, 16)
-                        sums[place, :] = sums[place, :] + moved[16 * i : 16 * i + 16]
-
-                if column == 0:
-                    add()
-                else:
-                    pl.when(row >= 0)(add)
-            return _
-
-        lax.fori_loop(0, devices * groups, block, 0)
-        at_base = at_base + devices * own_count
+    compact = jnp.zeros((64, 128), F32)
+    for slot in range(16):
+        row = tabs[group * 16 + slot]
+        z = tabs[total + group * 16 + slot]
+        node = fill([sums[pl.ds(row + i * ROWS_X, 16), :] for i in range(4)])
+        moved = pltpu.roll(node, (8 * slot + 128 - z) & 127, 1)
+        compact = jnp.where(lane // 8 == slot, moved, compact)
+    return compact
 
 
 def fill(blocks):
     return jnp.concatenate(blocks, axis=0)
 
 
-def kernel(first, last, total_count, *refs):
+def column_kernel(bins, tabs, patch_ref, out, sums):
+    lane = lax.broadcasted_iota(jnp.int32, (64, 128), 1)
+    total = tabs.shape[0] // 2
+    groups = bins // 16
+    clear_own(tabs, bins, sums)
+
+    def block(at, _):
+        start = pl.multiple_of((at % groups) * 64, 64)
+        first = bins + at * 16
+        for slot in range(16):
+            z = tabs[total + first + slot]
+            patch = patch_ref[at // groups, pl.ds(start, 64), :]
+            add_patch(sums, tabs[first + slot], patch, z + (128 - 8 * slot), z, lane)
+        return _
+
+    lax.fori_loop(0, patch_ref.shape[0] * groups, block, 0)
+    for g in range(groups):
+        out[g] = gather_group(tabs, g, sums, lane)
+
+
+def list_bins(tabs, bins, count, listed):
+    for side in range(2):
+
+        def one(at, place, side=side):
+            listed[side * count + place] = at
+            return place + (tabs[bins + side * count + at] >= 0).astype(jnp.int32)
+
+        listed[2 * count + side] = lax.fori_loop(0, count, one, jnp.int32(0), unroll=8)
+
+
+def scatter_listed(tabs, bins, listed, sides, sums, spare, lane):
+    total = tabs.shape[0] // 2
+    for side, patch_ref in enumerate(sides):
+        count = patch_ref.shape[0] * bins
+        many = listed[2 * count + side]
+
+        def some(at, _, side=side, patch_ref=patch_ref, count=count, many=many):
+            found = []
+            for step in range(4):
+                n = at * 4 + step
+                used = n < many
+                which = listed[side * count + jnp.where(used, n, 0)]
+                row = jnp.where(used, tabs[bins + side * count + which], spare)
+                z = tabs[total + bins + side * count + which]
+                inner = which % bins
+                start = pl.multiple_of((inner // 16) * 64, 64)
+                patch = patch_ref[which // bins, pl.ds(start, 64), :]
+                found.append((row, patch, z + 128 - 8 * (inner % 16), z))
+            for row, patch, shift, z in found:
+                add_patch(sums, row, patch, shift, z, lane)
+            return _
+
+        lax.fori_loop(0, (many + 3) // 4, some, 0)
+
+
+def kernel(first, listing, last, *refs):
     refs = list(refs)
     take = lambda n: [refs.pop(0) for _ in range(n)]
     if first:
-        offsets_in, cell, velocity_in, affine_in, strain, mass_in = take(6)
-        bins = mass_in.shape[0]
+        sources = take(6)
+        bins = sources[5].shape[0]
     else:
-        tabs, patch_own, patch_a, patch_b, inside_ref, state_in = take(6)
+        (tabs,) = take(1)
+        if not listing:
+            (listed,) = take(1)
+        patch_a, patch_b, compact_in, inside_ref, state_in, params, depth = take(7)
         bins = state_in.shape[1]
     if last:
         velocity_out, affine_out, deform_out = take(3)
     else:
-        patch_out, state_out = take(2)
-    params, depth, wide, wide_low, products = take(5)
-    if not first:
+        patch_out, state_out, params_out, depth_out = take(4)
+    if listing:
+        (listed,) = take(1)
+    wide, products = take(2)
+    if first:
+        held = take(6)
+        arrived = refs.pop(0)
+        copies = [
+            pltpu.make_async_copy(source, target, arrived.at[at])
+            for at, (source, target) in enumerate(zip(sources, held))
+        ]
+        for copy in copies:
+            copy.start()
+        for copy in copies:
+            copy.wait()
+        offsets_in, cell, velocity_in, affine_in, strain, mass_in = held
+    else:
         sums, results = take(2)
     if not last:
-        blends, products_low = take(2)
+        wide_low, blends, products_low = take(3)
     groups = bins // 16
     sub = lax.broadcasted_iota(jnp.int32, (8, 128), 0)
     lane = lax.broadcasted_iota(jnp.int32, (64, 128), 1)
@@ -223,32 +290,18 @@
             span = pl.ds(g8 * 8, 8)
             fractions, bases, deform, mass = load8(g8)
             store8(g8, fractions, bases, deform, mass)
-            stencil_rows(g8, fractions, bases, params)
+            stencil_rows(g8, fractions, bases, params_out)
             velocity = [velocity_in[a, span, :] for a in range(3)]
             affine = [affine_in[e, span, :] for e in range(9)]
             deposit_rows(g8, velocity, affine, deform, mass, blends)
     else:
-        total = tabs.shape[0] // 2
-        for g8 in range(bins // 8):
-            fractions, bases, _, _ = load8(g8)
-            stencil_rows(g8, fractions, bases, params)
-        depth_weights(bins, params, depth)
-
-        def clear(at, _):
-            for i in range(4):
-                sums[pl.ds(tabs[at] + i * ROWS_X, 16), :] = jnp.zeros((16, 128), F32)
-            return _
-
-        lax.fori_loop(0, bins, clear, 0, unroll=4)
-        scatter_bins(tabs, bins, lane, [patch_own, patch_a, patch_b], sums)
+        if listing:
+            list_bins(tabs, bins, patch_a.shape[0] * bins, listed)
+        clear_own(tabs, bins, sums)
+        spare = sums.shape[0] - 3 * ROWS_X - 16
+        scatter_listed(tabs, bins, listed, [patch_a, patch_b], sums, spare, lane)
         for g in range(groups):
-            compact = jnp.zeros((64, 128), F32)
-            for slot in range(16):
-                row = tabs[g * 16 + slot]
-                z = tabs[total + g * 16 + slot]
-                node = fill([sums[pl.ds(row + i * ROWS_X, 16), :] for i in range(4)])
-                moved = pltpu.roll(node, (8 * slot + 128 - z) & 127, 1)
-                compact = jnp.where(lane // 8 == slot, moved, compact)
+            compact = compact_in[g] + gather_group(tabs, g, sums, lane)
             channel = lax.broadcasted_iota(jnp.int32, (64, 128), 0) & 3
             mass = jnp.where(channel == 0, compact, 0.0)
             mass = mass + pltpu.roll(mass, 1, 0)
@@ -321,23 +374,23 @@
             else:
                 fractions = [fractions[a] + time_step * velocity[a] for a in range(3)]
                 store8(g8, fractions, bases, deform, mass)
-                stencil_rows(g8, fractions, bases, params)
+                stencil_rows(g8, fractions, bases, params_out)
                 deposit_rows(g8, velocity, affine, deform, mass, blends)
 
     if not last:
-        depth_weights(bins, params, depth)
+        depth_weights(bins, params_out, depth_out)
         for g in range(groups):
 
             def build(slot, _, g=g):
                 base = (g * 16 + slot) * 16
                 place = pl.multiple_of((g * 16 + slot) * 32, 32)
-                weights, moments = y_patterns(params, base, sub)
-                x0 = row_of(params, base + 8)
+                weights, moments = y_patterns(params_out, base, sub)
+                x0 = row_of(params_out, base + 8)
                 pushed, b0, b1, b2 = [blends[pl.ds(place + 8 * k, 8), :] for k in range(4)]
                 plain = []
                 deep = []
                 for i in range(4):
-                    wx = row_of(params, base + i)
+                    wx = row_of(params_out, base + i)
                     along = (pushed + b0 * (i - x0)) * wx
                     across = b1 * wx
                     depthwise = b2 * wx
@@ -354,10 +407,10 @@
             lax.fori_loop(0, 16, build, 0, unroll=2)
             turned = (((1,), (1,)), ((), ()))
             products[...] = lax.dot_general(
-                wide[...], depth[g, 128:384, :], turned, preferred_element_type=F32
+                wide[...], depth_out[g, 128:384, :], turned, preferred_element_type=F32
             )
             products_low[...] = lax.dot_general(
-                wide_low[...], depth[g, 128:256, :], turned, preferred_element_type=F32
+                wide_low[...], depth_out[g, 128:256, :], turned, preferred_element_type=F32
             )
             compact = jnp.zeros((64, 128), F32)
             for slot in range(16):
@@ -367,38 +420,78 @@
             patch_out[64 * g : 64 * g + 64, :] = compact
 
 
-def run_kernel(first, last, total_x, bins, operands):
-    vmem = pl.BlockSpec(memory_space=pltpu.VMEM)
-    smem = pl.BlockSpec(memory_space=pltpu.SMEM)
-    shape = lambda *dims: jax.ShapeDtypeStruct(dims, F32)
+VMEM_SPEC = pl.BlockSpec(memory_space=pltpu.VMEM)
+SMEM_SPEC = pl.BlockSpec(memory_space=pltpu.SMEM)
+
+
+def shape_of(*dims, dtype=F32):
+    return jax.ShapeDtypeStruct(dims, dtype)
+
+
+def grid_rows(total_x):
+    return (total_x + 7) * ROWS_X + 16
+
+
+def limit_for(operands, total_x):
+    held = sum(4 * op.size for op in operands) + 512 * grid_rows(total_x)
+    return held + (16 << 20)
+
+
+def run_column(total_x, bins, tabs, column):
+    return pl.pallas_call(
+        functools.partial(column_kernel, bins),
+        out_shape=shape_of(bins // 16, 64, 128),
+        in_specs=[SMEM_SPEC, VMEM_SPEC],
+        out_specs=VMEM_SPEC,
+        scratch_shapes=[pltpu.VMEM((grid_rows(total_x), 128), F32)],
+        cost_estimate=pl.CostEstimate(
+            flops=column.size * 10, bytes_accessed=column.size * 160, transcendentals=0
+        ),
+        compiler_params=pltpu.CompilerParams(vmem_limit_bytes=limit_for([column], total_x)),
+    )(tabs, column)
+
+
+def run_kernel(first, listing, last, total_x, bins, operands):
     if last:
-        outs = [shape(3, bins, 128), shape(9, bins, 128), shape(9, bins, 128)]
+        outs = [shape_of(3, bins, 128), shape_of(9, bins, 128), shape_of(9, bins, 128)]
     else:
-        outs = [shape(4 * bins, 128), shape(16, bins, 128)]
-    groups = bins // 16
-    scratch = [
-        pltpu.VMEM((16 * bins, 128), F32),
-        pltpu.VMEM((groups, 384, 256), BF16),
-        pltpu.VMEM((1024, 256), BF16),
-        pltpu.VMEM((1024, 256), BF16),
-        pltpu.VMEM((1024, 256), F32),
-    ]
-    grid_rows = (total_x + 4) * ROWS_X
-    if not first:
-        scratch += [pltpu.VMEM((grid_rows, 128), F32), pltpu.VMEM((32 * bins, 128), F32)]
+        outs = [
+            shape_of(4 * bins, 128),
+            shape_of(16, bins, 128),
+            shape_of(16 * bins, 128),
+            shape_of(bins // 16, 384, 256, dtype=BF16),
+        ]
+    out_specs = [VMEM_SPEC] * len(outs)
+    scratch = [pltpu.VMEM((1024, 256), BF16), pltpu.VMEM((1024, 256), F32)]
+    in_specs = [VMEM_SPEC] * len(operands)
+    if first:
+        in_specs = [pl.BlockSpec(memory_space=pl.ANY)] * len(operands)
+        scratch += [pltpu.VMEM(op.shape, op.dtype) for op in operands]
+        scratch += [pltpu.SemaphoreType.DMA((len(operands),))]
+    else:
+        in_specs[0] = SMEM_SPEC
+        if listing:
+            outs.append(shape_of(2 * operands[1].shape[0] * bins + 8, dtype=jnp.int32))
+            out_specs.append(SMEM_SPEC)
+        else:
+            in_specs[1] = SMEM_SPEC
+        scratch += [
+            pltpu.VMEM((grid_rows(total_x), 128), F32),
+            pltpu.VMEM((32 * bins, 128), F32),
+        ]
     if not last:
-        scratch += [pltpu.VMEM((32 * bins, 128), F32), pltpu.VMEM((1024, 128), F32)]
-    in_specs = [vmem] * len(operands)
-    if not first:
-        in_specs[0] = smem
-    held = sum(4 * op.size for op in operands) + 512 * grid_rows
+        scratch += [
+            pltpu.VMEM((1024, 256), BF16),
+            pltpu.VMEM((32 * bins, 128), F32),
+            pltpu.VMEM((1024, 128), F32),
+        ]
     return pl.pallas_call(
-        functools.partial(kernel, first, last, bins),
+        functools.partial(kernel, first, listing, last),
         out_shape=outs,
         in_specs=in_specs,
-        out_specs=[vmem] * len(outs),
+        out_specs=out_specs,
         scratch_shapes=scratch,
-        compiler_params=pltpu.CompilerParams(vmem_limit_bytes=held + (16 << 20)),
+        compiler_params=pltpu.CompilerParams(vmem_limit_bytes=limit_for(operands, total_x)),
     )(*operands)
 
 
@@ -447,8 +540,9 @@
     in_grid = (at_x >= 0) & (at_x < total_x) & (at_y >= 0) & (at_y < total_y)
     inside = ((at >= 2) & (at < limit - 2) & (channel > 0) & in_grid).astype(F32)
 
-    patch, state = run_kernel(
+    patch, state, params, depth = run_kernel(
         True,
+        False,
         False,
         total_x,
         bins,
@@ -466,29 +560,42 @@
     ).astype(F32)
     facts = jnp.pad(facts, ((0, 4), (0, 128 - bins)))
     payload = jnp.concatenate([patch, facts], axis=0)
-    tabs = None
+
+    def places(block, move):
+        known = block[:, 4 * bins : 4 * bins + 4, 0:bins].astype(jnp.int32)
+        y = known[:, 1] + LOW_Y + move
+        row = known[:, 0] * ROWS_X + 4 * y
+        good = (known[:, 3] > 0) & (y >= 0) & (y <= LOW_Y + TILE + 1)
+        return jnp.where(good, row, -1).reshape(-1), known[:, 2].reshape(-1)
+
+    step_a = jnp.where(place_y % 2 == 0, TILE, -TILE)
     for substep in range(SUBSTEPS):
         column = column_of(payload)
         beside = neighbours_of(column)
         if substep == 0:
-            even = place_y % 2 == 0
-            rows = []
-            depths = []
-            for at, block in enumerate([column] + beside):
-                known = block[:, 4 * bins : 4 * bins + 4, 0:bins].astype(jnp.int32)
-                move = (0, jnp.where(even, TILE, -TILE), jnp.where(even, -TILE, TILE))[at]
-                y = known[:, 1] + LOW_Y + move
-                row = known[:, 0] * ROWS_X + 4 * y
-                good = (known[:, 3] > 0) & (y >= 0) & (y <= LOW_Y + TILE + 1)
-                rows.append(jnp.where(good, row, -1).reshape(-1))
-                depths.append(known[:, 2].reshape(-1))
-            tabs = jnp.concatenate([own_row] + rows + [anchor_z] + depths)
+            row, z = places(column, 0)
+            column_tabs = jnp.concatenate([own_row, row, anchor_z, z])
+            row_a, z_a = places(beside[0], step_a)
+            row_b, z_b = places(beside[1], -step_a)
+            tabs = jnp.concatenate([own_row, row_a, row_b, anchor_z, z_a, z_b])
+        compact = run_column(total_x, bins, column_tabs, column)
+        listing = substep == 0
         last = substep == SUBSTEPS - 1
         results = run_kernel(
-            False, last, total_x, bins, [tabs, column] + beside + [inside, state]
+            False,
+            listing,
+            last,
+            total_x,
+            bins,
+            [tabs]
+            + ([] if listing else [listed])
+            + beside
+            + [compact, inside, state, params, depth],
         )
         if not last:
-            payload, state = results
+            payload, state, params, depth = results[:4]
+        if listing:
+            listed = results[4]
     return tuple(turn(array) for array in results)
 
 

time: 123 us -> 105 us (0.85)
  waiting for transfers between devices: 29.8 us -> 21.3 us
  Pallas kernels: 49.7 us -> 42.3 us
  starting transfers between devices: 35.8 us -> 33.3 us
    ppermute x8, waiting for transfers between devices: 15.6 us -> 5.05 us  [neighbours_of(): lax.ppermute(column, 'gy', pairs)]
    pallas_call x5 -> x9, Pallas kernels: 49.7 us -> 42.3 us  [the longest x5 31.6 us: run_kernel(): pl.pallas_call(functools.partial(kernel, first, listing, last), out_shape...]
    ppermute x8, starting transfers between devices: 21.3 us -> 17.9 us  [neighbours_of(): lax.ppermute(column, 'gy', pairs)]
    ppermute x12, waiting for transfers between devices: 14.2 us -> 16.2 us  [column_of(): pieces.append(lax.ppermute(payload, 'gx', pairs))]
  transfers between devices with their start and end apart: 20 -> 20, of which waited for: 13 -> 12; matrix products, arithmetic and copies ran while one was open for 1% -> 1% of each run, Pallas kernels for 0% -> 10%
where the time goes in v2:
time: 105 us; the launch traced here: 104 us
  Pallas kernels  42.3 us (40%)
  starting transfers between devices  33.3 us (32%)
  waiting for transfers between devices  21.3 us (20%)
  local copies, waits for them, and re-layouts  5.37 us (5%)
  other arithmetic  1.18 us (1%)
    pallas_call x5, Pallas kernels, run_kernel(): pl.pallas_call(functools.partial(kernel, first, listing, last), out_shape...  31.6 us
    ppermute x8, starting transfers between devices, neighbours_of(): lax.ppermute(column, 'gy', pairs)  17.9 us
    ppermute x12, waiting for transfers between devices, column_of(): pieces.append(lax.ppermute(payload, 'gx', pairs))  16.2 us
    ppermute x12, starting transfers between devices, column_of(): pieces.append(lax.ppermute(payload, 'gx', pairs))  15.4 us
    pallas_call x4, Pallas kernels, run_column(): pl.pallas_call(functools.partial(column_kernel, bins), out_shape=shape_of...  10.7 us
    ppermute x8, waiting for transfers between devices, neighbours_of(): lax.ppermute(column, 'gy', pairs)  5.05 us
    unnamed x18, local copies, waits for them, and re-layouts  3.48 us
  transfers between devices with their start and end apart: 20, of which 12 were waited for; matrix products, arithmetic and copies ran while one was open for 1% of the time, Pallas kernels for 10%

profile of v2, /device:TPU:1, one launch (start us, length us, event | category | flops | bytes accessed | tf_op | source)
XLA Modules:
  0.0 104.4 jit_solution(4361803896746574622)
XLA Ops:
  2.1 0.9 copy-done
  3.0 0.9 copy-done.1
  5.5 2.7 %shard_map.112 = (f32[128,128]{1,0:T(8,128)S(1)}, f32[16,32,128]{2,1,0:T(8,128)S(1)}, f32[512,128]{1,0:T(8,128)S(1)}, bf16[2,384,256]{2,1,0:T(8,128)(2,1)S(1)}) custom-call(f32[3,32,128]{2,1,0:T(8,128)S(1)} %bitcast.38, s32[32,128]{1,0:T(8,128)S(1)} %copy-done.4, f32[3,32,128]{2,1,0:T(8,128)S(1)} %bitcast.39, f32[9,32,128]{2,1,0:T(8,128)S(1)} %bitcast.33, ...), custom_call_target="tpu_custom_call" | custom-call | tf_op jit(solution)/shard_map/pallas_call | solution.py:488
  8.2 3.2 %collective-permute-start.1 = (f32[136,128]{1,0:T(8,128)S(1)}, f32[136,128]{1,0:T(8,128)S(1)}, u32[]{:S(2)}, u32[]{:S(2)}) collective-permute-start(f32[136,128]{1,0:T(8,128)S(1)} %get-tuple-element.52), channel_id=1, source_target_pairs={{0,8},{4,12},{8,0},{12,4},{1,9},{5,13},{9,1},{13,5},{2,10},{6,14},... | collective-permute-start | bytes 208904 | tf_op jit(solution)/shard_map/ppermute | solution.py:505
  11.4 1.3 %collective-permute-start = (f32[136,128]{1,0:T(8,128)S(1)}, f32[136,128]{1,0:T(8,128)S(1)}, u32[]{:S(2)}, u32[]{:S(2)}) collective-permute-start(f32[136,128]{1,0:T(8,128)S(1)} %get-tuple-element.52), channel_id=1, source_target_pairs={{0,4},{4,8},{8,12},{12,0},{1,5},{5,9},{9,13},{13,1},{2,6},{6,10},{... | collective-permute-start | bytes 208904 | tf_op jit(solution)/shard_map/ppermute | solution.py:505
  12.7 2.0 %collective-permute-start.2 = (f32[136,128]{1,0:T(8,128)S(1)}, f32[136,128]{1,0:T(8,128)S(1)}, u32[]{:S(2)}, u32[]{:S(2)}) collective-permute-start(f32[136,128]{1,0:T(8,128)S(1)} %get-tuple-element.52), channel_id=1, source_target_pairs={{0,12},{4,0},{8,4},{12,8},{1,13},{5,1},{9,5},{13,9},{2,14},{6,2},{... | collective-permute-start | bytes 208904 | tf_op jit(solution)/shard_map/ppermute | solution.py:505
  15.7 0.8 collective-permute-done
  16.8 5.4 %collective-permute-start.4 = (f32[4,136,128]{2,1,0:T(8,128)S(1)}, f32[4,136,128]{2,1,0:T(8,128)S(1)}, u32[]{:S(2)}, u32[]{:S(2)}) collective-permute-start(f32[4,136,128]{2,1,0:T(8,128)S(1)} %pad_maximum_fusion.patch_ref), channel_id=1, source_target_pairs={{1,2},{2,1},{5,6},{6,5},{9,10},{10,9},{13,14},{14,13},{17,18},{18,... | collective-permute-start | bytes 835592 | tf_op jit(solution)/shard_map/ppermute | solution.py:516
  22.6 2.7 %shard_map.113.refs_3_ = f32[2,64,128]{2,1,0:T(8,128)S(1)} custom-call(s32[320]{0:T(512)S(1)} %pad_add_fusion.tabs, f32[4,136,128]{2,1,0:T(8,128)S(1)} %pad_maximum_fusion.patch_ref), custom_call_target="tpu_custom_call" | custom-call | flops 696320 | bytes 11141120 | tf_op jit(solution)/shard_map/pallas_call | solution.py:441
  25.3 1.2 %collective-permute-done.4.refs_2_ = f32[4,136,128]{2,1,0:T(8,128)S(1)} collective-permute-done((f32[4,136,128]{2,1,0:T(8,128)S(1)}, f32[4,136,128]{2,1,0:T(8,128)S(1)}, u32[]{:S(2)}, u32[]{:S(2)}) %collective-permute-start.4) | collective-permute-done | bytes 278560 | tf_op jit(solution)/shard_map/ppermute | solution.py:516
  26.9 8.2 %shard_map.114 = (f32[128,128]{1,0:T(8,128)S(1)}, f32[16,32,128]{2,1,0:T(8,128)S(1)}, f32[512,128]{1,0:T(8,128)S(1)}, bf16[2,384,256]{2,1,0:T(8,128)(2,1)S(1)}, s32[264]{0:T(512)S(1)}) custom-call(s32[576]{0:T(1024)S(1)} %concatenate.10.refs_0_, f32[4,136,128]{2,1,0:T(8,128)S(1)} %collective-permute-done.3.refs_1_, ...), custom_call_target="tpu_custom_call" | custom-call | tf_op jit(solution)/shard_map/pallas_call | solution.py:488
  35.1 3.0 %collective-permute-start.7 = (f32[128,128]{1,0:T(8,128)S(1)}, f32[128,128]{1,0:T(8,128)S(1)}, u32[]{:S(2)}, u32[]{:S(2)}) collective-permute-start(f32[128,128]{1,0:T(8,128)S(1)} %get-tuple-element.28), channel_id=1, source_target_pairs={{0,12},{4,0},{8,4},{12,8},{1,13},{5,1},{9,5},{13,9},{2,14},{6,2},{... | collective-permute-start | bytes 196616 | tf_op jit(solution)/shard_map/ppermute | solution.py:505
  38.9 1.2 %collective-permute-done.7 = f32[128,128]{1,0:T(8,128)S(1)} collective-permute-done((f32[128,128]{1,0:T(8,128)S(1)}, f32[128,128]{1,0:T(8,128)S(1)}, u32[]{:S(2)}, u32[]{:S(2)}) %collective-permute-start.7) | collective-permute-done | bytes 65568 | tf_op jit(solution)/shard_map/ppermute | solution.py:505
  40.1 3.9 %collective-permute-done.6 = f32[128,128]{1,0:T(8,128)S(1)} collective-permute-done((f32[128,128]{1,0:T(8,128)S(1)}, f32[128,128]{1,0:T(8,128)S(1)}, u32[]{:S(2)}, u32[]{:S(2)}) %collective-permute-start.6) | collective-permute-done | bytes 65568 | tf_op jit(solution)/shard_map/ppermute | solution.py:505
  44.0 4.2 %collective-permute-start.9 = (f32[4,128,128]{2,1,0:T(8,128)S(1)}, f32[4,128,128]{2,1,0:T(8,128)S(1)}, u32[]{:S(2)}, u32[]{:S(2)}) collective-permute-start(f32[4,128,128]{2,1,0:T(8,128)S(1)} %pad_maximum_fusion.1.patch_ref), channel_id=1, source_target_pairs={{1,2},{2,1},{5,6},{6,5},{9,10},{10,9},{13,14},{14,13},{17,18},{18,... | collective-permute-start | bytes 786440 | tf_op jit(solution)/shard_map/ppermute | solution.py:516
  48.3 2.7 %shard_map.115.refs_4_ = f32[2,64,128]{2,1,0:T(8,128)S(1)} custom-call(s32[320]{0:T(512)S(1)} %pad_add_fusion.tabs, f32[4,128,128]{2,1,0:T(8,128)S(1)} %pad_maximum_fusion.1.patch_ref), custom_call_target="tpu_custom_call" | custom-call | flops 655360 | bytes 10485760 | tf_op jit(solution)/shard_map/pallas_call | solution.py:441
  50.9 1.3 %collective-permute-done.9.refs_3_ = f32[4,128,128]{2,1,0:T(8,128)S(1)} collective-permute-done((f32[4,128,128]{2,1,0:T(8,128)S(1)}, f32[4,128,128]{2,1,0:T(8,128)S(1)}, u32[]{:S(2)}, u32[]{:S(2)}) %collective-permute-start.9) | collective-permute-done | bytes 262176 | tf_op jit(solution)/shard_map/ppermute | solution.py:516
  52.2 7.4 %shard_map.116 = (f32[128,128]{1,0:T(8,128)S(1)}, f32[16,32,128]{2,1,0:T(8,128)S(1)}, f32[512,128]{1,0:T(8,128)S(1)}, bf16[2,384,256]{2,1,0:T(8,128)(2,1)S(1)}) custom-call(s32[576]{0:T(1024)S(1)} %concatenate.10.refs_0_, s32[264]{0:T(512)S(1)} %get-tuple-element.27.refs_1_, f32[4,128,128]{2,1,0:T(8,128)S(1)} %collective-permute-done.8.refs_2_, ...), custom_call_target="tpu_custom_call" | custom-call | tf_op jit(solution)/shard_map/pallas_call | solution.py:488
  59.6 1.0 collective-permute-start.12
  61.0 1.4 %collective-permute-start.10 = (f32[128,128]{1,0:T(8,128)S(1)}, f32[128,128]{1,0:T(8,128)S(1)}, u32[]{:S(2)}, u32[]{:S(2)}) collective-permute-start(f32[128,128]{1,0:T(8,128)S(1)} %get-tuple-element.32), channel_id=1, source_target_pairs={{0,4},{4,8},{8,12},{12,0},{1,5},{5,9},{9,13},{13,1},{2,6},{6,10},{... | collective-permute-start | bytes 196616 | tf_op jit(solution)/shard_map/ppermute | solution.py:505
  62.7 4.3 %collective-permute-done.11 = f32[128,128]{1,0:T(8,128)S(1)} collective-permute-done((f32[128,128]{1,0:T(8,128)S(1)}, f32[128,128]{1,0:T(8,128)S(1)}, u32[]{:S(2)}, u32[]{:S(2)}) %collective-permute-start.11) | collective-permute-done | bytes 65568 | tf_op jit(solution)/shard_map/ppermute | solution.py:505
  67.1 4.0 %collective-permute-start.14 = (f32[4,128,128]{2,1,0:T(8,128)S(1)}, f32[4,128,128]{2,1,0:T(8,128)S(1)}, u32[]{:S(2)}, u32[]{:S(2)}) collective-permute-start(f32[4,128,128]{2,1,0:T(8,128)S(1)} %pad_maximum_fusion.2.patch_ref), channel_id=1, source_target_pairs={{1,2},{2,1},{5,6},{6,5},{9,10},{10,9},{13,14},{14,13},{17,18},{18,... | collective-permute-start | bytes 786440 | tf_op jit(solution)/shard_map/ppermute | solution.py:516
  71.2 2.7 %shard_map.117.refs_4_ = f32[2,64,128]{2,1,0:T(8,128)S(1)} custom-call(s32[320]{0:T(512)S(1)} %pad_add_fusion.tabs, f32[4,128,128]{2,1,0:T(8,128)S(1)} %pad_maximum_fusion.2.patch_ref), custom_call_target="tpu_custom_call" | custom-call | flops 655360 | bytes 10485760 | tf_op jit(solution)/shard_map/pallas_call | solution.py:441
  73.8 1.3 %collective-permute-done.14.refs_3_ = f32[4,128,128]{2,1,0:T(8,128)S(1)} collective-permute-done((f32[4,128,128]{2,1,0:T(8,128)S(1)}, f32[4,128,128]{2,1,0:T(8,128)S(1)}, u32[]{:S(2)}, u32[]{:S(2)}) %collective-permute-start.14) | collective-permute-done | bytes 262176 | tf_op jit(solution)/shard_map/ppermute | solution.py:516
  75.1 7.5 %shard_map.118 = (f32[128,128]{1,0:T(8,128)S(1)}, f32[16,32,128]{2,1,0:T(8,128)S(1)}, f32[512,128]{1,0:T(8,128)S(1)}, bf16[2,384,256]{2,1,0:T(8,128)(2,1)S(1)}) custom-call(s32[576]{0:T(1024)S(1)} %concatenate.10.refs_0_, s32[264]{0:T(512)S(1)} %get-tuple-element.27.refs_1_, f32[4,128,128]{2,1,0:T(8,128)S(1)} %collective-permute-done.13.refs_2_, ...), custom_call_target="tpu_custom_call" | custom-call | tf_op jit(solution)/shard_map/pallas_call | solution.py:488
  82.7 1.2 %collective-permute-start.17 = (f32[128,128]{1,0:T(8,128)S(1)}, f32[128,128]{1,0:T(8,128)S(1)}, u32[]{:S(2)}, u32[]{:S(2)}) collective-permute-start(f32[128,128]{1,0:T(8,128)S(1)} %get-tuple-element.36), channel_id=1, source_target_pairs={{0,12},{4,0},{8,4},{12,8},{1,13},{5,1},{9,5},{13,9},{2,14},{6,2},{... | collective-permute-start | bytes 196616 | tf_op jit(solution)/shard_map/ppermute | solution.py:505
  83.9 1.2 %collective-permute-start.15 = (f32[128,128]{1,0:T(8,128)S(1)}, f32[128,128]{1,0:T(8,128)S(1)}, u32[]{:S(2)}, u32[]{:S(2)}) collective-permute-start(f32[128,128]{1,0:T(8,128)S(1)} %get-tuple-element.36), channel_id=1, source_target_pairs={{0,4},{4,8},{8,12},{12,0},{1,5},{5,9},{9,13},{13,1},{2,6},{6,10},{... | collective-permute-start | bytes 196616 | tf_op jit(solution)/shard_map/ppermute | solution.py:505
  85.9 4.5 %collective-permute-done.16 = f32[128,128]{1,0:T(8,128)S(1)} collective-permute-done((f32[128,128]{1,0:T(8,128)S(1)}, f32[128,128]{1,0:T(8,128)S(1)}, u32[]{:S(2)}, u32[]{:S(2)}) %collective-permute-start.16) | collective-permute-done | bytes 65568 | tf_op jit(solution)/shard_map/ppermute | solution.py:505
  90.4 4.0 %collective-permute-start.19 = (f32[4,128,128]{2,1,0:T(8,128)S(1)}, f32[4,128,128]{2,1,0:T(8,128)S(1)}, u32[]{:S(2)}, u32[]{:S(2)}) collective-permute-start(f32[4,128,128]{2,1,0:T(8,128)S(1)} %pad_maximum_fusion.3.patch_ref), channel_id=1, source_target_pairs={{1,2},{2,1},{5,6},{6,5},{9,10},{10,9},{13,14},{14,13},{17,18},{18,... | collective-permute-start | bytes 786440 | tf_op jit(solution)/shard_map/ppermute | solution.py:516
  94.5 2.7 %shard_map.119.refs_4_ = f32[2,64,128]{2,1,0:T(8,128)S(1)} custom-call(s32[320]{0:T(512)S(1)} %pad_add_fusion.tabs, f32[4,128,128]{2,1,0:T(8,128)S(1)} %pad_maximum_fusion.3.patch_ref), custom_call_target="tpu_custom_call" | custom-call | flops 655360 | bytes 10485760 | tf_op jit(solution)/shard_map/pallas_call | solution.py:441
  97.2 1.3 %collective-permute-done.19.refs_3_ = f32[4,128,128]{2,1,0:T(8,128)S(1)} collective-permute-done((f32[4,128,128]{2,1,0:T(8,128)S(1)}, f32[4,128,128]{2,1,0:T(8,128)S(1)}, u32[]{:S(2)}, u32[]{:S(2)}) %collective-permute-start.19) | collective-permute-done | bytes 262176 | tf_op jit(solution)/shard_map/ppermute | solution.py:516
  98.5 5.9 %shard_map.120 = (f32[3,32,128]{2,1,0:T(8,128)}, f32[9,32,128]{2,1,0:T(8,128)}, f32[9,32,128]{2,1,0:T(8,128)}) custom-call(s32[576]{0:T(1024)S(1)} %concatenate.10.refs_0_, s32[264]{0:T(512)S(1)} %get-tuple-element.27.refs_1_, f32[4,128,128]{2,1,0:T(8,128)S(1)} %collective-permute-done.18.refs_2_, f32[4,128,128]{2,1,0:T(8,128)S(1)} %collective-permute-done.19.refs_3_, ...), custom_call_target="tpu_custom_call" | custom-call | tf_op jit(solution)/shard_map/pallas_call | solution.py:488
  (74 shorter events, 7.6 us)
Async XLA Ops:
  0.6 0.7 copy-start.7
  0.6 0.7 copy-start.8
  0.7 1.4 %copy-start.6 = (s32[32]{0:T(128)S(1)}, s32[32]{0:T(128)}, u32[]{:S(2)}) copy-start(s32[32]{0:T(128)} %param.17) | copy-start | bytes 388
  0.7 1.4 %copy-start.4 = (s32[32,128]{1,0:T(8,128)S(1)}, s32[32,128]{1,0:T(8,128)}, u32[]{:S(2)}) copy-start(s32[32,128]{1,0:T(8,128)} %refs_1_.1) | copy-start | bytes 49156
  0.7 1.4 %copy-start.5 = (f32[32,128]{1,0:T(8,128)S(1)}, f32[32,128]{1,0:T(8,128)}, u32[]{:S(2)}) copy-start(f32[32,128]{1,0:T(8,128)} %refs_5_.1) | copy-start | bytes 49156
  2.1 0.9 copy-start
  3.0 0.9 copy-start.1
  3.9 0.8 copy-start.2
  4.7 0.8 copy-start.3
  8.2 7.4 %collective-permute-start.1 = (f32[136,128]{1,0:T(8,128)S(1)}, f32[136,128]{1,0:T(8,128)S(1)}, u32[]{:S(2)}, u32[]{:S(2)}) collective-permute-start(f32[136,128]{1,0:T(8,128)S(1)} %get-tuple-element.52), channel_id=1, source_target_pairs={{0,8},{4,12},{8,0},{12,4},{1,9},{5,13},{9,1},{13,5},{2,10},{6,14},... | collective-permute-start | bytes 208904 | tf_op jit(solution)/shard_map/ppermute | solution.py:505
  11.4 5.0 %collective-permute-start = (f32[136,128]{1,0:T(8,128)S(1)}, f32[136,128]{1,0:T(8,128)S(1)}, u32[]{:S(2)}, u32[]{:S(2)}) collective-permute-start(f32[136,128]{1,0:T(8,128)S(1)} %get-tuple-element.52), channel_id=1, source_target_pairs={{0,4},{4,8},{8,12},{12,0},{1,5},{5,9},{9,13},{13,1},{2,6},{6,10},{... | collective-permute-start | bytes 208904 | tf_op jit(solution)/shard_map/ppermute | solution.py:505
  12.7 4.1 %collective-permute-start.2 = (f32[136,128]{1,0:T(8,128)S(1)}, f32[136,128]{1,0:T(8,128)S(1)}, u32[]{:S(2)}, u32[]{:S(2)}) collective-permute-start(f32[136,128]{1,0:T(8,128)S(1)} %get-tuple-element.52), channel_id=1, source_target_pairs={{0,12},{4,0},{8,4},{12,8},{1,13},{5,1},{9,5},{13,9},{2,14},{6,2},{... | collective-permute-start | bytes 208904 | tf_op jit(solution)/shard_map/ppermute | solution.py:505
  16.8 9.6 %collective-permute-start.4 = (f32[4,136,128]{2,1,0:T(8,128)S(1)}, f32[4,136,128]{2,1,0:T(8,128)S(1)}, u32[]{:S(2)}, u32[]{:S(2)}) collective-permute-start(f32[4,136,128]{2,1,0:T(8,128)S(1)} %pad_maximum_fusion.patch_ref), channel_id=1, source_target_pairs={{1,2},{2,1},{5,6},{6,5},{9,10},{10,9},{13,14},{14,13},{17,18},{18,... | collective-permute-start | bytes 835592 | tf_op jit(solution)/shard_map/ppermute | solution.py:516
  22.2 4.2 %collective-permute-start.3 = (f32[4,136,128]{2,1,0:T(8,128)S(1)}, f32[4,136,128]{2,1,0:T(8,128)S(1)}, u32[]{:S(2)}, u32[]{:S(2)}) collective-permute-start(f32[4,136,128]{2,1,0:T(8,128)S(1)} %pad_maximum_fusion.patch_ref), channel_id=1, source_target_pairs={{0,1},{1,0},{2,3},{3,2},{4,5},{5,4},{6,7},{7,6},{8,9},{9,8},{10,11... | collective-permute-start | bytes 835592 | tf_op jit(solution)/shard_map/ppermute | solution.py:516
  35.1 5.0 %collective-permute-start.7 = (f32[128,128]{1,0:T(8,128)S(1)}, f32[128,128]{1,0:T(8,128)S(1)}, u32[]{:S(2)}, u32[]{:S(2)}) collective-permute-start(f32[128,128]{1,0:T(8,128)S(1)} %get-tuple-element.28), channel_id=1, source_target_pairs={{0,12},{4,0},{8,4},{12,8},{1,13},{5,1},{9,5},{13,9},{2,14},{6,2},{... | collective-permute-start | bytes 196616 | tf_op jit(solution)/shard_map/ppermute | solution.py:505
  38.2 5.8 %collective-permute-start.6 = (f32[128,128]{1,0:T(8,128)S(1)}, f32[128,128]{1,0:T(8,128)S(1)}, u32[]{:S(2)}, u32[]{:S(2)}) collective-permute-start(f32[128,128]{1,0:T(8,128)S(1)} %get-tuple-element.28), channel_id=1, source_target_pairs={{0,8},{4,12},{8,0},{12,4},{1,9},{5,13},{9,1},{13,5},{2,10},{6,14},... | collective-permute-start | bytes 196616 | tf_op jit(solution)/shard_map/ppermute | solution.py:505
  38.2 5.8 %collective-permute-start.5 = (f32[128,128]{1,0:T(8,128)S(1)}, f32[128,128]{1,0:T(8,128)S(1)}, u32[]{:S(2)}, u32[]{:S(2)}) collective-permute-start(f32[128,128]{1,0:T(8,128)S(1)} %get-tuple-element.28), channel_id=1, source_target_pairs={{0,4},{4,8},{8,12},{12,0},{1,5},{5,9},{9,13},{13,1},{2,6},{6,10},{... | collective-permute-start | bytes 196616 | tf_op jit(solution)/shard_map/ppermute | solution.py:505
  44.0 8.2 %collective-permute-start.9 = (f32[4,128,128]{2,1,0:T(8,128)S(1)}, f32[4,128,128]{2,1,0:T(8,128)S(1)}, u32[]{:S(2)}, u32[]{:S(2)}) collective-permute-start(f32[4,128,128]{2,1,0:T(8,128)S(1)} %pad_maximum_fusion.1.patch_ref), channel_id=1, source_target_pairs={{1,2},{2,1},{5,6},{6,5},{9,10},{10,9},{13,14},{14,13},{17,18},{18,... | collective-permute-start | bytes 786440 | tf_op jit(solution)/shard_map/ppermute | solution.py:516
  48.2 4.0 %collective-permute-start.8 = (f32[4,128,128]{2,1,0:T(8,128)S(1)}, f32[4,128,128]{2,1,0:T(8,128)S(1)}, u32[]{:S(2)}, u32[]{:S(2)}) collective-permute-start(f32[4,128,128]{2,1,0:T(8,128)S(1)} %pad_maximum_fusion.1.patch_ref), channel_id=1, source_target_pairs={{0,1},{1,0},{2,3},{3,2},{4,5},{5,4},{6,7},{7,6},{8,9},{9,8},{10,11... | collective-permute-start | bytes 786440 | tf_op jit(solution)/shard_map/ppermute | solution.py:516
  59.6 3.2 %collective-permute-start.12 = (f32[128,128]{1,0:T(8,128)S(1)}, f32[128,128]{1,0:T(8,128)S(1)}, u32[]{:S(2)}, u32[]{:S(2)}) collective-permute-start(f32[128,128]{1,0:T(8,128)S(1)} %get-tuple-element.32), channel_id=1, source_target_pairs={{0,12},{4,0},{8,4},{12,8},{1,13},{5,1},{9,5},{13,9},{2,14},{6,2},{... | collective-permute-start | bytes 196616 | tf_op jit(solution)/shard_map/ppermute | solution.py:505
  60.6 6.5 %collective-permute-start.11 = (f32[128,128]{1,0:T(8,128)S(1)}, f32[128,128]{1,0:T(8,128)S(1)}, u32[]{:S(2)}, u32[]{:S(2)}) collective-permute-start(f32[128,128]{1,0:T(8,128)S(1)} %get-tuple-element.32), channel_id=1, source_target_pairs={{0,8},{4,12},{8,0},{12,4},{1,9},{5,13},{9,1},{13,5},{2,10},{6,14},... | collective-permute-start | bytes 196616 | tf_op jit(solution)/shard_map/ppermute | solution.py:505
  61.0 6.1 %collective-permute-start.10 = (f32[128,128]{1,0:T(8,128)S(1)}, f32[128,128]{1,0:T(8,128)S(1)}, u32[]{:S(2)}, u32[]{:S(2)}) collective-permute-start(f32[128,128]{1,0:T(8,128)S(1)} %get-tuple-element.32), channel_id=1, source_target_pairs={{0,4},{4,8},{8,12},{12,0},{1,5},{5,9},{9,13},{13,1},{2,6},{6,10},{... | collective-permute-start | bytes 196616 | tf_op jit(solution)/shard_map/ppermute | solution.py:505
  67.1 8.1 %collective-permute-start.14 = (f32[4,128,128]{2,1,0:T(8,128)S(1)}, f32[4,128,128]{2,1,0:T(8,128)S(1)}, u32[]{:S(2)}, u32[]{:S(2)}) collective-permute-start(f32[4,128,128]{2,1,0:T(8,128)S(1)} %pad_maximum_fusion.2.patch_ref), channel_id=1, source_target_pairs={{1,2},{2,1},{5,6},{6,5},{9,10},{10,9},{13,14},{14,13},{17,18},{18,... | collective-permute-start | bytes 786440 | tf_op jit(solution)/shard_map/ppermute | solution.py:516
  71.1 4.0 %collective-permute-start.13 = (f32[4,128,128]{2,1,0:T(8,128)S(1)}, f32[4,128,128]{2,1,0:T(8,128)S(1)}, u32[]{:S(2)}, u32[]{:S(2)}) collective-permute-start(f32[4,128,128]{2,1,0:T(8,128)S(1)} %pad_maximum_fusion.2.patch_ref), channel_id=1, source_target_pairs={{0,1},{1,0},{2,3},{3,2},{4,5},{5,4},{6,7},{7,6},{8,9},{9,8},{10,11... | collective-permute-start | bytes 786440 | tf_op jit(solution)/shard_map/ppermute | solution.py:516
  82.7 3.2 %collective-permute-start.17 = (f32[128,128]{1,0:T(8,128)S(1)}, f32[128,128]{1,0:T(8,128)S(1)}, u32[]{:S(2)}, u32[]{:S(2)}) collective-permute-start(f32[128,128]{1,0:T(8,128)S(1)} %get-tuple-element.36), channel_id=1, source_target_pairs={{0,12},{4,0},{8,4},{12,8},{1,13},{5,1},{9,5},{13,9},{2,14},{6,2},{... | collective-permute-start | bytes 196616 | tf_op jit(solution)/shard_map/ppermute | solution.py:505
  83.9 6.5 %collective-permute-start.16 = (f32[128,128]{1,0:T(8,128)S(1)}, f32[128,128]{1,0:T(8,128)S(1)}, u32[]{:S(2)}, u32[]{:S(2)}) collective-permute-start(f32[128,128]{1,0:T(8,128)S(1)} %get-tuple-element.36), channel_id=1, source_target_pairs={{0,8},{4,12},{8,0},{12,4},{1,9},{5,13},{9,1},{13,5},{2,10},{6,14},... | collective-permute-start | bytes 196616 | tf_op jit(solution)/shard_map/ppermute | solution.py:505
  83.9 6.5 %collective-permute-start.15 = (f32[128,128]{1,0:T(8,128)S(1)}, f32[128,128]{1,0:T(8,128)S(1)}, u32[]{:S(2)}, u32[]{:S(2)}) collective-permute-start(f32[128,128]{1,0:T(8,128)S(1)} %get-tuple-element.36), channel_id=1, source_target_pairs={{0,4},{4,8},{8,12},{12,0},{1,5},{5,9},{9,13},{13,1},{2,6},{6,10},{... | collective-permute-start | bytes 196616 | tf_op jit(solution)/shard_map/ppermute | solution.py:505
  90.4 8.0 %collective-permute-start.19 = (f32[4,128,128]{2,1,0:T(8,128)S(1)}, f32[4,128,128]{2,1,0:T(8,128)S(1)}, u32[]{:S(2)}, u32[]{:S(2)}) collective-permute-start(f32[4,128,128]{2,1,0:T(8,128)S(1)} %pad_maximum_fusion.3.patch_ref), channel_id=1, source_target_pairs={{1,2},{2,1},{5,6},{6,5},{9,10},{10,9},{13,14},{14,13},{17,18},{18,... | collective-permute-start | bytes 786440 | tf_op jit(solution)/shard_map/ppermute | solution.py:516
  94.4 4.0 %collective-permute-start.18 = (f32[4,128,128]{2,1,0:T(8,128)S(1)}, f32[4,128,128]{2,1,0:T(8,128)S(1)}, u32[]{:S(2)}, u32[]{:S(2)}) collective-permute-start(f32[4,128,128]{2,1,0:T(8,128)S(1)} %pad_maximum_fusion.3.patch_ref), channel_id=1, source_target_pairs={{0,1},{1,0},{2,3},{3,2},{4,5},{5,4},{6,7},{7,6},{8,9},{9,8},{10,11... | collective-permute-start | bytes 786440 | tf_op jit(solution)/shard_map/ppermute | solution.py:516

commit v3 on v2

--- a/solution.py
+++ b/solution.py
@@ -195,34 +195,36 @@
 
 def scatter_listed(tabs, bins, listed, sides, sums, spare, lane):
     total = tabs.shape[0] // 2
-    for side, patch_ref in enumerate(sides):
-        count = patch_ref.shape[0] * bins
-        many = listed[2 * count + side]
-
-        def some(at, _, side=side, patch_ref=patch_ref, count=count, many=many):
-            found = []
-            for step in range(4):
-                n = at * 4 + step
-                used = n < many
+    count = sides[0].shape[0] * bins
+    many = [listed[2 * count + side] for side in range(2)]
+
+    def some(at, _):
+        found = []
+        for step in range(8):
+            n = at * 8 + step
+            for side, patch_ref in enumerate(sides):
+                used = n < many[side]
                 which = listed[side * count + jnp.where(used, n, 0)]
-                row = jnp.where(used, tabs[bins + side * count + which], spare)
-                z = tabs[total + bins + side * count + which]
+                which = jnp.where(used, which, 0)
+                place = bins + side * count + which
+                row = jnp.where(used, tabs[place], spare)
+                z = tabs[total + place]
                 inner = which % bins
                 start = pl.multiple_of((inner // 16) * 64, 64)
                 patch = patch_ref[which // bins, pl.ds(start, 64), :]
                 found.append((row, patch, z + 128 - 8 * (inner % 16), z))
-            for row, patch, shift, z in found:
-                add_patch(sums, row, patch, shift, z, lane)
-            return _
-
-        lax.fori_loop(0, (many + 3) // 4, some, 0)
+        for row, patch, shift, z in found:
+            add_patch(sums, row, patch, shift, z, lane)
+        return _
+
+    lax.fori_loop(0, (jnp.maximum(many[0], many[1]) + 7) // 8, some, 0)
 
 
 def kernel(first, listing, last, *refs):
     refs = list(refs)
     take = lambda n: [refs.pop(0) for _ in range(n)]
     if first:
-        sources = take(6)
+        sources = take(9)
         bins = sources[5].shape[0]
     else:
         (tabs,) = take(1)
@@ -236,9 +238,9 @@
         patch_out, state_out, params_out, depth_out = take(4)
     if listing:
         (listed,) = take(1)
-    wide, products = take(2)
+    wides, products_all = take(2)
     if first:
-        held = take(6)
+        held = take(9)
         arrived = refs.pop(0)
         copies = [
             pltpu.make_async_copy(source, target, arrived.at[at])
@@ -248,11 +250,17 @@
             copy.start()
         for copy in copies:
             copy.wait()
-        offsets_in, cell, velocity_in, affine_in, strain, mass_in = held
+        offsets_in, cell, velocity_in, affine_in, strain, mass_in, owner, corner, depth_at = held
+        facts = slice(4 * bins, 4 * bins + 8)
+        patch_out[facts, :] = jnp.zeros((8, 128), F32)
+        known = (owner[...] * TILE + corner[0:1, :] + 2, corner[1:2, :], depth_at[...])
+        for at, value in enumerate(known):
+            patch_out[4 * bins + at : 4 * bins + at + 1, 0:bins] = value.astype(F32)
+        patch_out[4 * bins + 3 : 4 * bins + 4, 0:bins] = jnp.ones((1, bins), F32)
     else:
         sums, results = take(2)
     if not last:
-        wide_low, blends, products_low = take(3)
+        wides_low, blends, products_lows = take(3)
     groups = bins // 16
     sub = lax.broadcasted_iota(jnp.int32, (8, 128), 0)
     lane = lax.broadcasted_iota(jnp.int32, (64, 128), 1)
@@ -302,6 +310,7 @@
         scatter_listed(tabs, bins, listed, [patch_a, patch_b], sums, spare, lane)
         for g in range(groups):
             compact = compact_in[g] + gather_group(tabs, g, sums, lane)
+            wide, products = wides.at[g], products_all.at[g]
             channel = lax.broadcasted_iota(jnp.int32, (64, 128), 0) & 3
             mass = jnp.where(channel == 0, compact, 0.0)
             mass = mass + pltpu.roll(mass, 1, 0)
@@ -319,11 +328,11 @@
                 wide[...], depth[g, 0:256, :], preferred_element_type=F32
             ) + jnp.dot(wide[:, 0:128], depth[g, 256:384, :], preferred_element_type=F32)
 
-            def finish(slot, _, g=g):
+            def finish(slot, _, g=g, products=products):
                 base = (g * 16 + slot) * 16
                 weights, moments = y_patterns(params, base, sub)
                 x0 = row_of(params, base + 8)
-                at = pl.multiple_of(slot * 64, 64)
+                at = slot * 64
                 plain = [None, None]
                 along = [None, None]
                 deep = [None, None]
@@ -343,12 +352,13 @@
                     moments[0] * plain[0] + moments[1] * plain[1],
                     weights[0] * deep[0] + weights[1] * deep[1],
                 )
-                place = pl.multiple_of((g * 16 + slot) * 32, 32)
+                place = (g * 16 + slot) * 32
                 for kind, value in enumerate(found):
                     results[pl.ds(place + 8 * kind, 8), :] = value + pltpu.roll(value, 4, 0)
                 return _
 
-            lax.fori_loop(0, 16, finish, 0, unroll=4)
+            for slot in range(16):
+                finish(slot, 0)
 
         for g8 in range(bins // 8):
             span = pl.ds(g8 * 8, 8)
@@ -380,10 +390,12 @@
     if not last:
         depth_weights(bins, params_out, depth_out)
         for g in range(groups):
-
-            def build(slot, _, g=g):
+            wide, wide_low = wides.at[g], wides_low.at[g]
+            products, products_low = products_all.at[g], products_lows.at[g]
+
+            def build(slot, _, g=g, wide=wide, wide_low=wide_low):
                 base = (g * 16 + slot) * 16
-                place = pl.multiple_of((g * 16 + slot) * 32, 32)
+                place = (g * 16 + slot) * 32
                 weights, moments = y_patterns(params_out, base, sub)
                 x0 = row_of(params_out, base + 8)
                 pushed, b0, b1, b2 = [blends[pl.ds(place + 8 * k, 8), :] for k in range(4)]
@@ -399,12 +411,13 @@
                         deep.append(depthwise * weights[half])
                 value = jnp.concatenate([fill(plain), fill(deep)], axis=1)
                 high, low = split(value)
-                at = pl.ds(pl.multiple_of(slot * 64, 64), 64)
+                at = pl.ds(slot * 64, 64)
                 wide[at, :] = high
                 wide_low[at, :] = low
                 return _
 
-            lax.fori_loop(0, 16, build, 0, unroll=2)
+            for slot in range(16):
+                build(slot, 0)
             turned = (((1,), (1,)), ((), ()))
             products[...] = lax.dot_general(
                 wide[...], depth_out[g, 128:384, :], turned, preferred_element_type=F32
@@ -456,16 +469,19 @@
         outs = [shape_of(3, bins, 128), shape_of(9, bins, 128), shape_of(9, bins, 128)]
     else:
         outs = [
-            shape_of(4 * bins, 128),
+            shape_of(4 * bins + (8 if first else 0), 128),
             shape_of(16, bins, 128),
             shape_of(16 * bins, 128),
             shape_of(bins // 16, 384, 256, dtype=BF16),
         ]
     out_specs = [VMEM_SPEC] * len(outs)
-    scratch = [pltpu.VMEM((1024, 256), BF16), pltpu.VMEM((1024, 256), F32)]
+    scratch = [
+        pltpu.VMEM((bins // 16, 1024, 256), BF16),
+        pltpu.VMEM((bins // 16, 1024, 256), F32),
+    ]
     in_specs = [VMEM_SPEC] * len(operands)
     if first:
-        in_specs = [pl.BlockSpec(memory_space=pl.ANY)] * len(operands)
+        in_specs = [pl.BlockSpec(memory_space=pltpu.HBM)] * len(operands)
         scratch += [pltpu.VMEM(op.shape, op.dtype) for op in operands]
         scratch += [pltpu.SemaphoreType.DMA((len(operands),))]
     else:
@@ -481,10 +497,12 @@
         ]
     if not last:
         scratch += [
-            pltpu.VMEM((1024, 256), BF16),
+            pltpu.VMEM((bins // 16, 1024, 256), BF16),
             pltpu.VMEM((32 * bins, 128), F32),
-            pltpu.VMEM((1024, 128), F32),
+            pltpu.VMEM((bins // 16, 1024, 128), F32),
         ]
+    if first:
+        operands = [pltpu.with_memory_space_constraint(op, pltpu.HBM) for op in operands]
     return pl.pallas_call(
         functools.partial(kernel, first, listing, last),
         out_shape=outs,
@@ -525,22 +543,7 @@
     total_y = TILE * lax.axis_size("gy")
     place_y = lax.axis_index("gy")
     turn = lambda array: jnp.transpose(array, (1, 0, 2))
-    corner_x = owner_row[:, 0] * TILE + anchor_xy[:, 0]
-    own_row = (corner_x + 2) * ROWS_X + 4 * (anchor_xy[:, 1] + LOW_Y)
-
-    serial = jnp.arange(64, dtype=jnp.int32)[None, :, None]
-    group = bins // 16
-    spread = lambda values: jnp.repeat(values.reshape(group, 16), 8, axis=1)[:, None, :]
-    at_x = spread(corner_x) + serial // 16
-    at_y = spread(place_y * TILE + anchor_xy[:, 1]) + serial // 4 % 4
-    at_z = spread(anchor_z) + (jnp.arange(128, dtype=jnp.int32) % 8)[None, None, :]
-    channel = serial % 4
-    at = jnp.where(channel == 1, at_x, jnp.where(channel == 2, at_y, at_z))
-    limit = jnp.where(channel == 1, total_x, jnp.where(channel == 2, total_y, CZ))
-    in_grid = (at_x >= 0) & (at_x < total_x) & (at_y >= 0) & (at_y < total_y)
-    inside = ((at >= 2) & (at < limit - 2) & (channel > 0) & in_grid).astype(F32)
-
-    patch, state, params, depth = run_kernel(
+    payload, state, params, depth = run_kernel(
         True,
         False,
         False,
@@ -553,13 +556,24 @@
             turn(affine),
             turn(strain),
             particle_mass,
+            owner_row.T,
+            anchor_xy.T,
+            anchor_z[None, :],
         ],
     )
-    facts = jnp.stack(
-        [corner_x + 2, anchor_xy[:, 1], anchor_z, jnp.ones((bins,), jnp.int32)]
-    ).astype(F32)
-    facts = jnp.pad(facts, ((0, 4), (0, 128 - bins)))
-    payload = jnp.concatenate([patch, facts], axis=0)
+    def inside_grid(late_x, late_y, late_z):
+        serial = jnp.arange(64, dtype=jnp.int32)[None, :, None]
+        group = bins // 16
+        spread = lambda values: jnp.repeat(values.reshape(group, 16), 8, axis=1)[:, None, :]
+        at_x = spread(late_x) + serial // 16
+        at_y = spread(place_y * TILE + late_y) + serial // 4 % 4
+        at_z = spread(late_z) + (jnp.arange(128, dtype=jnp.int32) % 8)[None, None, :]
+        channel = serial % 4
+        at = jnp.where(channel == 1, at_x, jnp.where(channel == 2, at_y, at_z))
+        limit = jnp.where(channel == 1, total_x, jnp.where(channel == 2, total_y, CZ))
+        in_grid = (at_x >= 0) & (at_x < total_x) & (at_y >= 0) & (at_y < total_y)
+        inside = ((at >= 2) & (at < limit - 2) & (channel > 0) & in_grid).astype(F32)
+        return inside
 
     def places(block, move):
         known = block[:, 4 * bins : 4 * bins + 4, 0:bins].astype(jnp.int32)
@@ -573,6 +587,12 @@
         column = column_of(payload)
         beside = neighbours_of(column)
         if substep == 0:
+            own = payload[4 * bins : 4 * bins + 3, 0:bins].astype(jnp.int32)
+            own_row = own[0] * ROWS_X + 4 * (own[1] + LOW_Y)
+            anchor_z = own[2]
+            late, _ = lax.optimization_barrier((payload[4 * bins : 4 * bins + 3], column))
+            late = late[:, 0:bins].astype(jnp.int32)
+            inside = inside_grid(late[0] - 2, late[1], late[2])
             row, z = places(column, 0)
             column_tabs = jnp.concatenate([own_row, row, anchor_z, z])
             row_a, z_a = places(beside[0], step_a)

time: 105 us -> 90.6 us (0.86); the launches traced: 104 us -> 91.1 us
  Pallas kernels: 42.3 us -> 32 us
  waiting for transfers between devices: 21.3 us -> 28.3 us
  starting transfers between devices: 33.3 us -> 28.2 us
  local copies, waits for them, and re-layouts: 5.37 us -> 1.31 us
    pallas_call x5, Pallas kernels: 31.6 us -> 21.3 us  [run_kernel(): pl.pallas_call(functools.partial(kernel, first, listing, last), out_shape...]
    ppermute x12, waiting for transfers between devices: 16.2 us -> 23.6 us  [column_of(): pieces.append(lax.ppermute(payload, 'gx', pairs))]
    ppermute x8, starting transfers between devices: 17.9 us -> 14.3 us  [neighbours_of(): lax.ppermute(column, 'gy', pairs)]
    unnamed x18 -> x0, local copies, waits for them, and re-layouts: 3.48 us -> none
    ppermute x12, starting transfers between devices: 15.4 us -> 13.8 us  [column_of(): pieces.append(lax.ppermute(payload, 'gx', pairs))]
  transfers between devices with their start and end apart: 20 -> 20, of which waited for: 12 -> 11; matrix products, arithmetic and copies ran while one was open for 1% -> 1% of each run, Pallas kernels for 10% -> 12%
where the time goes in v3:
time: 90.6 us; the launch traced here: 91.1 us
  Pallas kernels  32 us (35%)
  waiting for transfers between devices  28.3 us (31%)
  starting transfers between devices  28.2 us (31%)
  local copies, waits for them, and re-layouts  1.31 us (1%)
    ppermute x12, waiting for transfers between devices, column_of(): pieces.append(lax.ppermute(payload, 'gx', pairs))  23.6 us
    pallas_call x5, Pallas kernels, run_kernel(): pl.pallas_call(functools.partial(kernel, first, listing, last), out_shape...  21.3 us
    ppermute x8, starting transfers between devices, neighbours_of(): lax.ppermute(column, 'gy', pairs)  14.3 us
    ppermute x12, starting transfers between devices, column_of(): pieces.append(lax.ppermute(payload, 'gx', pairs))  13.8 us
    pallas_call x4, Pallas kernels, run_column(): pl.pallas_call(functools.partial(column_kernel, bins), out_shape=shape_of...  10.7 us
    ppermute x8, waiting for transfers between devices, neighbours_of(): lax.ppermute(column, 'gy', pairs)  4.66 us
  transfers between devices with their start and end apart: 20, of which 11 were waited for; matrix products, arithmetic and copies ran while one was open for 1% of the time, Pallas kernels for 12%

profile of v3, /device:TPU:1, one launch (start us, length us, event | category | flops | bytes accessed | tf_op | source)
XLA Modules:
  0.0 91.1 jit_solution(540120504630458121)
XLA Ops:
  0.6 2.5 %shard_map.112 = (f32[136,128]{1,0:T(8,128)S(1)}, f32[16,32,128]{2,1,0:T(8,128)S(1)}, f32[512,128]{1,0:T(8,128)S(1)}, bf16[2,384,256]{2,1,0:T(8,128)(2,1)S(1)}) custom-call(f32[3,32,128]{2,1,0:T(8,128)} %bitcast.48, s32[32,128]{1,0:T(8,128)} %refs_1_.1, f32[3,32,128]{2,1,0:T(8,128)} %bitcast.49, f32[9,32,128]{2,1,0:T(8,128)} %bitcast.34, ...), custom_call_target="tpu_custom_call" | custom-call | tf_op jit(solution)/shard_map/pallas_call | solution.py:506
  3.1 4.2 %collective-permute-start.2 = (f32[136,128]{1,0:T(8,128)S(1)}, f32[136,128]{1,0:T(8,128)S(1)}, u32[]{:S(2)}, u32[]{:S(2)}) collective-permute-start(f32[136,128]{1,0:T(8,128)S(1)} %get-tuple-element.24), channel_id=1, source_target_pairs={{0,12},{4,0},{8,4},{12,8},{1,13},{5,1},{9,5},{13,9},{2,14},{6,2},{... | collective-permute-start | bytes 208904 | tf_op jit(solution)/shard_map/ppermute | solution.py:523
  7.3 0.5 collective-permute-start
  7.9 0.8 collective-permute-done.2
  8.7 5.8 %collective-permute-done.1 = f32[136,128]{1,0:T(8,128)S(1)} collective-permute-done((f32[136,128]{1,0:T(8,128)S(1)}, f32[136,128]{1,0:T(8,128)S(1)}, u32[]{:S(2)}, u32[]{:S(2)}) %collective-permute-start.1) | collective-permute-done | bytes 69664 | tf_op jit(solution)/shard_map/ppermute | solution.py:523
  14.6 3.6 %collective-permute-start.4 = (f32[4,136,128]{2,1,0:T(8,128)S(1)}, f32[4,136,128]{2,1,0:T(8,128)S(1)}, u32[]{:S(2)}, u32[]{:S(2)}) collective-permute-start(f32[4,136,128]{2,1,0:T(8,128)S(1)} %pad_maximum_fusion.patch_ref), channel_id=1, source_target_pairs={{1,2},{2,1},{5,6},{6,5},{9,10},{10,9},{13,14},{14,13},{17,18},{18,... | collective-permute-start | bytes 835592 | tf_op jit(solution)/shard_map/ppermute | solution.py:534
  19.4 2.7 %shard_map.113.refs_3_ = f32[2,64,128]{2,1,0:T(8,128)S(1)} custom-call(s32[320]{0:T(512)S(1)} %pad_add_fusion.tabs, f32[4,136,128]{2,1,0:T(8,128)S(1)} %pad_maximum_fusion.patch_ref), custom_call_target="tpu_custom_call" | custom-call | flops 696320 | bytes 11141120 | tf_op jit(solution)/shard_map/pallas_call | solution.py:454
  22.9 5.3 %shard_map.114 = (f32[128,128]{1,0:T(8,128)S(1)}, f32[16,32,128]{2,1,0:T(8,128)S(1)}, f32[512,128]{1,0:T(8,128)S(1)}, bf16[2,384,256]{2,1,0:T(8,128)(2,1)S(1)}, s32[264]{0:T(512)S(1)}) custom-call(s32[576]{0:T(1024)S(1)} %concatenate.6.refs_0_, f32[4,136,128]{2,1,0:T(8,128)S(1)} %collective-permute-done.3.refs_1_, ...), custom_call_target="tpu_custom_call" | custom-call | tf_op jit(solution)/shard_map/pallas_call | solution.py:506
  28.3 1.6 %collective-permute-start.7 = (f32[128,128]{1,0:T(8,128)S(1)}, f32[128,128]{1,0:T(8,128)S(1)}, u32[]{:S(2)}, u32[]{:S(2)}) collective-permute-start(f32[128,128]{1,0:T(8,128)S(1)} %get-tuple-element.30), channel_id=1, source_target_pairs={{0,12},{4,0},{8,4},{12,8},{1,13},{5,1},{9,5},{13,9},{2,14},{6,2},{... | collective-permute-start | bytes 196616 | tf_op jit(solution)/shard_map/ppermute | solution.py:523
  29.8 1.4 %collective-permute-start.5 = (f32[128,128]{1,0:T(8,128)S(1)}, f32[128,128]{1,0:T(8,128)S(1)}, u32[]{:S(2)}, u32[]{:S(2)}) collective-permute-start(f32[128,128]{1,0:T(8,128)S(1)} %get-tuple-element.30), channel_id=1, source_target_pairs={{0,4},{4,8},{8,12},{12,0},{1,5},{5,9},{9,13},{13,1},{2,6},{6,10},{... | collective-permute-start | bytes 196616 | tf_op jit(solution)/shard_map/ppermute | solution.py:523
  31.2 0.7 collective-permute-done.7
  31.9 5.2 %collective-permute-done.6 = f32[128,128]{1,0:T(8,128)S(1)} collective-permute-done((f32[128,128]{1,0:T(8,128)S(1)}, f32[128,128]{1,0:T(8,128)S(1)}, u32[]{:S(2)}, u32[]{:S(2)}) %collective-permute-start.6) | collective-permute-done | bytes 65568 | tf_op jit(solution)/shard_map/ppermute | solution.py:523
  37.1 3.5 %collective-permute-start.9 = (f32[4,128,128]{2,1,0:T(8,128)S(1)}, f32[4,128,128]{2,1,0:T(8,128)S(1)}, u32[]{:S(2)}, u32[]{:S(2)}) collective-permute-start(f32[4,128,128]{2,1,0:T(8,128)S(1)} %pad_maximum_fusion.1.patch_ref), channel_id=1, source_target_pairs={{1,2},{2,1},{5,6},{6,5},{9,10},{10,9},{13,14},{14,13},{17,18},{18,... | collective-permute-start | bytes 786440 | tf_op jit(solution)/shard_map/ppermute | solution.py:534
  40.7 2.7 %shard_map.115.refs_4_ = f32[2,64,128]{2,1,0:T(8,128)S(1)} custom-call(s32[320]{0:T(512)S(1)} %pad_add_fusion.tabs, f32[4,128,128]{2,1,0:T(8,128)S(1)} %pad_maximum_fusion.1.patch_ref), custom_call_target="tpu_custom_call" | custom-call | flops 655360 | bytes 10485760 | tf_op jit(solution)/shard_map/pallas_call | solution.py:454
  43.4 1.4 %collective-permute-done.9.refs_3_ = f32[4,128,128]{2,1,0:T(8,128)S(1)} collective-permute-done((f32[4,128,128]{2,1,0:T(8,128)S(1)}, f32[4,128,128]{2,1,0:T(8,128)S(1)}, u32[]{:S(2)}, u32[]{:S(2)}) %collective-permute-start.9) | collective-permute-done | bytes 262176 | tf_op jit(solution)/shard_map/ppermute | solution.py:534
  44.8 4.6 %shard_map.116 = (f32[128,128]{1,0:T(8,128)S(1)}, f32[16,32,128]{2,1,0:T(8,128)S(1)}, f32[512,128]{1,0:T(8,128)S(1)}, bf16[2,384,256]{2,1,0:T(8,128)(2,1)S(1)}) custom-call(s32[576]{0:T(1024)S(1)} %concatenate.6.refs_0_, s32[264]{0:T(512)S(1)} %get-tuple-element.29.refs_1_, f32[4,128,128]{2,1,0:T(8,128)S(1)} %collective-permute-done.8.refs_2_, ...), custom_call_target="tpu_custom_call" | custom-call | tf_op jit(solution)/shard_map/pallas_call | solution.py:506
  49.5 1.4 %collective-permute-start.12 = (f32[128,128]{1,0:T(8,128)S(1)}, f32[128,128]{1,0:T(8,128)S(1)}, u32[]{:S(2)}, u32[]{:S(2)}) collective-permute-start(f32[128,128]{1,0:T(8,128)S(1)} %get-tuple-element.34), channel_id=1, source_target_pairs={{0,12},{4,0},{8,4},{12,8},{1,13},{5,1},{9,5},{13,9},{2,14},{6,2},{... | collective-permute-start | bytes 196616 | tf_op jit(solution)/shard_map/ppermute | solution.py:523
  50.9 0.6 collective-permute-start.11
  51.5 1.4 %collective-permute-start.10 = (f32[128,128]{1,0:T(8,128)S(1)}, f32[128,128]{1,0:T(8,128)S(1)}, u32[]{:S(2)}, u32[]{:S(2)}) collective-permute-start(f32[128,128]{1,0:T(8,128)S(1)} %get-tuple-element.34), channel_id=1, source_target_pairs={{0,4},{4,8},{8,12},{12,0},{1,5},{5,9},{9,13},{13,1},{2,6},{6,10},{... | collective-permute-start | bytes 196616 | tf_op jit(solution)/shard_map/ppermute | solution.py:523
  52.9 5.0 %collective-permute-done.11 = f32[128,128]{1,0:T(8,128)S(1)} collective-permute-done((f32[128,128]{1,0:T(8,128)S(1)}, f32[128,128]{1,0:T(8,128)S(1)}, u32[]{:S(2)}, u32[]{:S(2)}) %collective-permute-start.11) | collective-permute-done | bytes 65568 | tf_op jit(solution)/shard_map/ppermute | solution.py:523
  57.9 3.6 %collective-permute-start.14 = (f32[4,128,128]{2,1,0:T(8,128)S(1)}, f32[4,128,128]{2,1,0:T(8,128)S(1)}, u32[]{:S(2)}, u32[]{:S(2)}) collective-permute-start(f32[4,128,128]{2,1,0:T(8,128)S(1)} %pad_maximum_fusion.2.patch_ref), channel_id=1, source_target_pairs={{1,2},{2,1},{5,6},{6,5},{9,10},{10,9},{13,14},{14,13},{17,18},{18,... | collective-permute-start | bytes 786440 | tf_op jit(solution)/shard_map/ppermute | solution.py:534
  61.6 2.7 %shard_map.117.refs_4_ = f32[2,64,128]{2,1,0:T(8,128)S(1)} custom-call(s32[320]{0:T(512)S(1)} %pad_add_fusion.tabs, f32[4,128,128]{2,1,0:T(8,128)S(1)} %pad_maximum_fusion.2.patch_ref), custom_call_target="tpu_custom_call" | custom-call | flops 655360 | bytes 10485760 | tf_op jit(solution)/shard_map/pallas_call | solution.py:454
  64.3 1.3 %collective-permute-done.14.refs_3_ = f32[4,128,128]{2,1,0:T(8,128)S(1)} collective-permute-done((f32[4,128,128]{2,1,0:T(8,128)S(1)}, f32[4,128,128]{2,1,0:T(8,128)S(1)}, u32[]{:S(2)}, u32[]{:S(2)}) %collective-permute-start.14) | collective-permute-done | bytes 262176 | tf_op jit(solution)/shard_map/ppermute | solution.py:534
  65.6 4.8 %shard_map.118 = (f32[128,128]{1,0:T(8,128)S(1)}, f32[16,32,128]{2,1,0:T(8,128)S(1)}, f32[512,128]{1,0:T(8,128)S(1)}, bf16[2,384,256]{2,1,0:T(8,128)(2,1)S(1)}) custom-call(s32[576]{0:T(1024)S(1)} %concatenate.6.refs_0_, s32[264]{0:T(512)S(1)} %get-tuple-element.29.refs_1_, f32[4,128,128]{2,1,0:T(8,128)S(1)} %collective-permute-done.13.refs_2_, ...), custom_call_target="tpu_custom_call" | custom-call | tf_op jit(solution)/shard_map/pallas_call | solution.py:506
  70.4 1.1 %collective-permute-start.17 = (f32[128,128]{1,0:T(8,128)S(1)}, f32[128,128]{1,0:T(8,128)S(1)}, u32[]{:S(2)}, u32[]{:S(2)}) collective-permute-start(f32[128,128]{1,0:T(8,128)S(1)} %get-tuple-element.38), channel_id=1, source_target_pairs={{0,12},{4,0},{8,4},{12,8},{1,13},{5,1},{9,5},{13,9},{2,14},{6,2},{... | collective-permute-start | bytes 196616 | tf_op jit(solution)/shard_map/ppermute | solution.py:523
  71.9 1.4 %collective-permute-start.15 = (f32[128,128]{1,0:T(8,128)S(1)}, f32[128,128]{1,0:T(8,128)S(1)}, u32[]{:S(2)}, u32[]{:S(2)}) collective-permute-start(f32[128,128]{1,0:T(8,128)S(1)} %get-tuple-element.38), channel_id=1, source_target_pairs={{0,4},{4,8},{8,12},{12,0},{1,5},{5,9},{9,13},{13,1},{2,6},{6,10},{... | collective-permute-start | bytes 196616 | tf_op jit(solution)/shard_map/ppermute | solution.py:523
  73.3 0.7 collective-permute-done.17
  74.0 5.4 %collective-permute-done.16 = f32[128,128]{1,0:T(8,128)S(1)} collective-permute-done((f32[128,128]{1,0:T(8,128)S(1)}, f32[128,128]{1,0:T(8,128)S(1)}, u32[]{:S(2)}, u32[]{:S(2)}) %collective-permute-start.16) | collective-permute-done | bytes 65568 | tf_op jit(solution)/shard_map/ppermute | solution.py:523
  79.4 3.4 %collective-permute-start.19 = (f32[4,128,128]{2,1,0:T(8,128)S(1)}, f32[4,128,128]{2,1,0:T(8,128)S(1)}, u32[]{:S(2)}, u32[]{:S(2)}) collective-permute-start(f32[4,128,128]{2,1,0:T(8,128)S(1)} %pad_maximum_fusion.3.patch_ref), channel_id=1, source_target_pairs={{1,2},{2,1},{5,6},{6,5},{9,10},{10,9},{13,14},{14,13},{17,18},{18,... | collective-permute-start | bytes 786440 | tf_op jit(solution)/shard_map/ppermute | solution.py:534
  82.8 2.7 %shard_map.119.refs_4_ = f32[2,64,128]{2,1,0:T(8,128)S(1)} custom-call(s32[320]{0:T(512)S(1)} %pad_add_fusion.tabs, f32[4,128,128]{2,1,0:T(8,128)S(1)} %pad_maximum_fusion.3.patch_ref), custom_call_target="tpu_custom_call" | custom-call | flops 655360 | bytes 10485760 | tf_op jit(solution)/shard_map/pallas_call | solution.py:454
  85.5 1.6 %collective-permute-done.19.refs_3_ = f32[4,128,128]{2,1,0:T(8,128)S(1)} collective-permute-done((f32[4,128,128]{2,1,0:T(8,128)S(1)}, f32[4,128,128]{2,1,0:T(8,128)S(1)}, u32[]{:S(2)}, u32[]{:S(2)}) %collective-permute-start.19) | collective-permute-done | bytes 262176 | tf_op jit(solution)/shard_map/ppermute | solution.py:534
  87.1 4.0 %shard_map.120 = (f32[3,32,128]{2,1,0:T(8,128)}, f32[9,32,128]{2,1,0:T(8,128)}, f32[9,32,128]{2,1,0:T(8,128)}) custom-call(s32[576]{0:T(1024)S(1)} %concatenate.6.refs_0_, s32[264]{0:T(512)S(1)} %get-tuple-element.29.refs_1_, f32[4,128,128]{2,1,0:T(8,128)S(1)} %collective-permute-done.18.refs_2_, f32[4,128,128]{2,1,0:T(8,128)S(1)} %collective-permute-done.19.refs_3_, ...), custom_call_target="tpu_custom_call" | custom-call | tf_op jit(solution)/shard_map/pallas_call | solution.py:506
  (55 shorter events, 2.7 us)
Async XLA Ops:
  3.1 5.6 %collective-permute-start.2 = (f32[136,128]{1,0:T(8,128)S(1)}, f32[136,128]{1,0:T(8,128)S(1)}, u32[]{:S(2)}, u32[]{:S(2)}) collective-permute-start(f32[136,128]{1,0:T(8,128)S(1)} %get-tuple-element.24), channel_id=1, source_target_pairs={{0,12},{4,0},{8,4},{12,8},{1,13},{5,1},{9,5},{13,9},{2,14},{6,2},{... | collective-permute-start | bytes 208904 | tf_op jit(solution)/shard_map/ppermute | solution.py:523
  7.3 7.2 %collective-permute-start.1 = (f32[136,128]{1,0:T(8,128)S(1)}, f32[136,128]{1,0:T(8,128)S(1)}, u32[]{:S(2)}, u32[]{:S(2)}) collective-permute-start(f32[136,128]{1,0:T(8,128)S(1)} %get-tuple-element.24), channel_id=1, source_target_pairs={{0,8},{4,12},{8,0},{12,4},{1,9},{5,13},{9,1},{13,5},{2,10},{6,14},... | collective-permute-start | bytes 208904 | tf_op jit(solution)/shard_map/ppermute | solution.py:523
  7.3 7.2 %collective-permute-start = (f32[136,128]{1,0:T(8,128)S(1)}, f32[136,128]{1,0:T(8,128)S(1)}, u32[]{:S(2)}, u32[]{:S(2)}) collective-permute-start(f32[136,128]{1,0:T(8,128)S(1)} %get-tuple-element.24), channel_id=1, source_target_pairs={{0,4},{4,8},{8,12},{12,0},{1,5},{5,9},{9,13},{13,1},{2,6},{6,10},{... | collective-permute-start | bytes 208904 | tf_op jit(solution)/shard_map/ppermute | solution.py:523
  14.6 7.9 %collective-permute-start.4 = (f32[4,136,128]{2,1,0:T(8,128)S(1)}, f32[4,136,128]{2,1,0:T(8,128)S(1)}, u32[]{:S(2)}, u32[]{:S(2)}) collective-permute-start(f32[4,136,128]{2,1,0:T(8,128)S(1)} %pad_maximum_fusion.patch_ref), channel_id=1, source_target_pairs={{1,2},{2,1},{5,6},{6,5},{9,10},{10,9},{13,14},{14,13},{17,18},{18,... | collective-permute-start | bytes 835592 | tf_op jit(solution)/shard_map/ppermute | solution.py:534
  18.1 4.3 %collective-permute-start.3 = (f32[4,136,128]{2,1,0:T(8,128)S(1)}, f32[4,136,128]{2,1,0:T(8,128)S(1)}, u32[]{:S(2)}, u32[]{:S(2)}) collective-permute-start(f32[4,136,128]{2,1,0:T(8,128)S(1)} %pad_maximum_fusion.patch_ref), channel_id=1, source_target_pairs={{0,1},{1,0},{2,3},{3,2},{4,5},{5,4},{6,7},{7,6},{8,9},{9,8},{10,11... | collective-permute-start | bytes 835592 | tf_op jit(solution)/shard_map/ppermute | solution.py:534
  28.3 3.6 %collective-permute-start.7 = (f32[128,128]{1,0:T(8,128)S(1)}, f32[128,128]{1,0:T(8,128)S(1)}, u32[]{:S(2)}, u32[]{:S(2)}) collective-permute-start(f32[128,128]{1,0:T(8,128)S(1)} %get-tuple-element.30), channel_id=1, source_target_pairs={{0,12},{4,0},{8,4},{12,8},{1,13},{5,1},{9,5},{13,9},{2,14},{6,2},{... | collective-permute-start | bytes 196616 | tf_op jit(solution)/shard_map/ppermute | solution.py:523
  29.8 7.3 %collective-permute-start.6 = (f32[128,128]{1,0:T(8,128)S(1)}, f32[128,128]{1,0:T(8,128)S(1)}, u32[]{:S(2)}, u32[]{:S(2)}) collective-permute-start(f32[128,128]{1,0:T(8,128)S(1)} %get-tuple-element.30), channel_id=1, source_target_pairs={{0,8},{4,12},{8,0},{12,4},{1,9},{5,13},{9,1},{13,5},{2,10},{6,14},... | collective-permute-start | bytes 196616 | tf_op jit(solution)/shard_map/ppermute | solution.py:523
  29.8 7.3 %collective-permute-start.5 = (f32[128,128]{1,0:T(8,128)S(1)}, f32[128,128]{1,0:T(8,128)S(1)}, u32[]{:S(2)}, u32[]{:S(2)}) collective-permute-start(f32[128,128]{1,0:T(8,128)S(1)} %get-tuple-element.30), channel_id=1, source_target_pairs={{0,4},{4,8},{8,12},{12,0},{1,5},{5,9},{9,13},{13,1},{2,6},{6,10},{... | collective-permute-start | bytes 196616 | tf_op jit(solution)/shard_map/ppermute | solution.py:523
  37.1 7.7 %collective-permute-start.9 = (f32[4,128,128]{2,1,0:T(8,128)S(1)}, f32[4,128,128]{2,1,0:T(8,128)S(1)}, u32[]{:S(2)}, u32[]{:S(2)}) collective-permute-start(f32[4,128,128]{2,1,0:T(8,128)S(1)} %pad_maximum_fusion.1.patch_ref), channel_id=1, source_target_pairs={{1,2},{2,1},{5,6},{6,5},{9,10},{10,9},{13,14},{14,13},{17,18},{18,... | collective-permute-start | bytes 786440 | tf_op jit(solution)/shard_map/ppermute | solution.py:534
  40.6 4.2 %collective-permute-start.8 = (f32[4,128,128]{2,1,0:T(8,128)S(1)}, f32[4,128,128]{2,1,0:T(8,128)S(1)}, u32[]{:S(2)}, u32[]{:S(2)}) collective-permute-start(f32[4,128,128]{2,1,0:T(8,128)S(1)} %pad_maximum_fusion.1.patch_ref), channel_id=1, source_target_pairs={{0,1},{1,0},{2,3},{3,2},{4,5},{5,4},{6,7},{7,6},{8,9},{9,8},{10,11... | collective-permute-start | bytes 786440 | tf_op jit(solution)/shard_map/ppermute | solution.py:534
  49.5 3.4 %collective-permute-start.12 = (f32[128,128]{1,0:T(8,128)S(1)}, f32[128,128]{1,0:T(8,128)S(1)}, u32[]{:S(2)}, u32[]{:S(2)}) collective-permute-start(f32[128,128]{1,0:T(8,128)S(1)} %get-tuple-element.34), channel_id=1, source_target_pairs={{0,12},{4,0},{8,4},{12,8},{1,13},{5,1},{9,5},{13,9},{2,14},{6,2},{... | collective-permute-start | bytes 196616 | tf_op jit(solution)/shard_map/ppermute | solution.py:523
  50.9 7.0 %collective-permute-start.11 = (f32[128,128]{1,0:T(8,128)S(1)}, f32[128,128]{1,0:T(8,128)S(1)}, u32[]{:S(2)}, u32[]{:S(2)}) collective-permute-start(f32[128,128]{1,0:T(8,128)S(1)} %get-tuple-element.34), channel_id=1, source_target_pairs={{0,8},{4,12},{8,0},{12,4},{1,9},{5,13},{9,1},{13,5},{2,10},{6,14},... | collective-permute-start | bytes 196616 | tf_op jit(solution)/shard_map/ppermute | solution.py:523
  51.5 6.4 %collective-permute-start.10 = (f32[128,128]{1,0:T(8,128)S(1)}, f32[128,128]{1,0:T(8,128)S(1)}, u32[]{:S(2)}, u32[]{:S(2)}) collective-permute-start(f32[128,128]{1,0:T(8,128)S(1)} %get-tuple-element.34), channel_id=1, source_target_pairs={{0,4},{4,8},{8,12},{12,0},{1,5},{5,9},{9,13},{13,1},{2,6},{6,10},{... | collective-permute-start | bytes 196616 | tf_op jit(solution)/shard_map/ppermute | solution.py:523
  57.9 7.7 %collective-permute-start.14 = (f32[4,128,128]{2,1,0:T(8,128)S(1)}, f32[4,128,128]{2,1,0:T(8,128)S(1)}, u32[]{:S(2)}, u32[]{:S(2)}) collective-permute-start(f32[4,128,128]{2,1,0:T(8,128)S(1)} %pad_maximum_fusion.2.patch_ref), channel_id=1, source_target_pairs={{1,2},{2,1},{5,6},{6,5},{9,10},{10,9},{13,14},{14,13},{17,18},{18,... | collective-permute-start | bytes 786440 | tf_op jit(solution)/shard_map/ppermute | solution.py:534
  61.6 4.0 %collective-permute-start.13 = (f32[4,128,128]{2,1,0:T(8,128)S(1)}, f32[4,128,128]{2,1,0:T(8,128)S(1)}, u32[]{:S(2)}, u32[]{:S(2)}) collective-permute-start(f32[4,128,128]{2,1,0:T(8,128)S(1)} %pad_maximum_fusion.2.patch_ref), channel_id=1, source_target_pairs={{0,1},{1,0},{2,3},{3,2},{4,5},{5,4},{6,7},{7,6},{8,9},{9,8},{10,11... | collective-permute-start | bytes 786440 | tf_op jit(solution)/shard_map/ppermute | solution.py:534
  70.4 3.6 %collective-permute-start.17 = (f32[128,128]{1,0:T(8,128)S(1)}, f32[128,128]{1,0:T(8,128)S(1)}, u32[]{:S(2)}, u32[]{:S(2)}) collective-permute-start(f32[128,128]{1,0:T(8,128)S(1)} %get-tuple-element.38), channel_id=1, source_target_pairs={{0,12},{4,0},{8,4},{12,8},{1,13},{5,1},{9,5},{13,9},{2,14},{6,2},{... | collective-permute-start | bytes 196616 | tf_op jit(solution)/shard_map/ppermute | solution.py:523
  71.6 7.8 %collective-permute-start.16 = (f32[128,128]{1,0:T(8,128)S(1)}, f32[128,128]{1,0:T(8,128)S(1)}, u32[]{:S(2)}, u32[]{:S(2)}) collective-permute-start(f32[128,128]{1,0:T(8,128)S(1)} %get-tuple-element.38), channel_id=1, source_target_pairs={{0,8},{4,12},{8,0},{12,4},{1,9},{5,13},{9,1},{13,5},{2,10},{6,14},... | collective-permute-start | bytes 196616 | tf_op jit(solution)/shard_map/ppermute | solution.py:523
  71.9 7.5 %collective-permute-start.15 = (f32[128,128]{1,0:T(8,128)S(1)}, f32[128,128]{1,0:T(8,128)S(1)}, u32[]{:S(2)}, u32[]{:S(2)}) collective-permute-start(f32[128,128]{1,0:T(8,128)S(1)} %get-tuple-element.38), channel_id=1, source_target_pairs={{0,4},{4,8},{8,12},{12,0},{1,5},{5,9},{9,13},{13,1},{2,6},{6,10},{... | collective-permute-start | bytes 196616 | tf_op jit(solution)/shard_map/ppermute | solution.py:523
  79.4 7.7 %collective-permute-start.19 = (f32[4,128,128]{2,1,0:T(8,128)S(1)}, f32[4,128,128]{2,1,0:T(8,128)S(1)}, u32[]{:S(2)}, u32[]{:S(2)}) collective-permute-start(f32[4,128,128]{2,1,0:T(8,128)S(1)} %pad_maximum_fusion.3.patch_ref), channel_id=1, source_target_pairs={{1,2},{2,1},{5,6},{6,5},{9,10},{10,9},{13,14},{14,13},{17,18},{18,... | collective-permute-start | bytes 786440 | tf_op jit(solution)/shard_map/ppermute | solution.py:534
  82.8 4.3 %collective-permute-start.18 = (f32[4,128,128]{2,1,0:T(8,128)S(1)}, f32[4,128,128]{2,1,0:T(8,128)S(1)}, u32[]{:S(2)}, u32[]{:S(2)}) collective-permute-start(f32[4,128,128]{2,1,0:T(8,128)S(1)} %pad_maximum_fusion.3.patch_ref), channel_id=1, source_target_pairs={{0,1},{1,0},{2,3},{3,2},{4,5},{5,4},{6,7},{7,6},{8,9},{9,8},{10,11... | collective-permute-start | bytes 786440 | tf_op jit(solution)/shard_map/ppermute | solution.py:534

commit v4 on v3

--- a/solution.py
+++ b/solution.py
@@ -59,7 +59,7 @@
         put(12 + at, value)
 
 
-def depth_weights(bins, params, depth):
+def depth_weights(group, params, depth):
     serial = lax.broadcasted_iota(jnp.int32, (8, 128), 0).astype(F32)
 
     def one(at):
@@ -76,17 +76,13 @@
         )
         return jnp.concatenate([w, (t - row_of(params, base + 10)) * w], axis=1)
 
-    def pair(at, _):
-        value = jnp.concatenate([one(2 * at), one(2 * at + 1)], axis=0)
-        high, low = split(value)
-        group = at // 8
-        row = pl.multiple_of((at % 8) * 16, 16)
-        depth[group, pl.ds(row, 16), :] = high
-        depth[group, pl.ds(row + 128, 16), :] = high
-        depth[group, pl.ds(row + 256, 16), :] = low
-        return _
-
-    lax.fori_loop(0, bins // 2, pair, 0, unroll=4)
+    for pair in range(8):
+        at = 16 * group + 2 * pair
+        high, low = split(jnp.concatenate([one(at), one(at + 1)], axis=0))
+        row = 16 * pair
+        depth[group, row : row + 16, :] = high
+        depth[group, row + 128 : row + 144, :] = high
+        depth[group, row + 256 : row + 272, :] = low
 
 
 def y_patterns(params, base, sub):
@@ -139,12 +135,9 @@
 
 
 def clear_own(tabs, bins, sums):
-    def clear(at, _):
+    for at in range(bins):
         for i in range(4):
             sums[pl.ds(tabs[at] + i * ROWS_X, 16), :] = jnp.zeros((16, 128), F32)
-        return _
-
-    lax.fori_loop(0, bins, clear, 0, unroll=4)
 
 
 def gather_group(tabs, group, sums, lane):
@@ -388,8 +381,8 @@
                 deposit_rows(g8, velocity, affine, deform, mass, blends)
 
     if not last:
-        depth_weights(bins, params_out, depth_out)
         for g in range(groups):
+            depth_weights(g, params_out, depth_out)
             wide, wide_low = wides.at[g], wides_low.at[g]
             products, products_low = products_all.at[g], products_lows.at[g]
 
@@ -519,7 +512,7 @@
         return lax.all_gather(payload, "gx")
     pieces = [payload]
     for shift in range(1, count):
-        pairs = [(i, (i + shift) % count) for i in range(count)]
+        pairs = [(i, i ^ shift if count & (count - 1) == 0 else (i + shift) % count) for i in range(count)]
         pieces.append(lax.ppermute(payload, "gx", pairs))
     return jnp.stack(pieces)
 

time: 90.6 us -> 89 us (0.982)
  waiting for transfers between devices: 28.3 us -> 25.3 us
    ppermute x12, waiting for transfers between devices: 23.6 us -> 18.7 us  [column_of(): pieces.append(lax.ppermute(payload, 'gx', pairs))]
    ppermute x8, waiting for transfers between devices: 4.66 us -> 6.55 us  [neighbours_of(): lax.ppermute(column, 'gy', pairs)]
    ppermute x12, starting transfers between devices: 13.8 us -> 15.4 us  [column_of(): pieces.append(lax.ppermute(payload, 'gx', pairs))]
    ppermute x8, starting transfers between devices: 14.3 us -> 13 us  [neighbours_of(): lax.ppermute(column, 'gy', pairs)]
  transfers between devices with their start and end apart: 20 -> 20, of which waited for: 11 -> 12; matrix products, arithmetic and copies ran while one was open for 1% -> 1% of each run, Pallas kernels for 12% -> 12%
where the time goes in v4:
time: 89 us; the launch traced here: 88.9 us
  Pallas kernels  32.6 us (37%)
  starting transfers between devices  28.4 us (32%)
  waiting for transfers between devices  25.3 us (28%)
  local copies, waits for them, and re-layouts  1.31 us (1%)
  between operations  0.89 us (1%)
    pallas_call x5, Pallas kernels, run_kernel(): pl.pallas_call(functools.partial(kernel, first, listing, last), out_shape...  22.1 us
    ppermute x12, waiting for transfers between devices, column_of(): pieces.append(lax.ppermute(payload, 'gx', pairs))  18.7 us
    ppermute x12, starting transfers between devices, column_of(): pieces.append(lax.ppermute(payload, 'gx', pairs))  15.4 us
    ppermute x8, starting transfers between devices, neighbours_of(): lax.ppermute(column, 'gy', pairs)  13 us
    pallas_call x4, Pallas kernels, run_column(): pl.pallas_call(functools.partial(column_kernel, bins), out_shape=shape_of...  10.5 us
    ppermute x8, waiting for transfers between devices, neighbours_of(): lax.ppermute(column, 'gy', pairs)  6.55 us
  transfers between devices with their start and end apart: 20, of which 12 were waited for; matrix products, arithmetic and copies ran while one was open for 1% of the time, Pallas kernels for 12%

profile of v4, /device:TPU:1, one launch (start us, length us, event | category | flops | bytes accessed | tf_op | source)
XLA Modules:
  0.0 88.9 jit_solution(12701670787867254697)
XLA Ops:
  0.6 2.4 %shard_map.112 = (f32[136,128]{1,0:T(8,128)S(1)}, f32[16,32,128]{2,1,0:T(8,128)S(1)}, f32[512,128]{1,0:T(8,128)S(1)}, bf16[2,384,256]{2,1,0:T(8,128)(2,1)S(1)}) custom-call(f32[3,32,128]{2,1,0:T(8,128)} %bitcast.48, s32[32,128]{1,0:T(8,128)} %refs_1_.1, f32[3,32,128]{2,1,0:T(8,128)} %bitcast.49, f32[9,32,128]{2,1,0:T(8,128)} %bitcast.34, ...), custom_call_target="tpu_custom_call" | custom-call | tf_op jit(solution)/shard_map/pallas_call | solution.py:499
  3.0 4.2 %collective-permute-start.2 = (f32[136,128]{1,0:T(8,128)S(1)}, f32[136,128]{1,0:T(8,128)S(1)}, u32[]{:S(2)}, u32[]{:S(2)}) collective-permute-start(f32[136,128]{1,0:T(8,128)S(1)} %get-tuple-element.24), channel_id=1, source_target_pairs={{0,12},{4,8},{8,4},{12,0},{1,13},{5,9},{9,5},{13,1},{2,14},{6,10},... | collective-permute-start | bytes 208904 | tf_op jit(solution)/shard_map/ppermute | solution.py:516
  7.3 0.4 collective-permute-start
  7.7 1.3 %collective-permute-done.2 = f32[136,128]{1,0:T(8,128)S(1)} collective-permute-done((f32[136,128]{1,0:T(8,128)S(1)}, f32[136,128]{1,0:T(8,128)S(1)}, u32[]{:S(2)}, u32[]{:S(2)}) %collective-permute-start.2) | collective-permute-done | bytes 69664 | tf_op jit(solution)/shard_map/ppermute | solution.py:516
  9.0 4.1 %collective-permute-done.1 = f32[136,128]{1,0:T(8,128)S(1)} collective-permute-done((f32[136,128]{1,0:T(8,128)S(1)}, f32[136,128]{1,0:T(8,128)S(1)}, u32[]{:S(2)}, u32[]{:S(2)}) %collective-permute-start.1) | collective-permute-done | bytes 69664 | tf_op jit(solution)/shard_map/ppermute | solution.py:516
  13.2 4.0 %collective-permute-start.4 = (f32[4,136,128]{2,1,0:T(8,128)S(1)}, f32[4,136,128]{2,1,0:T(8,128)S(1)}, u32[]{:S(2)}, u32[]{:S(2)}) collective-permute-start(f32[4,136,128]{2,1,0:T(8,128)S(1)} %pad_maximum_fusion.patch_ref), channel_id=1, source_target_pairs={{1,2},{2,1},{5,6},{6,5},{9,10},{10,9},{13,14},{14,13},{17,18},{18,... | collective-permute-start | bytes 835592 | tf_op jit(solution)/shard_map/ppermute | solution.py:527
  18.5 2.6 %shard_map.113.refs_3_ = f32[2,64,128]{2,1,0:T(8,128)S(1)} custom-call(s32[320]{0:T(512)S(1)} %pad_add_fusion.tabs, f32[4,136,128]{2,1,0:T(8,128)S(1)} %pad_maximum_fusion.patch_ref), custom_call_target="tpu_custom_call" | custom-call | flops 696320 | bytes 11141120 | tf_op jit(solution)/shard_map/pallas_call | solution.py:447
  21.9 5.7 %shard_map.114 = (f32[128,128]{1,0:T(8,128)S(1)}, f32[16,32,128]{2,1,0:T(8,128)S(1)}, f32[512,128]{1,0:T(8,128)S(1)}, bf16[2,384,256]{2,1,0:T(8,128)(2,1)S(1)}, s32[264]{0:T(512)S(1)}) custom-call(s32[576]{0:T(1024)S(1)} %concatenate.6.refs_0_, f32[4,136,128]{2,1,0:T(8,128)S(1)} %collective-permute-done.3.refs_1_, ...), custom_call_target="tpu_custom_call" | custom-call | tf_op jit(solution)/shard_map/pallas_call | solution.py:499
  27.6 2.5 %collective-permute-start.7 = (f32[128,128]{1,0:T(8,128)S(1)}, f32[128,128]{1,0:T(8,128)S(1)}, u32[]{:S(2)}, u32[]{:S(2)}) collective-permute-start(f32[128,128]{1,0:T(8,128)S(1)} %get-tuple-element.30), channel_id=1, source_target_pairs={{0,12},{4,8},{8,4},{12,0},{1,13},{5,9},{9,5},{13,1},{2,14},{6,10},... | collective-permute-start | bytes 196616 | tf_op jit(solution)/shard_map/ppermute | solution.py:516
  30.1 1.1 %collective-permute-start.5 = (f32[128,128]{1,0:T(8,128)S(1)}, f32[128,128]{1,0:T(8,128)S(1)}, u32[]{:S(2)}, u32[]{:S(2)}) collective-permute-start(f32[128,128]{1,0:T(8,128)S(1)} %get-tuple-element.30), channel_id=1, source_target_pairs={{0,4},{4,0},{8,12},{12,8},{1,5},{5,1},{9,13},{13,9},{2,6},{6,2},{1... | collective-permute-start | bytes 196616 | tf_op jit(solution)/shard_map/ppermute | solution.py:516
  31.2 1.7 %collective-permute-done.7 = f32[128,128]{1,0:T(8,128)S(1)} collective-permute-done((f32[128,128]{1,0:T(8,128)S(1)}, f32[128,128]{1,0:T(8,128)S(1)}, u32[]{:S(2)}, u32[]{:S(2)}) %collective-permute-start.7) | collective-permute-done | bytes 65568 | tf_op jit(solution)/shard_map/ppermute | solution.py:516
  33.0 3.5 %collective-permute-done.6 = f32[128,128]{1,0:T(8,128)S(1)} collective-permute-done((f32[128,128]{1,0:T(8,128)S(1)}, f32[128,128]{1,0:T(8,128)S(1)}, u32[]{:S(2)}, u32[]{:S(2)}) %collective-permute-start.6) | collective-permute-done | bytes 65568 | tf_op jit(solution)/shard_map/ppermute | solution.py:516
  36.5 2.7 %collective-permute-start.9 = (f32[4,128,128]{2,1,0:T(8,128)S(1)}, f32[4,128,128]{2,1,0:T(8,128)S(1)}, u32[]{:S(2)}, u32[]{:S(2)}) collective-permute-start(f32[4,128,128]{2,1,0:T(8,128)S(1)} %pad_maximum_fusion.1.patch_ref), channel_id=1, source_target_pairs={{1,2},{2,1},{5,6},{6,5},{9,10},{10,9},{13,14},{14,13},{17,18},{18,... | collective-permute-start | bytes 786440 | tf_op jit(solution)/shard_map/ppermute | solution.py:527
  39.3 2.6 %shard_map.115.refs_4_ = f32[2,64,128]{2,1,0:T(8,128)S(1)} custom-call(s32[320]{0:T(512)S(1)} %pad_add_fusion.tabs, f32[4,128,128]{2,1,0:T(8,128)S(1)} %pad_maximum_fusion.1.patch_ref), custom_call_target="tpu_custom_call" | custom-call | flops 655360 | bytes 10485760 | tf_op jit(solution)/shard_map/pallas_call | solution.py:447
  41.9 2.3 %collective-permute-done.9.refs_3_ = f32[4,128,128]{2,1,0:T(8,128)S(1)} collective-permute-done((f32[4,128,128]{2,1,0:T(8,128)S(1)}, f32[4,128,128]{2,1,0:T(8,128)S(1)}, u32[]{:S(2)}, u32[]{:S(2)}) %collective-permute-start.9) | collective-permute-done | bytes 262176 | tf_op jit(solution)/shard_map/ppermute | solution.py:527
  44.2 4.8 %shard_map.116 = (f32[128,128]{1,0:T(8,128)S(1)}, f32[16,32,128]{2,1,0:T(8,128)S(1)}, f32[512,128]{1,0:T(8,128)S(1)}, bf16[2,384,256]{2,1,0:T(8,128)(2,1)S(1)}) custom-call(s32[576]{0:T(1024)S(1)} %concatenate.6.refs_0_, s32[264]{0:T(512)S(1)} %get-tuple-element.29.refs_1_, f32[4,128,128]{2,1,0:T(8,128)S(1)} %collective-permute-done.8.refs_2_, ...), custom_call_target="tpu_custom_call" | custom-call | tf_op jit(solution)/shard_map/pallas_call | solution.py:499
  49.0 2.2 %collective-permute-start.12 = (f32[128,128]{1,0:T(8,128)S(1)}, f32[128,128]{1,0:T(8,128)S(1)}, u32[]{:S(2)}, u32[]{:S(2)}) collective-permute-start(f32[128,128]{1,0:T(8,128)S(1)} %get-tuple-element.34), channel_id=1, source_target_pairs={{0,12},{4,8},{8,4},{12,0},{1,13},{5,9},{9,5},{13,1},{2,14},{6,10},... | collective-permute-start | bytes 196616 | tf_op jit(solution)/shard_map/ppermute | solution.py:516
  51.2 1.4 %collective-permute-start.10 = (f32[128,128]{1,0:T(8,128)S(1)}, f32[128,128]{1,0:T(8,128)S(1)}, u32[]{:S(2)}, u32[]{:S(2)}) collective-permute-start(f32[128,128]{1,0:T(8,128)S(1)} %get-tuple-element.34), channel_id=1, source_target_pairs={{0,4},{4,0},{8,12},{12,8},{1,5},{5,1},{9,13},{13,9},{2,6},{6,2},{1... | collective-permute-start | bytes 196616 | tf_op jit(solution)/shard_map/ppermute | solution.py:516
  52.6 1.7 %collective-permute-done.12 = f32[128,128]{1,0:T(8,128)S(1)} collective-permute-done((f32[128,128]{1,0:T(8,128)S(1)}, f32[128,128]{1,0:T(8,128)S(1)}, u32[]{:S(2)}, u32[]{:S(2)}) %collective-permute-start.12) | collective-permute-done | bytes 65568 | tf_op jit(solution)/shard_map/ppermute | solution.py:516
  54.3 2.2 %collective-permute-done.11 = f32[128,128]{1,0:T(8,128)S(1)} collective-permute-done((f32[128,128]{1,0:T(8,128)S(1)}, f32[128,128]{1,0:T(8,128)S(1)}, u32[]{:S(2)}, u32[]{:S(2)}) %collective-permute-start.11) | collective-permute-done | bytes 65568 | tf_op jit(solution)/shard_map/ppermute | solution.py:516
  56.5 3.0 %collective-permute-start.14 = (f32[4,128,128]{2,1,0:T(8,128)S(1)}, f32[4,128,128]{2,1,0:T(8,128)S(1)}, u32[]{:S(2)}, u32[]{:S(2)}) collective-permute-start(f32[4,128,128]{2,1,0:T(8,128)S(1)} %pad_maximum_fusion.2.patch_ref), channel_id=1, source_target_pairs={{1,2},{2,1},{5,6},{6,5},{9,10},{10,9},{13,14},{14,13},{17,18},{18,... | collective-permute-start | bytes 786440 | tf_op jit(solution)/shard_map/ppermute | solution.py:527
  59.7 2.6 %shard_map.117.refs_4_ = f32[2,64,128]{2,1,0:T(8,128)S(1)} custom-call(s32[320]{0:T(512)S(1)} %pad_add_fusion.tabs, f32[4,128,128]{2,1,0:T(8,128)S(1)} %pad_maximum_fusion.2.patch_ref), custom_call_target="tpu_custom_call" | custom-call | flops 655360 | bytes 10485760 | tf_op jit(solution)/shard_map/pallas_call | solution.py:447
  62.3 1.9 %collective-permute-done.14.refs_3_ = f32[4,128,128]{2,1,0:T(8,128)S(1)} collective-permute-done((f32[4,128,128]{2,1,0:T(8,128)S(1)}, f32[4,128,128]{2,1,0:T(8,128)S(1)}, u32[]{:S(2)}, u32[]{:S(2)}) %collective-permute-start.14) | collective-permute-done | bytes 262176 | tf_op jit(solution)/shard_map/ppermute | solution.py:527
  64.2 4.9 %shard_map.118 = (f32[128,128]{1,0:T(8,128)S(1)}, f32[16,32,128]{2,1,0:T(8,128)S(1)}, f32[512,128]{1,0:T(8,128)S(1)}, bf16[2,384,256]{2,1,0:T(8,128)(2,1)S(1)}) custom-call(s32[576]{0:T(1024)S(1)} %concatenate.6.refs_0_, s32[264]{0:T(512)S(1)} %get-tuple-element.29.refs_1_, f32[4,128,128]{2,1,0:T(8,128)S(1)} %collective-permute-done.13.refs_2_, ...), custom_call_target="tpu_custom_call" | custom-call | tf_op jit(solution)/shard_map/pallas_call | solution.py:499
  69.2 2.2 %collective-permute-start.17 = (f32[128,128]{1,0:T(8,128)S(1)}, f32[128,128]{1,0:T(8,128)S(1)}, u32[]{:S(2)}, u32[]{:S(2)}) collective-permute-start(f32[128,128]{1,0:T(8,128)S(1)} %get-tuple-element.38), channel_id=1, source_target_pairs={{0,12},{4,8},{8,4},{12,0},{1,13},{5,9},{9,5},{13,1},{2,14},{6,10},... | collective-permute-start | bytes 196616 | tf_op jit(solution)/shard_map/ppermute | solution.py:516
  71.3 1.4 %collective-permute-start.15 = (f32[128,128]{1,0:T(8,128)S(1)}, f32[128,128]{1,0:T(8,128)S(1)}, u32[]{:S(2)}, u32[]{:S(2)}) collective-permute-start(f32[128,128]{1,0:T(8,128)S(1)} %get-tuple-element.38), channel_id=1, source_target_pairs={{0,4},{4,0},{8,12},{12,8},{1,5},{5,1},{9,13},{13,9},{2,6},{6,2},{1... | collective-permute-start | bytes 196616 | tf_op jit(solution)/shard_map/ppermute | solution.py:516
  72.8 1.9 %collective-permute-done.17 = f32[128,128]{1,0:T(8,128)S(1)} collective-permute-done((f32[128,128]{1,0:T(8,128)S(1)}, f32[128,128]{1,0:T(8,128)S(1)}, u32[]{:S(2)}, u32[]{:S(2)}) %collective-permute-start.17) | collective-permute-done | bytes 65568 | tf_op jit(solution)/shard_map/ppermute | solution.py:516
  74.7 2.2 %collective-permute-done.16 = f32[128,128]{1,0:T(8,128)S(1)} collective-permute-done((f32[128,128]{1,0:T(8,128)S(1)}, f32[128,128]{1,0:T(8,128)S(1)}, u32[]{:S(2)}, u32[]{:S(2)}) %collective-permute-start.16) | collective-permute-done | bytes 65568 | tf_op jit(solution)/shard_map/ppermute | solution.py:516
  76.9 3.0 %collective-permute-start.19 = (f32[4,128,128]{2,1,0:T(8,128)S(1)}, f32[4,128,128]{2,1,0:T(8,128)S(1)}, u32[]{:S(2)}, u32[]{:S(2)}) collective-permute-start(f32[4,128,128]{2,1,0:T(8,128)S(1)} %pad_maximum_fusion.3.patch_ref), channel_id=1, source_target_pairs={{1,2},{2,1},{5,6},{6,5},{9,10},{10,9},{13,14},{14,13},{17,18},{18,... | collective-permute-start | bytes 786440 | tf_op jit(solution)/shard_map/ppermute | solution.py:527
  80.0 2.6 %shard_map.119.refs_4_ = f32[2,64,128]{2,1,0:T(8,128)S(1)} custom-call(s32[320]{0:T(512)S(1)} %pad_add_fusion.tabs, f32[4,128,128]{2,1,0:T(8,128)S(1)} %pad_maximum_fusion.3.patch_ref), custom_call_target="tpu_custom_call" | custom-call | flops 655360 | bytes 10485760 | tf_op jit(solution)/shard_map/pallas_call | solution.py:447
  82.6 2.0 %collective-permute-done.19.refs_3_ = f32[4,128,128]{2,1,0:T(8,128)S(1)} collective-permute-done((f32[4,128,128]{2,1,0:T(8,128)S(1)}, f32[4,128,128]{2,1,0:T(8,128)S(1)}, u32[]{:S(2)}, u32[]{:S(2)}) %collective-permute-start.19) | collective-permute-done | bytes 262176 | tf_op jit(solution)/shard_map/ppermute | solution.py:527
  84.6 4.3 %shard_map.120 = (f32[3,32,128]{2,1,0:T(8,128)}, f32[9,32,128]{2,1,0:T(8,128)}, f32[9,32,128]{2,1,0:T(8,128)}) custom-call(s32[576]{0:T(1024)S(1)} %concatenate.6.refs_0_, s32[264]{0:T(512)S(1)} %get-tuple-element.29.refs_1_, f32[4,128,128]{2,1,0:T(8,128)S(1)} %collective-permute-done.18.refs_2_, f32[4,128,128]{2,1,0:T(8,128)S(1)} %collective-permute-done.19.refs_3_, ...), custom_call_target="tpu_custom_call" | custom-call | tf_op jit(solution)/shard_map/pallas_call | solution.py:499
  (55 shorter events, 2.4 us)
Async XLA Ops:
  3.0 6.0 %collective-permute-start.2 = (f32[136,128]{1,0:T(8,128)S(1)}, f32[136,128]{1,0:T(8,128)S(1)}, u32[]{:S(2)}, u32[]{:S(2)}) collective-permute-start(f32[136,128]{1,0:T(8,128)S(1)} %get-tuple-element.24), channel_id=1, source_target_pairs={{0,12},{4,8},{8,4},{12,0},{1,13},{5,9},{9,5},{13,1},{2,14},{6,10},... | collective-permute-start | bytes 208904 | tf_op jit(solution)/shard_map/ppermute | solution.py:516
  7.3 5.9 %collective-permute-start.1 = (f32[136,128]{1,0:T(8,128)S(1)}, f32[136,128]{1,0:T(8,128)S(1)}, u32[]{:S(2)}, u32[]{:S(2)}) collective-permute-start(f32[136,128]{1,0:T(8,128)S(1)} %get-tuple-element.24), channel_id=1, source_target_pairs={{0,8},{4,12},{8,0},{12,4},{1,9},{5,13},{9,1},{13,5},{2,10},{6,14},... | collective-permute-start | bytes 208904 | tf_op jit(solution)/shard_map/ppermute | solution.py:516
  7.3 5.9 %collective-permute-start = (f32[136,128]{1,0:T(8,128)S(1)}, f32[136,128]{1,0:T(8,128)S(1)}, u32[]{:S(2)}, u32[]{:S(2)}) collective-permute-start(f32[136,128]{1,0:T(8,128)S(1)} %get-tuple-element.24), channel_id=1, source_target_pairs={{0,4},{4,0},{8,12},{12,8},{1,5},{5,1},{9,13},{13,9},{2,6},{6,2},{1... | collective-permute-start | bytes 208904 | tf_op jit(solution)/shard_map/ppermute | solution.py:516
  13.2 8.2 %collective-permute-start.4 = (f32[4,136,128]{2,1,0:T(8,128)S(1)}, f32[4,136,128]{2,1,0:T(8,128)S(1)}, u32[]{:S(2)}, u32[]{:S(2)}) collective-permute-start(f32[4,136,128]{2,1,0:T(8,128)S(1)} %pad_maximum_fusion.patch_ref), channel_id=1, source_target_pairs={{1,2},{2,1},{5,6},{6,5},{9,10},{10,9},{13,14},{14,13},{17,18},{18,... | collective-permute-start | bytes 835592 | tf_op jit(solution)/shard_map/ppermute | solution.py:527
  17.2 4.2 %collective-permute-start.3 = (f32[4,136,128]{2,1,0:T(8,128)S(1)}, f32[4,136,128]{2,1,0:T(8,128)S(1)}, u32[]{:S(2)}, u32[]{:S(2)}) collective-permute-start(f32[4,136,128]{2,1,0:T(8,128)S(1)} %pad_maximum_fusion.patch_ref), channel_id=1, source_target_pairs={{0,1},{1,0},{2,3},{3,2},{4,5},{5,4},{6,7},{7,6},{8,9},{9,8},{10,11... | collective-permute-start | bytes 835592 | tf_op jit(solution)/shard_map/ppermute | solution.py:527
  27.6 5.4 %collective-permute-start.7 = (f32[128,128]{1,0:T(8,128)S(1)}, f32[128,128]{1,0:T(8,128)S(1)}, u32[]{:S(2)}, u32[]{:S(2)}) collective-permute-start(f32[128,128]{1,0:T(8,128)S(1)} %get-tuple-element.30), channel_id=1, source_target_pairs={{0,12},{4,8},{8,4},{12,0},{1,13},{5,9},{9,5},{13,1},{2,14},{6,10},... | collective-permute-start | bytes 196616 | tf_op jit(solution)/shard_map/ppermute | solution.py:516
  30.1 6.3 %collective-permute-start.6 = (f32[128,128]{1,0:T(8,128)S(1)}, f32[128,128]{1,0:T(8,128)S(1)}, u32[]{:S(2)}, u32[]{:S(2)}) collective-permute-start(f32[128,128]{1,0:T(8,128)S(1)} %get-tuple-element.30), channel_id=1, source_target_pairs={{0,8},{4,12},{8,0},{12,4},{1,9},{5,13},{9,1},{13,5},{2,10},{6,14},... | collective-permute-start | bytes 196616 | tf_op jit(solution)/shard_map/ppermute | solution.py:516
  30.1 6.3 %collective-permute-start.5 = (f32[128,128]{1,0:T(8,128)S(1)}, f32[128,128]{1,0:T(8,128)S(1)}, u32[]{:S(2)}, u32[]{:S(2)}) collective-permute-start(f32[128,128]{1,0:T(8,128)S(1)} %get-tuple-element.30), channel_id=1, source_target_pairs={{0,4},{4,0},{8,12},{12,8},{1,5},{5,1},{9,13},{13,9},{2,6},{6,2},{1... | collective-permute-start | bytes 196616 | tf_op jit(solution)/shard_map/ppermute | solution.py:516
  36.5 7.7 %collective-permute-start.9 = (f32[4,128,128]{2,1,0:T(8,128)S(1)}, f32[4,128,128]{2,1,0:T(8,128)S(1)}, u32[]{:S(2)}, u32[]{:S(2)}) collective-permute-start(f32[4,128,128]{2,1,0:T(8,128)S(1)} %pad_maximum_fusion.1.patch_ref), channel_id=1, source_target_pairs={{1,2},{2,1},{5,6},{6,5},{9,10},{10,9},{13,14},{14,13},{17,18},{18,... | collective-permute-start | bytes 786440 | tf_op jit(solution)/shard_map/ppermute | solution.py:527
  39.2 5.0 %collective-permute-start.8 = (f32[4,128,128]{2,1,0:T(8,128)S(1)}, f32[4,128,128]{2,1,0:T(8,128)S(1)}, u32[]{:S(2)}, u32[]{:S(2)}) collective-permute-start(f32[4,128,128]{2,1,0:T(8,128)S(1)} %pad_maximum_fusion.1.patch_ref), channel_id=1, source_target_pairs={{0,1},{1,0},{2,3},{3,2},{4,5},{5,4},{6,7},{7,6},{8,9},{9,8},{10,11... | collective-permute-start | bytes 786440 | tf_op jit(solution)/shard_map/ppermute | solution.py:527
  49.0 5.4 %collective-permute-start.12 = (f32[128,128]{1,0:T(8,128)S(1)}, f32[128,128]{1,0:T(8,128)S(1)}, u32[]{:S(2)}, u32[]{:S(2)}) collective-permute-start(f32[128,128]{1,0:T(8,128)S(1)} %get-tuple-element.34), channel_id=1, source_target_pairs={{0,12},{4,8},{8,4},{12,0},{1,13},{5,9},{9,5},{13,1},{2,14},{6,10},... | collective-permute-start | bytes 196616 | tf_op jit(solution)/shard_map/ppermute | solution.py:516
  51.2 5.3 %collective-permute-start.11 = (f32[128,128]{1,0:T(8,128)S(1)}, f32[128,128]{1,0:T(8,128)S(1)}, u32[]{:S(2)}, u32[]{:S(2)}) collective-permute-start(f32[128,128]{1,0:T(8,128)S(1)} %get-tuple-element.34), channel_id=1, source_target_pairs={{0,8},{4,12},{8,0},{12,4},{1,9},{5,13},{9,1},{13,5},{2,10},{6,14},... | collective-permute-start | bytes 196616 | tf_op jit(solution)/shard_map/ppermute | solution.py:516
  51.2 5.3 %collective-permute-start.10 = (f32[128,128]{1,0:T(8,128)S(1)}, f32[128,128]{1,0:T(8,128)S(1)}, u32[]{:S(2)}, u32[]{:S(2)}) collective-permute-start(f32[128,128]{1,0:T(8,128)S(1)} %get-tuple-element.34), channel_id=1, source_target_pairs={{0,4},{4,0},{8,12},{12,8},{1,5},{5,1},{9,13},{13,9},{2,6},{6,2},{1... | collective-permute-start | bytes 196616 | tf_op jit(solution)/shard_map/ppermute | solution.py:516
  56.5 7.7 %collective-permute-start.14 = (f32[4,128,128]{2,1,0:T(8,128)S(1)}, f32[4,128,128]{2,1,0:T(8,128)S(1)}, u32[]{:S(2)}, u32[]{:S(2)}) collective-permute-start(f32[4,128,128]{2,1,0:T(8,128)S(1)} %pad_maximum_fusion.2.patch_ref), channel_id=1, source_target_pairs={{1,2},{2,1},{5,6},{6,5},{9,10},{10,9},{13,14},{14,13},{17,18},{18,... | collective-permute-start | bytes 786440 | tf_op jit(solution)/shard_map/ppermute | solution.py:527
  59.6 4.7 %collective-permute-start.13 = (f32[4,128,128]{2,1,0:T(8,128)S(1)}, f32[4,128,128]{2,1,0:T(8,128)S(1)}, u32[]{:S(2)}, u32[]{:S(2)}) collective-permute-start(f32[4,128,128]{2,1,0:T(8,128)S(1)} %pad_maximum_fusion.2.patch_ref), channel_id=1, source_target_pairs={{0,1},{1,0},{2,3},{3,2},{4,5},{5,4},{6,7},{7,6},{8,9},{9,8},{10,11... | collective-permute-start | bytes 786440 | tf_op jit(solution)/shard_map/ppermute | solution.py:527
  69.2 5.5 %collective-permute-start.17 = (f32[128,128]{1,0:T(8,128)S(1)}, f32[128,128]{1,0:T(8,128)S(1)}, u32[]{:S(2)}, u32[]{:S(2)}) collective-permute-start(f32[128,128]{1,0:T(8,128)S(1)} %get-tuple-element.38), channel_id=1, source_target_pairs={{0,12},{4,8},{8,4},{12,0},{1,13},{5,9},{9,5},{13,1},{2,14},{6,10},... | collective-permute-start | bytes 196616 | tf_op jit(solution)/shard_map/ppermute | solution.py:516
  71.3 5.6 %collective-permute-start.16 = (f32[128,128]{1,0:T(8,128)S(1)}, f32[128,128]{1,0:T(8,128)S(1)}, u32[]{:S(2)}, u32[]{:S(2)}) collective-permute-start(f32[128,128]{1,0:T(8,128)S(1)} %get-tuple-element.38), channel_id=1, source_target_pairs={{0,8},{4,12},{8,0},{12,4},{1,9},{5,13},{9,1},{13,5},{2,10},{6,14},... | collective-permute-start | bytes 196616 | tf_op jit(solution)/shard_map/ppermute | solution.py:516
  71.3 5.6 %collective-permute-start.15 = (f32[128,128]{1,0:T(8,128)S(1)}, f32[128,128]{1,0:T(8,128)S(1)}, u32[]{:S(2)}, u32[]{:S(2)}) collective-permute-start(f32[128,128]{1,0:T(8,128)S(1)} %get-tuple-element.38), channel_id=1, source_target_pairs={{0,4},{4,0},{8,12},{12,8},{1,5},{5,1},{9,13},{13,9},{2,6},{6,2},{1... | collective-permute-start | bytes 196616 | tf_op jit(solution)/shard_map/ppermute | solution.py:516
  76.9 7.7 %collective-permute-start.19 = (f32[4,128,128]{2,1,0:T(8,128)S(1)}, f32[4,128,128]{2,1,0:T(8,128)S(1)}, u32[]{:S(2)}, u32[]{:S(2)}) collective-permute-start(f32[4,128,128]{2,1,0:T(8,128)S(1)} %pad_maximum_fusion.3.patch_ref), channel_id=1, source_target_pairs={{1,2},{2,1},{5,6},{6,5},{9,10},{10,9},{13,14},{14,13},{17,18},{18,... | collective-permute-start | bytes 786440 | tf_op jit(solution)/shard_map/ppermute | solution.py:527
  79.9 4.7 %collective-permute-start.18 = (f32[4,128,128]{2,1,0:T(8,128)S(1)}, f32[4,128,128]{2,1,0:T(8,128)S(1)}, u32[]{:S(2)}, u32[]{:S(2)}) collective-permute-start(f32[4,128,128]{2,1,0:T(8,128)S(1)} %pad_maximum_fusion.3.patch_ref), channel_id=1, source_target_pairs={{0,1},{1,0},{2,3},{3,2},{4,5},{5,4},{6,7},{7,6},{8,9},{9,8},{10,11... | collective-permute-start | bytes 786440 | tf_op jit(solution)/shard_map/ppermute | solution.py:527

commit v5 on v4

--- a/solution.py
+++ b/solution.py
@@ -12,6 +12,7 @@
 SUBSTEPS = 4
 SPAN_Y = 26
 LOW_Y = 5
+AT_ONCE = 16
 ROWS_X = 4 * SPAN_Y
 
 time_step = 0.05
@@ -127,11 +128,14 @@
 
 
 def add_patch(sums, row, patch, shift, z, lane):
-    moved = pltpu.roll(patch, shift & 127, 1)
-    moved = jnp.where((lane >= z) & (lane < z + 8), moved, 0.0)
+    moved = pltpu.roll(patch, shift, 1)
+    at = lane - z
+    inside = (at >= 0) & (at < 8)
     for i in range(4):
-        place = pl.ds(row + i * ROWS_X, 16)
-        sums[place, :] = sums[place, :] + moved[16 * i : 16 * i + 16]
+        for half in range(2):
+            place = pl.ds(row + i * ROWS_X + 8 * half, 8)
+            first = 16 * i + 8 * half
+            sums[place, :] = sums[place, :] + jnp.where(inside, moved[first : first + 8], 0.0)
 
 
 def clear_own(tabs, bins, sums):
@@ -142,22 +146,67 @@
 
 def gather_group(tabs, group, sums, lane):
     total = tabs.shape[0] // 2
-    compact = jnp.zeros((64, 128), F32)
+    compact = [jnp.zeros((8, 128), F32)] * 8
     for slot in range(16):
         row = tabs[group * 16 + slot]
         z = tabs[total + group * 16 + slot]
         node = fill([sums[pl.ds(row + i * ROWS_X, 16), :] for i in range(4)])
         moved = pltpu.roll(node, (8 * slot + 128 - z) & 127, 1)
-        compact = jnp.where(lane // 8 == slot, moved, compact)
-    return compact
+        mine = lane // 8 == slot
+        compact = [jnp.where(mine, moved[8 * k : 8 * k + 8], compact[k]) for k in range(8)]
+    return fill(compact)
 
 
 def fill(blocks):
     return jnp.concatenate(blocks, axis=0)
 
 
+def list_bins(tabs, bins, listed, spare):
+    total = tabs.shape[0] // 2
+    stride = listed.shape[0] // 4
+
+    def one(at, place):
+        listed[place] = at
+        return place + (tabs[bins + at] >= 0).astype(jnp.int32)
+
+    many = lax.fori_loop(0, total - bins, one, jnp.int32(0), unroll=16)
+
+    def widen(at, _):
+        for step in range(AT_ONCE):
+            n = at * AT_ONCE + step
+            used = n < many
+            which = jnp.where(used, listed[n], 0)
+            z = tabs[total + bins + which]
+            listed[n] = jnp.where(used, tabs[bins + which], spare)
+            listed[stride + n] = z
+            listed[2 * stride + n] = (z + 128 - 8 * (which & 15)) & 127
+            listed[3 * stride + n] = which >> 4
+        return _
+
+    lax.fori_loop(0, (many + AT_ONCE - 1) // AT_ONCE, widen, 0)
+    listed[stride - 1] = many
+
+
+def scatter_listed(bins, listed, patch_ref, sums, lane):
+    stride = listed.shape[0] // 4
+    groups = bins // 16
+
+    def some(at, _):
+        found = []
+        for step in range(AT_ONCE):
+            n = at * AT_ONCE + step
+            row, z, shift, block = [listed[k * stride + n] for k in range(4)]
+            start = pl.multiple_of((block % groups) * 64, 64)
+            found.append((row, patch_ref[block // groups, pl.ds(start, 64), :], shift, z))
+        for row, patch, shift, z in found:
+            add_patch(sums, row, patch, shift, z, lane)
+        return _
+
+    lax.fori_loop(0, (listed[stride - 1] + AT_ONCE - 1) // AT_ONCE, some, 0)
+
+
 def column_kernel(bins, tabs, patch_ref, out, sums):
-    lane = lax.broadcasted_iota(jnp.int32, (64, 128), 1)
+    lane = lax.broadcasted_iota(jnp.int32, (8, 128), 1)
     total = tabs.shape[0] // 2
     groups = bins // 16
     clear_own(tabs, bins, sums)
@@ -168,7 +217,7 @@
         for slot in range(16):
             z = tabs[total + first + slot]
             patch = patch_ref[at // groups, pl.ds(start, 64), :]
-            add_patch(sums, tabs[first + slot], patch, z + (128 - 8 * slot), z, lane)
+            add_patch(sums, tabs[first + slot], patch, (z + (128 - 8 * slot)) & 127, z, lane)
         return _
 
     lax.fori_loop(0, patch_ref.shape[0] * groups, block, 0)
@@ -176,41 +225,8 @@
         out[g] = gather_group(tabs, g, sums, lane)
 
 
-def list_bins(tabs, bins, count, listed):
-    for side in range(2):
-
-        def one(at, place, side=side):
-            listed[side * count + place] = at
-            return place + (tabs[bins + side * count + at] >= 0).astype(jnp.int32)
-
-        listed[2 * count + side] = lax.fori_loop(0, count, one, jnp.int32(0), unroll=8)
-
-
-def scatter_listed(tabs, bins, listed, sides, sums, spare, lane):
-    total = tabs.shape[0] // 2
-    count = sides[0].shape[0] * bins
-    many = [listed[2 * count + side] for side in range(2)]
-
-    def some(at, _):
-        found = []
-        for step in range(8):
-            n = at * 8 + step
-            for side, patch_ref in enumerate(sides):
-                used = n < many[side]
-                which = listed[side * count + jnp.where(used, n, 0)]
-                which = jnp.where(used, which, 0)
-                place = bins + side * count + which
-                row = jnp.where(used, tabs[place], spare)
-                z = tabs[total + place]
-                inner = which % bins
-                start = pl.multiple_of((inner // 16) * 64, 64)
-                patch = patch_ref[which // bins, pl.ds(start, 64), :]
-                found.append((row, patch, z + 128 - 8 * (inner % 16), z))
-        for row, patch, shift, z in found:
-            add_patch(sums, row, patch, shift, z, lane)
-        return _
-
-    lax.fori_loop(0, (jnp.maximum(many[0], many[1]) + 7) // 8, some, 0)
+def spare_row(sums):
+    return sums.shape[0] - 3 * ROWS_X - 16
 
 
 def kernel(first, listing, last, *refs):
@@ -221,16 +237,17 @@
         bins = sources[5].shape[0]
     else:
         (tabs,) = take(1)
-        if not listing:
-            (listed,) = take(1)
-        patch_a, patch_b, compact_in, inside_ref, state_in, params, depth = take(7)
+        lists = take(1 if listing else 2)
+        sides = take(2)
+        compact_in, inside_ref, state_in, params, depth = take(5)
         bins = state_in.shape[1]
     if last:
         velocity_out, affine_out, deform_out = take(3)
     else:
         patch_out, state_out, params_out, depth_out = take(4)
     if listing:
-        (listed,) = take(1)
+        side_tabs = [tabs] + lists
+        lists = take(2)
     wides, products_all = take(2)
     if first:
         held = take(9)
@@ -256,7 +273,7 @@
         wides_low, blends, products_lows = take(3)
     groups = bins // 16
     sub = lax.broadcasted_iota(jnp.int32, (8, 128), 0)
-    lane = lax.broadcasted_iota(jnp.int32, (64, 128), 1)
+    lane = lax.broadcasted_iota(jnp.int32, (8, 128), 1)
     lane_row = lax.broadcasted_iota(jnp.int32, (1, 128), 1)
 
     def load8(g8):
@@ -297,10 +314,11 @@
             deposit_rows(g8, velocity, affine, deform, mass, blends)
     else:
         if listing:
-            list_bins(tabs, bins, patch_a.shape[0] * bins, listed)
+            for own_tabs, listed in zip(side_tabs, lists):
+                list_bins(own_tabs, bins, listed, spare_row(sums))
         clear_own(tabs, bins, sums)
-        spare = sums.shape[0] - 3 * ROWS_X - 16
-        scatter_listed(tabs, bins, listed, [patch_a, patch_b], sums, spare, lane)
+        for listed, side_ref in zip(lists, sides):
+            scatter_listed(bins, listed, side_ref, sums, lane)
         for g in range(groups):
             compact = compact_in[g] + gather_group(tabs, g, sums, lane)
             wide, products = wides.at[g], products_all.at[g]
@@ -418,12 +436,14 @@
             products_low[...] = lax.dot_general(
                 wide_low[...], depth_out[g, 128:256, :], turned, preferred_element_type=F32
             )
-            compact = jnp.zeros((64, 128), F32)
+            compact = [jnp.zeros((8, 128), F32)] * 8
             for slot in range(16):
-                at = slice(64 * slot, 64 * slot + 64)
-                value = products[at, 0:128] + products[at, 128:256] + products_low[at, :]
-                compact = jnp.where(lane // 8 == slot, value, compact)
-            patch_out[64 * g : 64 * g + 64, :] = compact
+                mine = lane // 8 == slot
+                for k in range(8):
+                    at = slice(64 * slot + 8 * k, 64 * slot + 8 * k + 8)
+                    value = products[at, 0:128] + products[at, 128:256] + products_low[at, :]
+                    compact[k] = jnp.where(mine, value, compact[k])
+            patch_out[64 * g : 64 * g + 64, :] = fill(compact)
 
 
 VMEM_SPEC = pl.BlockSpec(memory_space=pltpu.VMEM)
@@ -441,6 +461,11 @@
 def limit_for(operands, total_x):
     held = sum(4 * op.size for op in operands) + 512 * grid_rows(total_x)
     return held + (16 << 20)
+
+
+def list_shape(bins_near):
+    stride = bins_near + AT_ONCE + 8
+    return shape_of(4 * stride, dtype=jnp.int32)
 
 
 def run_column(total_x, bins, tabs, column):
@@ -478,12 +503,11 @@
         scratch += [pltpu.VMEM(op.shape, op.dtype) for op in operands]
         scratch += [pltpu.SemaphoreType.DMA((len(operands),))]
     else:
-        in_specs[0] = SMEM_SPEC
+        scalars = 2 if listing else 3
+        in_specs[:scalars] = [SMEM_SPEC] * scalars
         if listing:
-            outs.append(shape_of(2 * operands[1].shape[0] * bins + 8, dtype=jnp.int32))
-            out_specs.append(SMEM_SPEC)
-        else:
-            in_specs[1] = SMEM_SPEC
+            outs += [list_shape(operands[scalars].shape[0] * bins)] * 2
+            out_specs += [SMEM_SPEC] * 2
         scratch += [
             pltpu.VMEM((grid_rows(total_x), 128), F32),
             pltpu.VMEM((32 * bins, 128), F32),
@@ -517,15 +541,12 @@
     return jnp.stack(pieces)
 
 
-def neighbours_of(column):
+def neighbour_of(column, start):
     count = lax.axis_size("gy")
-    got = []
-    for start in range(2):
-        pairs = []
-        for low in range(start, count - 1, 2):
-            pairs += [(low, low + 1), (low + 1, low)]
-        got.append(lax.ppermute(column, "gy", pairs) if pairs else jnp.zeros_like(column))
-    return got
+    pairs = []
+    for low in range(start, count - 1, 2):
+        pairs += [(low, low + 1), (low + 1, low)]
+    return lax.ppermute(column, "gy", pairs) if pairs else jnp.zeros_like(column)
 
 
 def shards(
@@ -569,7 +590,7 @@
         return inside
 
     def places(block, move):
-        known = block[:, 4 * bins : 4 * bins + 4, 0:bins].astype(jnp.int32)
+        known = block[:, 0:4, 0:bins].astype(jnp.int32)
         y = known[:, 1] + LOW_Y + move
         row = known[:, 0] * ROWS_X + 4 * y
         good = (known[:, 3] > 0) & (y >= 0) & (y <= LOW_Y + TILE + 1)
@@ -578,7 +599,7 @@
     step_a = jnp.where(place_y % 2 == 0, TILE, -TILE)
     for substep in range(SUBSTEPS):
         column = column_of(payload)
-        beside = neighbours_of(column)
+        beside_a, beside_b = neighbour_of(column, 0), neighbour_of(column, 1)
         if substep == 0:
             own = payload[4 * bins : 4 * bins + 3, 0:bins].astype(jnp.int32)
             own_row = own[0] * ROWS_X + 4 * (own[1] + LOW_Y)
@@ -586,13 +607,18 @@
             late, _ = lax.optimization_barrier((payload[4 * bins : 4 * bins + 3], column))
             late = late[:, 0:bins].astype(jnp.int32)
             inside = inside_grid(late[0] - 2, late[1], late[2])
-            row, z = places(column, 0)
+            row, z = places(column[:, 4 * bins :], 0)
             column_tabs = jnp.concatenate([own_row, row, anchor_z, z])
-            row_a, z_a = places(beside[0], step_a)
-            row_b, z_b = places(beside[1], -step_a)
-            tabs = jnp.concatenate([own_row, row_a, row_b, anchor_z, z_a, z_b])
         compact = run_column(total_x, bins, column_tabs, column)
         listing = substep == 0
+        if listing:
+            facts_a, facts_b, _ = lax.optimization_barrier(
+                (beside_a[:, 4 * bins :], beside_b[:, 4 * bins :], compact)
+            )
+            row_a, z_a = places(facts_a, step_a)
+            row_b, z_b = places(facts_b, -step_a)
+            tabs_a = jnp.concatenate([own_row, row_a, anchor_z, z_a])
+            tabs_b = jnp.concatenate([own_row, row_b, anchor_z, z_b])
         last = substep == SUBSTEPS - 1
         results = run_kernel(
             False,
@@ -600,15 +626,13 @@
             last,
             total_x,
             bins,
-            [tabs]
-            + ([] if listing else [listed])
-            + beside
-            + [compact, inside, state, params, depth],
+            [tabs_a] + ([tabs_b] if listing else [list_a, list_b])
+            + [beside_a, beside_b, compact, inside, state, params, depth],
         )
         if not last:
             payload, state, params, depth = results[:4]
         if listing:
-            listed = results[4]
+            list_a, list_b = results[4:]
     return tuple(turn(array) for array in results)
 
 

time: 89 us -> 86.8 us (0.975)
  Pallas kernels: 32.6 us -> 30.2 us
    pallas_call x5, Pallas kernels: 22.1 us -> 19.8 us  [run_kernel(): pl.pallas_call(functools.partial(kernel, first, listing, last), out_shape...]
where the time goes in v5:
time: 86.8 us; the launch traced here: 86.5 us
  Pallas kernels  30.2 us (35%)
  starting transfers between devices  28.5 us (33%)
  waiting for transfers between devices  25.1 us (29%)
  local copies, waits for them, and re-layouts  1.23 us (1%)
  between operations  0.9 us (1%)
    pallas_call x5, Pallas kernels, run_kernel(): pl.pallas_call(functools.partial(kernel, first, listing, last), out_shape...  19.8 us
    ppermute x12, waiting for transfers between devices, column_of(): pieces.append(lax.ppermute(payload, 'gx', pairs))  18.6 us
    ppermute x12, starting transfers between devices, column_of(): pieces.append(lax.ppermute(payload, 'gx', pairs))  15.4 us
    ppermute x8, starting transfers between devices, neighbour_of(): lax.ppermute(column, 'gy', pairs)  13 us
    pallas_call x4, Pallas kernels, run_column(): pl.pallas_call(functools.partial(column_kernel, bins), out_shape=shape_of...  10.5 us
    ppermute x8, waiting for transfers between devices, neighbour_of(): lax.ppermute(column, 'gy', pairs)  6.48 us
  transfers between devices with their start and end apart: 20, of which 12 were waited for; matrix products, arithmetic and copies ran while one was open for 1% of the time, Pallas kernels for 12%

profile of v5, /device:TPU:1, one launch (start us, length us, event | category | flops | bytes accessed | tf_op | source)
XLA Modules:
  0.0 86.5 jit_solution(5595598202390483733)
XLA Ops:
  0.6 2.4 %shard_map.112 = (f32[136,128]{1,0:T(8,128)S(1)}, f32[16,32,128]{2,1,0:T(8,128)S(1)}, f32[512,128]{1,0:T(8,128)S(1)}, bf16[2,384,256]{2,1,0:T(8,128)(2,1)S(1)}) custom-call(f32[3,32,128]{2,1,0:T(8,128)} %bitcast.48, s32[32,128]{1,0:T(8,128)} %refs_1_.1, f32[3,32,128]{2,1,0:T(8,128)} %bitcast.49, f32[9,32,128]{2,1,0:T(8,128)} %bitcast.34, ...), custom_call_target="tpu_custom_call" | custom-call | tf_op jit(solution)/shard_map/pallas_call | solution.py:523
  3.0 4.2 %collective-permute-start.2 = (f32[136,128]{1,0:T(8,128)S(1)}, f32[136,128]{1,0:T(8,128)S(1)}, u32[]{:S(2)}, u32[]{:S(2)}) collective-permute-start(f32[136,128]{1,0:T(8,128)S(1)} %get-tuple-element.27), channel_id=1, source_target_pairs={{0,12},{4,8},{8,4},{12,0},{1,13},{5,9},{9,5},{13,1},{2,14},{6,10},... | collective-permute-start | bytes 208904 | tf_op jit(solution)/shard_map/ppermute | solution.py:540
  7.3 0.4 collective-permute-start
  7.7 1.3 %collective-permute-done.2 = f32[136,128]{1,0:T(8,128)S(1)} collective-permute-done((f32[136,128]{1,0:T(8,128)S(1)}, f32[136,128]{1,0:T(8,128)S(1)}, u32[]{:S(2)}, u32[]{:S(2)}) %collective-permute-start.2) | collective-permute-done | bytes 69664 | tf_op jit(solution)/shard_map/ppermute | solution.py:540
  9.0 4.1 %collective-permute-done.1 = f32[136,128]{1,0:T(8,128)S(1)} collective-permute-done((f32[136,128]{1,0:T(8,128)S(1)}, f32[136,128]{1,0:T(8,128)S(1)}, u32[]{:S(2)}, u32[]{:S(2)}) %collective-permute-start.1) | collective-permute-done | bytes 69664 | tf_op jit(solution)/shard_map/ppermute | solution.py:540
  13.2 4.0 %collective-permute-start.4 = (f32[4,136,128]{2,1,0:T(8,128)S(1)}, f32[4,136,128]{2,1,0:T(8,128)S(1)}, u32[]{:S(2)}, u32[]{:S(2)}) collective-permute-start(f32[4,136,128]{2,1,0:T(8,128)S(1)} %pad_maximum_fusion.patch_ref), channel_id=1, source_target_pairs={{1,2},{2,1},{5,6},{6,5},{9,10},{10,9},{13,14},{14,13},{17,18},{18,... | collective-permute-start | bytes 835592 | tf_op jit(solution)/shard_map/ppermute | solution.py:549
  18.3 2.6 %shard_map.113.refs_4_ = f32[2,64,128]{2,1,0:T(8,128)S(1)} custom-call(s32[320]{0:T(512)S(1)} %fusion.9.tabs, f32[4,136,128]{2,1,0:T(8,128)S(1)} %pad_maximum_fusion.patch_ref), custom_call_target="tpu_custom_call" | custom-call | flops 696320 | bytes 11141120 | tf_op jit(solution)/shard_map/pallas_call | solution.py:472
  21.9 5.5 %shard_map.114 = (f32[128,128]{1,0:T(8,128)S(1)}, f32[16,32,128]{2,1,0:T(8,128)S(1)}, f32[512,128]{1,0:T(8,128)S(1)}, bf16[2,384,256]{2,1,0:T(8,128)(2,1)S(1)}, s32[608]{0:T(1024)S(1)}, /*index=5*/s32[608]{0:T(1024)S(1)}) custom-call(s32[320]{0:T(512)S(1)} %get-tuple-element.63.refs_0_, s32[320]{0:T(512)S(1)} %get-tuple-element.62.refs_1_, ...), custom_call_target="tpu_custom_call" | custom-call | tf_op jit(solution)/shard_map/pallas_call | solution.py:523
  27.4 2.5 %collective-permute-start.7 = (f32[128,128]{1,0:T(8,128)S(1)}, f32[128,128]{1,0:T(8,128)S(1)}, u32[]{:S(2)}, u32[]{:S(2)}) collective-permute-start(f32[128,128]{1,0:T(8,128)S(1)} %get-tuple-element.36), channel_id=1, source_target_pairs={{0,12},{4,8},{8,4},{12,0},{1,13},{5,9},{9,5},{13,1},{2,14},{6,10},... | collective-permute-start | bytes 196616 | tf_op jit(solution)/shard_map/ppermute | solution.py:540
  29.9 1.1 %collective-permute-start.5 = (f32[128,128]{1,0:T(8,128)S(1)}, f32[128,128]{1,0:T(8,128)S(1)}, u32[]{:S(2)}, u32[]{:S(2)}) collective-permute-start(f32[128,128]{1,0:T(8,128)S(1)} %get-tuple-element.36), channel_id=1, source_target_pairs={{0,4},{4,0},{8,12},{12,8},{1,5},{5,1},{9,13},{13,9},{2,6},{6,2},{1... | collective-permute-start | bytes 196616 | tf_op jit(solution)/shard_map/ppermute | solution.py:540
  31.1 2.1 %collective-permute-done.7 = f32[128,128]{1,0:T(8,128)S(1)} collective-permute-done((f32[128,128]{1,0:T(8,128)S(1)}, f32[128,128]{1,0:T(8,128)S(1)}, u32[]{:S(2)}, u32[]{:S(2)}) %collective-permute-start.7) | collective-permute-done | bytes 65568 | tf_op jit(solution)/shard_map/ppermute | solution.py:540
  33.1 3.1 %collective-permute-done.6 = f32[128,128]{1,0:T(8,128)S(1)} collective-permute-done((f32[128,128]{1,0:T(8,128)S(1)}, f32[128,128]{1,0:T(8,128)S(1)}, u32[]{:S(2)}, u32[]{:S(2)}) %collective-permute-start.6) | collective-permute-done | bytes 65568 | tf_op jit(solution)/shard_map/ppermute | solution.py:540
  36.3 2.8 %collective-permute-start.9 = (f32[4,128,128]{2,1,0:T(8,128)S(1)}, f32[4,128,128]{2,1,0:T(8,128)S(1)}, u32[]{:S(2)}, u32[]{:S(2)}) collective-permute-start(f32[4,128,128]{2,1,0:T(8,128)S(1)} %pad_maximum_fusion.1.patch_ref), channel_id=1, source_target_pairs={{1,2},{2,1},{5,6},{6,5},{9,10},{10,9},{13,14},{14,13},{17,18},{18,... | collective-permute-start | bytes 786440 | tf_op jit(solution)/shard_map/ppermute | solution.py:549
  39.2 2.6 %shard_map.115.refs_5_ = f32[2,64,128]{2,1,0:T(8,128)S(1)} custom-call(s32[320]{0:T(512)S(1)} %fusion.9.tabs, f32[4,128,128]{2,1,0:T(8,128)S(1)} %pad_maximum_fusion.1.patch_ref), custom_call_target="tpu_custom_call" | custom-call | flops 655360 | bytes 10485760 | tf_op jit(solution)/shard_map/pallas_call | solution.py:472
  41.8 2.2 %collective-permute-done.9.refs_4_ = f32[4,128,128]{2,1,0:T(8,128)S(1)} collective-permute-done((f32[4,128,128]{2,1,0:T(8,128)S(1)}, f32[4,128,128]{2,1,0:T(8,128)S(1)}, u32[]{:S(2)}, u32[]{:S(2)}) %collective-permute-start.9) | collective-permute-done | bytes 262176 | tf_op jit(solution)/shard_map/ppermute | solution.py:549
  44.0 4.0 %shard_map.116 = (f32[128,128]{1,0:T(8,128)S(1)}, f32[16,32,128]{2,1,0:T(8,128)S(1)}, f32[512,128]{1,0:T(8,128)S(1)}, bf16[2,384,256]{2,1,0:T(8,128)(2,1)S(1)}) custom-call(s32[320]{0:T(512)S(1)} %get-tuple-element.63.refs_0_, s32[608]{0:T(1024)S(1)} %get-tuple-element.34.refs_1_, s32[608]{0:T(1024)S(1)} %get-tuple-element.35.refs_2_, ...), custom_call_target="tpu_custom_call" | custom-call | tf_op jit(solution)/shard_map/pallas_call | solution.py:523
  48.0 2.2 %collective-permute-start.12 = (f32[128,128]{1,0:T(8,128)S(1)}, f32[128,128]{1,0:T(8,128)S(1)}, u32[]{:S(2)}, u32[]{:S(2)}) collective-permute-start(f32[128,128]{1,0:T(8,128)S(1)} %get-tuple-element.40), channel_id=1, source_target_pairs={{0,12},{4,8},{8,4},{12,0},{1,13},{5,9},{9,5},{13,1},{2,14},{6,10},... | collective-permute-start | bytes 196616 | tf_op jit(solution)/shard_map/ppermute | solution.py:540
  50.2 1.4 %collective-permute-start.10 = (f32[128,128]{1,0:T(8,128)S(1)}, f32[128,128]{1,0:T(8,128)S(1)}, u32[]{:S(2)}, u32[]{:S(2)}) collective-permute-start(f32[128,128]{1,0:T(8,128)S(1)} %get-tuple-element.40), channel_id=1, source_target_pairs={{0,4},{4,0},{8,12},{12,8},{1,5},{5,1},{9,13},{13,9},{2,6},{6,2},{1... | collective-permute-start | bytes 196616 | tf_op jit(solution)/shard_map/ppermute | solution.py:540
  51.6 1.8 %collective-permute-done.12 = f32[128,128]{1,0:T(8,128)S(1)} collective-permute-done((f32[128,128]{1,0:T(8,128)S(1)}, f32[128,128]{1,0:T(8,128)S(1)}, u32[]{:S(2)}, u32[]{:S(2)}) %collective-permute-start.12) | collective-permute-done | bytes 65568 | tf_op jit(solution)/shard_map/ppermute | solution.py:540
  53.5 2.3 %collective-permute-done.11 = f32[128,128]{1,0:T(8,128)S(1)} collective-permute-done((f32[128,128]{1,0:T(8,128)S(1)}, f32[128,128]{1,0:T(8,128)S(1)}, u32[]{:S(2)}, u32[]{:S(2)}) %collective-permute-start.11) | collective-permute-done | bytes 65568 | tf_op jit(solution)/shard_map/ppermute | solution.py:540
  55.8 3.0 %collective-permute-start.14 = (f32[4,128,128]{2,1,0:T(8,128)S(1)}, f32[4,128,128]{2,1,0:T(8,128)S(1)}, u32[]{:S(2)}, u32[]{:S(2)}) collective-permute-start(f32[4,128,128]{2,1,0:T(8,128)S(1)} %pad_maximum_fusion.2.patch_ref), channel_id=1, source_target_pairs={{1,2},{2,1},{5,6},{6,5},{9,10},{10,9},{13,14},{14,13},{17,18},{18,... | collective-permute-start | bytes 786440 | tf_op jit(solution)/shard_map/ppermute | solution.py:549
  58.9 2.6 %shard_map.117.refs_5_ = f32[2,64,128]{2,1,0:T(8,128)S(1)} custom-call(s32[320]{0:T(512)S(1)} %fusion.9.tabs, f32[4,128,128]{2,1,0:T(8,128)S(1)} %pad_maximum_fusion.2.patch_ref), custom_call_target="tpu_custom_call" | custom-call | flops 655360 | bytes 10485760 | tf_op jit(solution)/shard_map/pallas_call | solution.py:472
  61.5 2.0 %collective-permute-done.14.refs_4_ = f32[4,128,128]{2,1,0:T(8,128)S(1)} collective-permute-done((f32[4,128,128]{2,1,0:T(8,128)S(1)}, f32[4,128,128]{2,1,0:T(8,128)S(1)}, u32[]{:S(2)}, u32[]{:S(2)}) %collective-permute-start.14) | collective-permute-done | bytes 262176 | tf_op jit(solution)/shard_map/ppermute | solution.py:549
  63.5 4.2 %shard_map.118 = (f32[128,128]{1,0:T(8,128)S(1)}, f32[16,32,128]{2,1,0:T(8,128)S(1)}, f32[512,128]{1,0:T(8,128)S(1)}, bf16[2,384,256]{2,1,0:T(8,128)(2,1)S(1)}) custom-call(s32[320]{0:T(512)S(1)} %get-tuple-element.63.refs_0_, s32[608]{0:T(1024)S(1)} %get-tuple-element.34.refs_1_, s32[608]{0:T(1024)S(1)} %get-tuple-element.35.refs_2_, ...), custom_call_target="tpu_custom_call" | custom-call | tf_op jit(solution)/shard_map/pallas_call | solution.py:523
  67.7 1.8 %collective-permute-start.17 = (f32[128,128]{1,0:T(8,128)S(1)}, f32[128,128]{1,0:T(8,128)S(1)}, u32[]{:S(2)}, u32[]{:S(2)}) collective-permute-start(f32[128,128]{1,0:T(8,128)S(1)} %get-tuple-element.44), channel_id=1, source_target_pairs={{0,12},{4,8},{8,4},{12,0},{1,13},{5,9},{9,5},{13,1},{2,14},{6,10},... | collective-permute-start | bytes 196616 | tf_op jit(solution)/shard_map/ppermute | solution.py:540
  69.5 1.8 %collective-permute-start.15 = (f32[128,128]{1,0:T(8,128)S(1)}, f32[128,128]{1,0:T(8,128)S(1)}, u32[]{:S(2)}, u32[]{:S(2)}) collective-permute-start(f32[128,128]{1,0:T(8,128)S(1)} %get-tuple-element.44), channel_id=1, source_target_pairs={{0,4},{4,0},{8,12},{12,8},{1,5},{5,1},{9,13},{13,9},{2,6},{6,2},{1... | collective-permute-start | bytes 196616 | tf_op jit(solution)/shard_map/ppermute | solution.py:540
  71.3 1.7 %collective-permute-done.17 = f32[128,128]{1,0:T(8,128)S(1)} collective-permute-done((f32[128,128]{1,0:T(8,128)S(1)}, f32[128,128]{1,0:T(8,128)S(1)}, u32[]{:S(2)}, u32[]{:S(2)}) %collective-permute-start.17) | collective-permute-done | bytes 65568 | tf_op jit(solution)/shard_map/ppermute | solution.py:540
  73.0 2.1 %collective-permute-done.16 = f32[128,128]{1,0:T(8,128)S(1)} collective-permute-done((f32[128,128]{1,0:T(8,128)S(1)}, f32[128,128]{1,0:T(8,128)S(1)}, u32[]{:S(2)}, u32[]{:S(2)}) %collective-permute-start.16) | collective-permute-done | bytes 65568 | tf_op jit(solution)/shard_map/ppermute | solution.py:540
  75.2 3.0 %collective-permute-start.19 = (f32[4,128,128]{2,1,0:T(8,128)S(1)}, f32[4,128,128]{2,1,0:T(8,128)S(1)}, u32[]{:S(2)}, u32[]{:S(2)}) collective-permute-start(f32[4,128,128]{2,1,0:T(8,128)S(1)} %pad_maximum_fusion.3.patch_ref), channel_id=1, source_target_pairs={{1,2},{2,1},{5,6},{6,5},{9,10},{10,9},{13,14},{14,13},{17,18},{18,... | collective-permute-start | bytes 786440 | tf_op jit(solution)/shard_map/ppermute | solution.py:549
  78.3 2.6 %shard_map.119.refs_5_ = f32[2,64,128]{2,1,0:T(8,128)S(1)} custom-call(s32[320]{0:T(512)S(1)} %fusion.9.tabs, f32[4,128,128]{2,1,0:T(8,128)S(1)} %pad_maximum_fusion.3.patch_ref), custom_call_target="tpu_custom_call" | custom-call | flops 655360 | bytes 10485760 | tf_op jit(solution)/shard_map/pallas_call | solution.py:472
  81.0 1.9 %collective-permute-done.19.refs_4_ = f32[4,128,128]{2,1,0:T(8,128)S(1)} collective-permute-done((f32[4,128,128]{2,1,0:T(8,128)S(1)}, f32[4,128,128]{2,1,0:T(8,128)S(1)}, u32[]{:S(2)}, u32[]{:S(2)}) %collective-permute-start.19) | collective-permute-done | bytes 262176 | tf_op jit(solution)/shard_map/ppermute | solution.py:549
  82.9 3.6 %shard_map.120 = (f32[3,32,128]{2,1,0:T(8,128)}, f32[9,32,128]{2,1,0:T(8,128)}, f32[9,32,128]{2,1,0:T(8,128)}) custom-call(s32[320]{0:T(512)S(1)} %get-tuple-element.63.refs_0_, s32[608]{0:T(1024)S(1)} %get-tuple-element.34.refs_1_, s32[608]{0:T(1024)S(1)} %get-tuple-element.35.refs_2_, f32[4,128,128]{2,1,0:T(8,128)S(1)} %collective-permute-done.18.refs_3_, ...), custom_call_target="tpu_custom_call" | custom-call | tf_op jit(solution)/shard_map/pallas_call | solution.py:523
  (57 shorter events, 2.4 us)
Async XLA Ops:
  3.0 6.0 %collective-permute-start.2 = (f32[136,128]{1,0:T(8,128)S(1)}, f32[136,128]{1,0:T(8,128)S(1)}, u32[]{:S(2)}, u32[]{:S(2)}) collective-permute-start(f32[136,128]{1,0:T(8,128)S(1)} %get-tuple-element.27), channel_id=1, source_target_pairs={{0,12},{4,8},{8,4},{12,0},{1,13},{5,9},{9,5},{13,1},{2,14},{6,10},... | collective-permute-start | bytes 208904 | tf_op jit(solution)/shard_map/ppermute | solution.py:540
  7.2 5.9 %collective-permute-start.1 = (f32[136,128]{1,0:T(8,128)S(1)}, f32[136,128]{1,0:T(8,128)S(1)}, u32[]{:S(2)}, u32[]{:S(2)}) collective-permute-start(f32[136,128]{1,0:T(8,128)S(1)} %get-tuple-element.27), channel_id=1, source_target_pairs={{0,8},{4,12},{8,0},{12,4},{1,9},{5,13},{9,1},{13,5},{2,10},{6,14},... | collective-permute-start | bytes 208904 | tf_op jit(solution)/shard_map/ppermute | solution.py:540
  7.3 5.9 %collective-permute-start = (f32[136,128]{1,0:T(8,128)S(1)}, f32[136,128]{1,0:T(8,128)S(1)}, u32[]{:S(2)}, u32[]{:S(2)}) collective-permute-start(f32[136,128]{1,0:T(8,128)S(1)} %get-tuple-element.27), channel_id=1, source_target_pairs={{0,4},{4,0},{8,12},{12,8},{1,5},{5,1},{9,13},{13,9},{2,6},{6,2},{1... | collective-permute-start | bytes 208904 | tf_op jit(solution)/shard_map/ppermute | solution.py:540
  13.2 8.2 %collective-permute-start.4 = (f32[4,136,128]{2,1,0:T(8,128)S(1)}, f32[4,136,128]{2,1,0:T(8,128)S(1)}, u32[]{:S(2)}, u32[]{:S(2)}) collective-permute-start(f32[4,136,128]{2,1,0:T(8,128)S(1)} %pad_maximum_fusion.patch_ref), channel_id=1, source_target_pairs={{1,2},{2,1},{5,6},{6,5},{9,10},{10,9},{13,14},{14,13},{17,18},{18,... | collective-permute-start | bytes 835592 | tf_op jit(solution)/shard_map/ppermute | solution.py:549
  17.2 4.2 %collective-permute-start.3 = (f32[4,136,128]{2,1,0:T(8,128)S(1)}, f32[4,136,128]{2,1,0:T(8,128)S(1)}, u32[]{:S(2)}, u32[]{:S(2)}) collective-permute-start(f32[4,136,128]{2,1,0:T(8,128)S(1)} %pad_maximum_fusion.patch_ref), channel_id=1, source_target_pairs={{0,1},{1,0},{2,3},{3,2},{4,5},{5,4},{6,7},{7,6},{8,9},{9,8},{10,11... | collective-permute-start | bytes 835592 | tf_op jit(solution)/shard_map/ppermute | solution.py:549
  27.4 5.7 %collective-permute-start.7 = (f32[128,128]{1,0:T(8,128)S(1)}, f32[128,128]{1,0:T(8,128)S(1)}, u32[]{:S(2)}, u32[]{:S(2)}) collective-permute-start(f32[128,128]{1,0:T(8,128)S(1)} %get-tuple-element.36), channel_id=1, source_target_pairs={{0,12},{4,8},{8,4},{12,0},{1,13},{5,9},{9,5},{13,1},{2,14},{6,10},... | collective-permute-start | bytes 196616 | tf_op jit(solution)/shard_map/ppermute | solution.py:540
  29.9 6.3 %collective-permute-start.6 = (f32[128,128]{1,0:T(8,128)S(1)}, f32[128,128]{1,0:T(8,128)S(1)}, u32[]{:S(2)}, u32[]{:S(2)}) collective-permute-start(f32[128,128]{1,0:T(8,128)S(1)} %get-tuple-element.36), channel_id=1, source_target_pairs={{0,8},{4,12},{8,0},{12,4},{1,9},{5,13},{9,1},{13,5},{2,10},{6,14},... | collective-permute-start | bytes 196616 | tf_op jit(solution)/shard_map/ppermute | solution.py:540
  29.9 6.3 %collective-permute-start.5 = (f32[128,128]{1,0:T(8,128)S(1)}, f32[128,128]{1,0:T(8,128)S(1)}, u32[]{:S(2)}, u32[]{:S(2)}) collective-permute-start(f32[128,128]{1,0:T(8,128)S(1)} %get-tuple-element.36), channel_id=1, source_target_pairs={{0,4},{4,0},{8,12},{12,8},{1,5},{5,1},{9,13},{13,9},{2,6},{6,2},{1... | collective-permute-start | bytes 196616 | tf_op jit(solution)/shard_map/ppermute | solution.py:540
  36.3 7.7 %collective-permute-start.9 = (f32[4,128,128]{2,1,0:T(8,128)S(1)}, f32[4,128,128]{2,1,0:T(8,128)S(1)}, u32[]{:S(2)}, u32[]{:S(2)}) collective-permute-start(f32[4,128,128]{2,1,0:T(8,128)S(1)} %pad_maximum_fusion.1.patch_ref), channel_id=1, source_target_pairs={{1,2},{2,1},{5,6},{6,5},{9,10},{10,9},{13,14},{14,13},{17,18},{18,... | collective-permute-start | bytes 786440 | tf_op jit(solution)/shard_map/ppermute | solution.py:549
  39.1 4.9 %collective-permute-start.8 = (f32[4,128,128]{2,1,0:T(8,128)S(1)}, f32[4,128,128]{2,1,0:T(8,128)S(1)}, u32[]{:S(2)}, u32[]{:S(2)}) collective-permute-start(f32[4,128,128]{2,1,0:T(8,128)S(1)} %pad_maximum_fusion.1.patch_ref), channel_id=1, source_target_pairs={{0,1},{1,0},{2,3},{3,2},{4,5},{5,4},{6,7},{7,6},{8,9},{9,8},{10,11... | collective-permute-start | bytes 786440 | tf_op jit(solution)/shard_map/ppermute | solution.py:549
  48.0 5.5 %collective-permute-start.12 = (f32[128,128]{1,0:T(8,128)S(1)}, f32[128,128]{1,0:T(8,128)S(1)}, u32[]{:S(2)}, u32[]{:S(2)}) collective-permute-start(f32[128,128]{1,0:T(8,128)S(1)} %get-tuple-element.40), channel_id=1, source_target_pairs={{0,12},{4,8},{8,4},{12,0},{1,13},{5,9},{9,5},{13,1},{2,14},{6,10},... | collective-permute-start | bytes 196616 | tf_op jit(solution)/shard_map/ppermute | solution.py:540
  50.2 5.5 %collective-permute-start.11 = (f32[128,128]{1,0:T(8,128)S(1)}, f32[128,128]{1,0:T(8,128)S(1)}, u32[]{:S(2)}, u32[]{:S(2)}) collective-permute-start(f32[128,128]{1,0:T(8,128)S(1)} %get-tuple-element.40), channel_id=1, source_target_pairs={{0,8},{4,12},{8,0},{12,4},{1,9},{5,13},{9,1},{13,5},{2,10},{6,14},... | collective-permute-start | bytes 196616 | tf_op jit(solution)/shard_map/ppermute | solution.py:540
  50.2 5.5 %collective-permute-start.10 = (f32[128,128]{1,0:T(8,128)S(1)}, f32[128,128]{1,0:T(8,128)S(1)}, u32[]{:S(2)}, u32[]{:S(2)}) collective-permute-start(f32[128,128]{1,0:T(8,128)S(1)} %get-tuple-element.40), channel_id=1, source_target_pairs={{0,4},{4,0},{8,12},{12,8},{1,5},{5,1},{9,13},{13,9},{2,6},{6,2},{1... | collective-permute-start | bytes 196616 | tf_op jit(solution)/shard_map/ppermute | solution.py:540
  55.8 7.7 %collective-permute-start.14 = (f32[4,128,128]{2,1,0:T(8,128)S(1)}, f32[4,128,128]{2,1,0:T(8,128)S(1)}, u32[]{:S(2)}, u32[]{:S(2)}) collective-permute-start(f32[4,128,128]{2,1,0:T(8,128)S(1)} %pad_maximum_fusion.2.patch_ref), channel_id=1, source_target_pairs={{1,2},{2,1},{5,6},{6,5},{9,10},{10,9},{13,14},{14,13},{17,18},{18,... | collective-permute-start | bytes 786440 | tf_op jit(solution)/shard_map/ppermute | solution.py:549
  58.8 4.7 %collective-permute-start.13 = (f32[4,128,128]{2,1,0:T(8,128)S(1)}, f32[4,128,128]{2,1,0:T(8,128)S(1)}, u32[]{:S(2)}, u32[]{:S(2)}) collective-permute-start(f32[4,128,128]{2,1,0:T(8,128)S(1)} %pad_maximum_fusion.2.patch_ref), channel_id=1, source_target_pairs={{0,1},{1,0},{2,3},{3,2},{4,5},{5,4},{6,7},{7,6},{8,9},{9,8},{10,11... | collective-permute-start | bytes 786440 | tf_op jit(solution)/shard_map/ppermute | solution.py:549
  67.7 5.3 %collective-permute-start.17 = (f32[128,128]{1,0:T(8,128)S(1)}, f32[128,128]{1,0:T(8,128)S(1)}, u32[]{:S(2)}, u32[]{:S(2)}) collective-permute-start(f32[128,128]{1,0:T(8,128)S(1)} %get-tuple-element.44), channel_id=1, source_target_pairs={{0,12},{4,8},{8,4},{12,0},{1,13},{5,9},{9,5},{13,1},{2,14},{6,10},... | collective-permute-start | bytes 196616 | tf_op jit(solution)/shard_map/ppermute | solution.py:540
  69.5 5.6 %collective-permute-start.16 = (f32[128,128]{1,0:T(8,128)S(1)}, f32[128,128]{1,0:T(8,128)S(1)}, u32[]{:S(2)}, u32[]{:S(2)}) collective-permute-start(f32[128,128]{1,0:T(8,128)S(1)} %get-tuple-element.44), channel_id=1, source_target_pairs={{0,8},{4,12},{8,0},{12,4},{1,9},{5,13},{9,1},{13,5},{2,10},{6,14},... | collective-permute-start | bytes 196616 | tf_op jit(solution)/shard_map/ppermute | solution.py:540
  69.5 5.6 %collective-permute-start.15 = (f32[128,128]{1,0:T(8,128)S(1)}, f32[128,128]{1,0:T(8,128)S(1)}, u32[]{:S(2)}, u32[]{:S(2)}) collective-permute-start(f32[128,128]{1,0:T(8,128)S(1)} %get-tuple-element.44), channel_id=1, source_target_pairs={{0,4},{4,0},{8,12},{12,8},{1,5},{5,1},{9,13},{13,9},{2,6},{6,2},{1... | collective-permute-start | bytes 196616 | tf_op jit(solution)/shard_map/ppermute | solution.py:540
  75.2 7.7 %collective-permute-start.19 = (f32[4,128,128]{2,1,0:T(8,128)S(1)}, f32[4,128,128]{2,1,0:T(8,128)S(1)}, u32[]{:S(2)}, u32[]{:S(2)}) collective-permute-start(f32[4,128,128]{2,1,0:T(8,128)S(1)} %pad_maximum_fusion.3.patch_ref), channel_id=1, source_target_pairs={{1,2},{2,1},{5,6},{6,5},{9,10},{10,9},{13,14},{14,13},{17,18},{18,... | collective-permute-start | bytes 786440 | tf_op jit(solution)/shard_map/ppermute | solution.py:549
  78.3 4.6 %collective-permute-start.18 = (f32[4,128,128]{2,1,0:T(8,128)S(1)}, f32[4,128,128]{2,1,0:T(8,128)S(1)}, u32[]{:S(2)}, u32[]{:S(2)}) collective-permute-start(f32[4,128,128]{2,1,0:T(8,128)S(1)} %pad_maximum_fusion.3.patch_ref), channel_id=1, source_target_pairs={{0,1},{1,0},{2,3},{3,2},{4,5},{5,4},{6,7},{7,6},{8,9},{9,8},{10,11... | collective-permute-start | bytes 786440 | tf_op jit(solution)/shard_map/ppermute | solution.py:549

commit v6 on v5

--- a/solution.py
+++ b/solution.py
@@ -12,7 +12,7 @@
 SUBSTEPS = 4
 SPAN_Y = 26
 LOW_Y = 5
-AT_ONCE = 16
+AT_ONCE = 8
 ROWS_X = 4 * SPAN_Y
 
 time_step = 0.05

time: 86.8 us -> 87.9 us (1.013)
  Pallas kernels: 30.2 us -> 32 us
  waiting for transfers between devices: 25.1 us -> 23.8 us
  starting transfers between devices: 28.5 us -> 29.5 us
    pallas_call x5, Pallas kernels: 19.8 us -> 21.5 us  [run_kernel(): pl.pallas_call(functools.partial(kernel, first, listing, last), out_shape...]
    ppermute x8, waiting for transfers between devices: 6.48 us -> 5.44 us  [neighbour_of(): lax.ppermute(column, 'gy', pairs)]
    ppermute x8, starting transfers between devices: 13 us -> 14.1 us  [neighbour_of(): lax.ppermute(column, 'gy', pairs)]
where the time goes in v6:
time: 87.9 us; the launch traced here: 88 us
  Pallas kernels  32 us (36%)
  starting transfers between devices  29.5 us (34%)
  waiting for transfers between devices  23.8 us (27%)
  local copies, waits for them, and re-layouts  1.23 us (1%)
  between operations  0.9 us (1%)
    pallas_call x5, Pallas kernels, run_kernel(): pl.pallas_call(functools.partial(kernel, first, listing, last), out_shape...  21.5 us
    ppermute x12, waiting for transfers between devices, column_of(): pieces.append(lax.ppermute(payload, 'gx', pairs))  18.4 us
    ppermute x12, starting transfers between devices, column_of(): pieces.append(lax.ppermute(payload, 'gx', pairs))  15.4 us
    ppermute x8, starting transfers between devices, neighbour_of(): lax.ppermute(column, 'gy', pairs)  14.1 us
    pallas_call x4, Pallas kernels, run_column(): pl.pallas_call(functools.partial(column_kernel, bins), out_shape=shape_of...  10.5 us
    ppermute x8, waiting for transfers between devices, neighbour_of(): lax.ppermute(column, 'gy', pairs)  5.44 us
  transfers between devices with their start and end apart: 20, of which 12 were waited for; matrix products, arithmetic and copies ran while one was open for 1% of the time, Pallas kernels for 12%

profile of v6, /device:TPU:1, one launch (start us, length us, event | category | flops | bytes accessed | tf_op | source)
XLA Modules:
  0.0 88.0 jit_solution(314978126309999822)
XLA Ops:
  0.6 2.4 %shard_map.112 = (f32[136,128]{1,0:T(8,128)S(1)}, f32[16,32,128]{2,1,0:T(8,128)S(1)}, f32[512,128]{1,0:T(8,128)S(1)}, bf16[2,384,256]{2,1,0:T(8,128)(2,1)S(1)}) custom-call(f32[3,32,128]{2,1,0:T(8,128)} %bitcast.48, s32[32,128]{1,0:T(8,128)} %refs_1_.1, f32[3,32,128]{2,1,0:T(8,128)} %bitcast.49, f32[9,32,128]{2,1,0:T(8,128)} %bitcast.34, ...), custom_call_target="tpu_custom_call" | custom-call | tf_op jit(solution)/shard_map/pallas_call | solution.py:523
  3.0 4.2 %collective-permute-start.2 = (f32[136,128]{1,0:T(8,128)S(1)}, f32[136,128]{1,0:T(8,128)S(1)}, u32[]{:S(2)}, u32[]{:S(2)}) collective-permute-start(f32[136,128]{1,0:T(8,128)S(1)} %get-tuple-element.27), channel_id=1, source_target_pairs={{0,12},{4,8},{8,4},{12,0},{1,13},{5,9},{9,5},{13,1},{2,14},{6,10},... | collective-permute-start | bytes 208904 | tf_op jit(solution)/shard_map/ppermute | solution.py:540
  7.3 0.4 collective-permute-start
  7.7 1.3 %collective-permute-done.2 = f32[136,128]{1,0:T(8,128)S(1)} collective-permute-done((f32[136,128]{1,0:T(8,128)S(1)}, f32[136,128]{1,0:T(8,128)S(1)}, u32[]{:S(2)}, u32[]{:S(2)}) %collective-permute-start.2) | collective-permute-done | bytes 69664 | tf_op jit(solution)/shard_map/ppermute | solution.py:540
  9.0 4.1 %collective-permute-done.1 = f32[136,128]{1,0:T(8,128)S(1)} collective-permute-done((f32[136,128]{1,0:T(8,128)S(1)}, f32[136,128]{1,0:T(8,128)S(1)}, u32[]{:S(2)}, u32[]{:S(2)}) %collective-permute-start.1) | collective-permute-done | bytes 69664 | tf_op jit(solution)/shard_map/ppermute | solution.py:540
  13.2 4.0 %collective-permute-start.4 = (f32[4,136,128]{2,1,0:T(8,128)S(1)}, f32[4,136,128]{2,1,0:T(8,128)S(1)}, u32[]{:S(2)}, u32[]{:S(2)}) collective-permute-start(f32[4,136,128]{2,1,0:T(8,128)S(1)} %pad_maximum_fusion.patch_ref), channel_id=1, source_target_pairs={{1,2},{2,1},{5,6},{6,5},{9,10},{10,9},{13,14},{14,13},{17,18},{18,... | collective-permute-start | bytes 835592 | tf_op jit(solution)/shard_map/ppermute | solution.py:549
  18.3 2.6 %shard_map.113.refs_4_ = f32[2,64,128]{2,1,0:T(8,128)S(1)} custom-call(s32[320]{0:T(512)S(1)} %fusion.9.tabs, f32[4,136,128]{2,1,0:T(8,128)S(1)} %pad_maximum_fusion.patch_ref), custom_call_target="tpu_custom_call" | custom-call | flops 696320 | bytes 11141120 | tf_op jit(solution)/shard_map/pallas_call | solution.py:472
  21.9 6.0 %shard_map.114 = (f32[128,128]{1,0:T(8,128)S(1)}, f32[16,32,128]{2,1,0:T(8,128)S(1)}, f32[512,128]{1,0:T(8,128)S(1)}, bf16[2,384,256]{2,1,0:T(8,128)(2,1)S(1)}, s32[576]{0:T(1024)S(1)}, /*index=5*/s32[576]{0:T(1024)S(1)}) custom-call(s32[320]{0:T(512)S(1)} %get-tuple-element.63.refs_0_, s32[320]{0:T(512)S(1)} %get-tuple-element.62.refs_1_, ...), custom_call_target="tpu_custom_call" | custom-call | tf_op jit(solution)/shard_map/pallas_call | solution.py:523
  27.9 2.5 %collective-permute-start.7 = (f32[128,128]{1,0:T(8,128)S(1)}, f32[128,128]{1,0:T(8,128)S(1)}, u32[]{:S(2)}, u32[]{:S(2)}) collective-permute-start(f32[128,128]{1,0:T(8,128)S(1)} %get-tuple-element.36), channel_id=1, source_target_pairs={{0,12},{4,8},{8,4},{12,0},{1,13},{5,9},{9,5},{13,1},{2,14},{6,10},... | collective-permute-start | bytes 196616 | tf_op jit(solution)/shard_map/ppermute | solution.py:540
  30.4 1.1 %collective-permute-start.5 = (f32[128,128]{1,0:T(8,128)S(1)}, f32[128,128]{1,0:T(8,128)S(1)}, u32[]{:S(2)}, u32[]{:S(2)}) collective-permute-start(f32[128,128]{1,0:T(8,128)S(1)} %get-tuple-element.36), channel_id=1, source_target_pairs={{0,4},{4,0},{8,12},{12,8},{1,5},{5,1},{9,13},{13,9},{2,6},{6,2},{1... | collective-permute-start | bytes 196616 | tf_op jit(solution)/shard_map/ppermute | solution.py:540
  31.6 2.1 %collective-permute-done.7 = f32[128,128]{1,0:T(8,128)S(1)} collective-permute-done((f32[128,128]{1,0:T(8,128)S(1)}, f32[128,128]{1,0:T(8,128)S(1)}, u32[]{:S(2)}, u32[]{:S(2)}) %collective-permute-start.7) | collective-permute-done | bytes 65568 | tf_op jit(solution)/shard_map/ppermute | solution.py:540
  33.6 2.8 %collective-permute-done.6 = f32[128,128]{1,0:T(8,128)S(1)} collective-permute-done((f32[128,128]{1,0:T(8,128)S(1)}, f32[128,128]{1,0:T(8,128)S(1)}, u32[]{:S(2)}, u32[]{:S(2)}) %collective-permute-start.6) | collective-permute-done | bytes 65568 | tf_op jit(solution)/shard_map/ppermute | solution.py:540
  36.4 3.1 %collective-permute-start.9 = (f32[4,128,128]{2,1,0:T(8,128)S(1)}, f32[4,128,128]{2,1,0:T(8,128)S(1)}, u32[]{:S(2)}, u32[]{:S(2)}) collective-permute-start(f32[4,128,128]{2,1,0:T(8,128)S(1)} %pad_maximum_fusion.1.patch_ref), channel_id=1, source_target_pairs={{1,2},{2,1},{5,6},{6,5},{9,10},{10,9},{13,14},{14,13},{17,18},{18,... | collective-permute-start | bytes 786440 | tf_op jit(solution)/shard_map/ppermute | solution.py:549
  39.6 2.6 %shard_map.115.refs_5_ = f32[2,64,128]{2,1,0:T(8,128)S(1)} custom-call(s32[320]{0:T(512)S(1)} %fusion.9.tabs, f32[4,128,128]{2,1,0:T(8,128)S(1)} %pad_maximum_fusion.1.patch_ref), custom_call_target="tpu_custom_call" | custom-call | flops 655360 | bytes 10485760 | tf_op jit(solution)/shard_map/pallas_call | solution.py:472
  42.3 1.8 %collective-permute-done.9.refs_4_ = f32[4,128,128]{2,1,0:T(8,128)S(1)} collective-permute-done((f32[4,128,128]{2,1,0:T(8,128)S(1)}, f32[4,128,128]{2,1,0:T(8,128)S(1)}, u32[]{:S(2)}, u32[]{:S(2)}) %collective-permute-start.9) | collective-permute-done | bytes 262176 | tf_op jit(solution)/shard_map/ppermute | solution.py:549
  44.1 4.4 %shard_map.116 = (f32[128,128]{1,0:T(8,128)S(1)}, f32[16,32,128]{2,1,0:T(8,128)S(1)}, f32[512,128]{1,0:T(8,128)S(1)}, bf16[2,384,256]{2,1,0:T(8,128)(2,1)S(1)}) custom-call(s32[320]{0:T(512)S(1)} %get-tuple-element.63.refs_0_, s32[576]{0:T(1024)S(1)} %get-tuple-element.34.refs_1_, s32[576]{0:T(1024)S(1)} %get-tuple-element.35.refs_2_, ...), custom_call_target="tpu_custom_call" | custom-call | tf_op jit(solution)/shard_map/pallas_call | solution.py:523
  48.6 2.4 %collective-permute-start.12 = (f32[128,128]{1,0:T(8,128)S(1)}, f32[128,128]{1,0:T(8,128)S(1)}, u32[]{:S(2)}, u32[]{:S(2)}) collective-permute-start(f32[128,128]{1,0:T(8,128)S(1)} %get-tuple-element.40), channel_id=1, source_target_pairs={{0,12},{4,8},{8,4},{12,0},{1,13},{5,9},{9,5},{13,1},{2,14},{6,10},... | collective-permute-start | bytes 196616 | tf_op jit(solution)/shard_map/ppermute | solution.py:540
  51.0 1.2 %collective-permute-start.10 = (f32[128,128]{1,0:T(8,128)S(1)}, f32[128,128]{1,0:T(8,128)S(1)}, u32[]{:S(2)}, u32[]{:S(2)}) collective-permute-start(f32[128,128]{1,0:T(8,128)S(1)} %get-tuple-element.40), channel_id=1, source_target_pairs={{0,4},{4,0},{8,12},{12,8},{1,5},{5,1},{9,13},{13,9},{2,6},{6,2},{1... | collective-permute-start | bytes 196616 | tf_op jit(solution)/shard_map/ppermute | solution.py:540
  52.2 1.7 %collective-permute-done.12 = f32[128,128]{1,0:T(8,128)S(1)} collective-permute-done((f32[128,128]{1,0:T(8,128)S(1)}, f32[128,128]{1,0:T(8,128)S(1)}, u32[]{:S(2)}, u32[]{:S(2)}) %collective-permute-start.12) | collective-permute-done | bytes 65568 | tf_op jit(solution)/shard_map/ppermute | solution.py:540
  53.9 2.4 %collective-permute-done.11 = f32[128,128]{1,0:T(8,128)S(1)} collective-permute-done((f32[128,128]{1,0:T(8,128)S(1)}, f32[128,128]{1,0:T(8,128)S(1)}, u32[]{:S(2)}, u32[]{:S(2)}) %collective-permute-start.11) | collective-permute-done | bytes 65568 | tf_op jit(solution)/shard_map/ppermute | solution.py:540
  56.3 3.4 %collective-permute-start.14 = (f32[4,128,128]{2,1,0:T(8,128)S(1)}, f32[4,128,128]{2,1,0:T(8,128)S(1)}, u32[]{:S(2)}, u32[]{:S(2)}) collective-permute-start(f32[4,128,128]{2,1,0:T(8,128)S(1)} %pad_maximum_fusion.2.patch_ref), channel_id=1, source_target_pairs={{1,2},{2,1},{5,6},{6,5},{9,10},{10,9},{13,14},{14,13},{17,18},{18,... | collective-permute-start | bytes 786440 | tf_op jit(solution)/shard_map/ppermute | solution.py:549
  59.8 2.6 %shard_map.117.refs_5_ = f32[2,64,128]{2,1,0:T(8,128)S(1)} custom-call(s32[320]{0:T(512)S(1)} %fusion.9.tabs, f32[4,128,128]{2,1,0:T(8,128)S(1)} %pad_maximum_fusion.2.patch_ref), custom_call_target="tpu_custom_call" | custom-call | flops 655360 | bytes 10485760 | tf_op jit(solution)/shard_map/pallas_call | solution.py:472
  62.4 1.6 %collective-permute-done.14.refs_4_ = f32[4,128,128]{2,1,0:T(8,128)S(1)} collective-permute-done((f32[4,128,128]{2,1,0:T(8,128)S(1)}, f32[4,128,128]{2,1,0:T(8,128)S(1)}, u32[]{:S(2)}, u32[]{:S(2)}) %collective-permute-start.14) | collective-permute-done | bytes 262176 | tf_op jit(solution)/shard_map/ppermute | solution.py:549
  64.0 4.6 %shard_map.118 = (f32[128,128]{1,0:T(8,128)S(1)}, f32[16,32,128]{2,1,0:T(8,128)S(1)}, f32[512,128]{1,0:T(8,128)S(1)}, bf16[2,384,256]{2,1,0:T(8,128)(2,1)S(1)}) custom-call(s32[320]{0:T(512)S(1)} %get-tuple-element.63.refs_0_, s32[576]{0:T(1024)S(1)} %get-tuple-element.34.refs_1_, s32[576]{0:T(1024)S(1)} %get-tuple-element.35.refs_2_, ...), custom_call_target="tpu_custom_call" | custom-call | tf_op jit(solution)/shard_map/pallas_call | solution.py:523
  68.6 1.9 %collective-permute-start.17 = (f32[128,128]{1,0:T(8,128)S(1)}, f32[128,128]{1,0:T(8,128)S(1)}, u32[]{:S(2)}, u32[]{:S(2)}) collective-permute-start(f32[128,128]{1,0:T(8,128)S(1)} %get-tuple-element.44), channel_id=1, source_target_pairs={{0,12},{4,8},{8,4},{12,0},{1,13},{5,9},{9,5},{13,1},{2,14},{6,10},... | collective-permute-start | bytes 196616 | tf_op jit(solution)/shard_map/ppermute | solution.py:540
  70.5 1.7 %collective-permute-start.15 = (f32[128,128]{1,0:T(8,128)S(1)}, f32[128,128]{1,0:T(8,128)S(1)}, u32[]{:S(2)}, u32[]{:S(2)}) collective-permute-start(f32[128,128]{1,0:T(8,128)S(1)} %get-tuple-element.44), channel_id=1, source_target_pairs={{0,4},{4,0},{8,12},{12,8},{1,5},{5,1},{9,13},{13,9},{2,6},{6,2},{1... | collective-permute-start | bytes 196616 | tf_op jit(solution)/shard_map/ppermute | solution.py:540
  72.3 1.6 %collective-permute-done.17 = f32[128,128]{1,0:T(8,128)S(1)} collective-permute-done((f32[128,128]{1,0:T(8,128)S(1)}, f32[128,128]{1,0:T(8,128)S(1)}, u32[]{:S(2)}, u32[]{:S(2)}) %collective-permute-start.17) | collective-permute-done | bytes 65568 | tf_op jit(solution)/shard_map/ppermute | solution.py:540
  73.9 2.4 %collective-permute-done.16 = f32[128,128]{1,0:T(8,128)S(1)} collective-permute-done((f32[128,128]{1,0:T(8,128)S(1)}, f32[128,128]{1,0:T(8,128)S(1)}, u32[]{:S(2)}, u32[]{:S(2)}) %collective-permute-start.16) | collective-permute-done | bytes 65568 | tf_op jit(solution)/shard_map/ppermute | solution.py:540
  76.3 3.3 %collective-permute-start.19 = (f32[4,128,128]{2,1,0:T(8,128)S(1)}, f32[4,128,128]{2,1,0:T(8,128)S(1)}, u32[]{:S(2)}, u32[]{:S(2)}) collective-permute-start(f32[4,128,128]{2,1,0:T(8,128)S(1)} %pad_maximum_fusion.3.patch_ref), channel_id=1, source_target_pairs={{1,2},{2,1},{5,6},{6,5},{9,10},{10,9},{13,14},{14,13},{17,18},{18,... | collective-permute-start | bytes 786440 | tf_op jit(solution)/shard_map/ppermute | solution.py:549
  79.7 2.6 %shard_map.119.refs_5_ = f32[2,64,128]{2,1,0:T(8,128)S(1)} custom-call(s32[320]{0:T(512)S(1)} %fusion.9.tabs, f32[4,128,128]{2,1,0:T(8,128)S(1)} %pad_maximum_fusion.3.patch_ref), custom_call_target="tpu_custom_call" | custom-call | flops 655360 | bytes 10485760 | tf_op jit(solution)/shard_map/pallas_call | solution.py:472
  82.3 1.7 %collective-permute-done.19.refs_4_ = f32[4,128,128]{2,1,0:T(8,128)S(1)} collective-permute-done((f32[4,128,128]{2,1,0:T(8,128)S(1)}, f32[4,128,128]{2,1,0:T(8,128)S(1)}, u32[]{:S(2)}, u32[]{:S(2)}) %collective-permute-start.19) | collective-permute-done | bytes 262176 | tf_op jit(solution)/shard_map/ppermute | solution.py:549
  84.0 4.0 %shard_map.120 = (f32[3,32,128]{2,1,0:T(8,128)}, f32[9,32,128]{2,1,0:T(8,128)}, f32[9,32,128]{2,1,0:T(8,128)}) custom-call(s32[320]{0:T(512)S(1)} %get-tuple-element.63.refs_0_, s32[576]{0:T(1024)S(1)} %get-tuple-element.34.refs_1_, s32[576]{0:T(1024)S(1)} %get-tuple-element.35.refs_2_, f32[4,128,128]{2,1,0:T(8,128)S(1)} %collective-permute-done.18.refs_3_, ...), custom_call_target="tpu_custom_call" | custom-call | tf_op jit(solution)/shard_map/pallas_call | solution.py:523
  (57 shorter events, 2.4 us)
Async XLA Ops:
  3.0 6.0 %collective-permute-start.2 = (f32[136,128]{1,0:T(8,128)S(1)}, f32[136,128]{1,0:T(8,128)S(1)}, u32[]{:S(2)}, u32[]{:S(2)}) collective-permute-start(f32[136,128]{1,0:T(8,128)S(1)} %get-tuple-element.27), channel_id=1, source_target_pairs={{0,12},{4,8},{8,4},{12,0},{1,13},{5,9},{9,5},{13,1},{2,14},{6,10},... | collective-permute-start | bytes 208904 | tf_op jit(solution)/shard_map/ppermute | solution.py:540
  7.2 5.9 %collective-permute-start.1 = (f32[136,128]{1,0:T(8,128)S(1)}, f32[136,128]{1,0:T(8,128)S(1)}, u32[]{:S(2)}, u32[]{:S(2)}) collective-permute-start(f32[136,128]{1,0:T(8,128)S(1)} %get-tuple-element.27), channel_id=1, source_target_pairs={{0,8},{4,12},{8,0},{12,4},{1,9},{5,13},{9,1},{13,5},{2,10},{6,14},... | collective-permute-start | bytes 208904 | tf_op jit(solution)/shard_map/ppermute | solution.py:540
  7.3 5.9 %collective-permute-start = (f32[136,128]{1,0:T(8,128)S(1)}, f32[136,128]{1,0:T(8,128)S(1)}, u32[]{:S(2)}, u32[]{:S(2)}) collective-permute-start(f32[136,128]{1,0:T(8,128)S(1)} %get-tuple-element.27), channel_id=1, source_target_pairs={{0,4},{4,0},{8,12},{12,8},{1,5},{5,1},{9,13},{13,9},{2,6},{6,2},{1... | collective-permute-start | bytes 208904 | tf_op jit(solution)/shard_map/ppermute | solution.py:540
  13.2 8.2 %collective-permute-start.4 = (f32[4,136,128]{2,1,0:T(8,128)S(1)}, f32[4,136,128]{2,1,0:T(8,128)S(1)}, u32[]{:S(2)}, u32[]{:S(2)}) collective-permute-start(f32[4,136,128]{2,1,0:T(8,128)S(1)} %pad_maximum_fusion.patch_ref), channel_id=1, source_target_pairs={{1,2},{2,1},{5,6},{6,5},{9,10},{10,9},{13,14},{14,13},{17,18},{18,... | collective-permute-start | bytes 835592 | tf_op jit(solution)/shard_map/ppermute | solution.py:549
  17.2 4.2 %collective-permute-start.3 = (f32[4,136,128]{2,1,0:T(8,128)S(1)}, f32[4,136,128]{2,1,0:T(8,128)S(1)}, u32[]{:S(2)}, u32[]{:S(2)}) collective-permute-start(f32[4,136,128]{2,1,0:T(8,128)S(1)} %pad_maximum_fusion.patch_ref), channel_id=1, source_target_pairs={{0,1},{1,0},{2,3},{3,2},{4,5},{5,4},{6,7},{7,6},{8,9},{9,8},{10,11... | collective-permute-start | bytes 835592 | tf_op jit(solution)/shard_map/ppermute | solution.py:549
  27.9 5.7 %collective-permute-start.7 = (f32[128,128]{1,0:T(8,128)S(1)}, f32[128,128]{1,0:T(8,128)S(1)}, u32[]{:S(2)}, u32[]{:S(2)}) collective-permute-start(f32[128,128]{1,0:T(8,128)S(1)} %get-tuple-element.36), channel_id=1, source_target_pairs={{0,12},{4,8},{8,4},{12,0},{1,13},{5,9},{9,5},{13,1},{2,14},{6,10},... | collective-permute-start | bytes 196616 | tf_op jit(solution)/shard_map/ppermute | solution.py:540
  30.4 5.9 %collective-permute-start.6 = (f32[128,128]{1,0:T(8,128)S(1)}, f32[128,128]{1,0:T(8,128)S(1)}, u32[]{:S(2)}, u32[]{:S(2)}) collective-permute-start(f32[128,128]{1,0:T(8,128)S(1)} %get-tuple-element.36), channel_id=1, source_target_pairs={{0,8},{4,12},{8,0},{12,4},{1,9},{5,13},{9,1},{13,5},{2,10},{6,14},... | collective-permute-start | bytes 196616 | tf_op jit(solution)/shard_map/ppermute | solution.py:540
  30.4 5.9 %collective-permute-start.5 = (f32[128,128]{1,0:T(8,128)S(1)}, f32[128,128]{1,0:T(8,128)S(1)}, u32[]{:S(2)}, u32[]{:S(2)}) collective-permute-start(f32[128,128]{1,0:T(8,128)S(1)} %get-tuple-element.36), channel_id=1, source_target_pairs={{0,4},{4,0},{8,12},{12,8},{1,5},{5,1},{9,13},{13,9},{2,6},{6,2},{1... | collective-permute-start | bytes 196616 | tf_op jit(solution)/shard_map/ppermute | solution.py:540
  36.4 7.7 %collective-permute-start.9 = (f32[4,128,128]{2,1,0:T(8,128)S(1)}, f32[4,128,128]{2,1,0:T(8,128)S(1)}, u32[]{:S(2)}, u32[]{:S(2)}) collective-permute-start(f32[4,128,128]{2,1,0:T(8,128)S(1)} %pad_maximum_fusion.1.patch_ref), channel_id=1, source_target_pairs={{1,2},{2,1},{5,6},{6,5},{9,10},{10,9},{13,14},{14,13},{17,18},{18,... | collective-permute-start | bytes 786440 | tf_op jit(solution)/shard_map/ppermute | solution.py:549
  39.6 4.5 %collective-permute-start.8 = (f32[4,128,128]{2,1,0:T(8,128)S(1)}, f32[4,128,128]{2,1,0:T(8,128)S(1)}, u32[]{:S(2)}, u32[]{:S(2)}) collective-permute-start(f32[4,128,128]{2,1,0:T(8,128)S(1)} %pad_maximum_fusion.1.patch_ref), channel_id=1, source_target_pairs={{0,1},{1,0},{2,3},{3,2},{4,5},{5,4},{6,7},{7,6},{8,9},{9,8},{10,11... | collective-permute-start | bytes 786440 | tf_op jit(solution)/shard_map/ppermute | solution.py:549
  48.6 5.4 %collective-permute-start.12 = (f32[128,128]{1,0:T(8,128)S(1)}, f32[128,128]{1,0:T(8,128)S(1)}, u32[]{:S(2)}, u32[]{:S(2)}) collective-permute-start(f32[128,128]{1,0:T(8,128)S(1)} %get-tuple-element.40), channel_id=1, source_target_pairs={{0,12},{4,8},{8,4},{12,0},{1,13},{5,9},{9,5},{13,1},{2,14},{6,10},... | collective-permute-start | bytes 196616 | tf_op jit(solution)/shard_map/ppermute | solution.py:540
  51.0 5.3 %collective-permute-start.11 = (f32[128,128]{1,0:T(8,128)S(1)}, f32[128,128]{1,0:T(8,128)S(1)}, u32[]{:S(2)}, u32[]{:S(2)}) collective-permute-start(f32[128,128]{1,0:T(8,128)S(1)} %get-tuple-element.40), channel_id=1, source_target_pairs={{0,8},{4,12},{8,0},{12,4},{1,9},{5,13},{9,1},{13,5},{2,10},{6,14},... | collective-permute-start | bytes 196616 | tf_op jit(solution)/shard_map/ppermute | solution.py:540
  51.0 5.3 %collective-permute-start.10 = (f32[128,128]{1,0:T(8,128)S(1)}, f32[128,128]{1,0:T(8,128)S(1)}, u32[]{:S(2)}, u32[]{:S(2)}) collective-permute-start(f32[128,128]{1,0:T(8,128)S(1)} %get-tuple-element.40), channel_id=1, source_target_pairs={{0,4},{4,0},{8,12},{12,8},{1,5},{5,1},{9,13},{13,9},{2,6},{6,2},{1... | collective-permute-start | bytes 196616 | tf_op jit(solution)/shard_map/ppermute | solution.py:540
  56.3 7.7 %collective-permute-start.14 = (f32[4,128,128]{2,1,0:T(8,128)S(1)}, f32[4,128,128]{2,1,0:T(8,128)S(1)}, u32[]{:S(2)}, u32[]{:S(2)}) collective-permute-start(f32[4,128,128]{2,1,0:T(8,128)S(1)} %pad_maximum_fusion.2.patch_ref), channel_id=1, source_target_pairs={{1,2},{2,1},{5,6},{6,5},{9,10},{10,9},{13,14},{14,13},{17,18},{18,... | collective-permute-start | bytes 786440 | tf_op jit(solution)/shard_map/ppermute | solution.py:549
  59.7 4.3 %collective-permute-start.13 = (f32[4,128,128]{2,1,0:T(8,128)S(1)}, f32[4,128,128]{2,1,0:T(8,128)S(1)}, u32[]{:S(2)}, u32[]{:S(2)}) collective-permute-start(f32[4,128,128]{2,1,0:T(8,128)S(1)} %pad_maximum_fusion.2.patch_ref), channel_id=1, source_target_pairs={{0,1},{1,0},{2,3},{3,2},{4,5},{5,4},{6,7},{7,6},{8,9},{9,8},{10,11... | collective-permute-start | bytes 786440 | tf_op jit(solution)/shard_map/ppermute | solution.py:549
  68.6 5.2 %collective-permute-start.17 = (f32[128,128]{1,0:T(8,128)S(1)}, f32[128,128]{1,0:T(8,128)S(1)}, u32[]{:S(2)}, u32[]{:S(2)}) collective-permute-start(f32[128,128]{1,0:T(8,128)S(1)} %get-tuple-element.44), channel_id=1, source_target_pairs={{0,12},{4,8},{8,4},{12,0},{1,13},{5,9},{9,5},{13,1},{2,14},{6,10},... | collective-permute-start | bytes 196616 | tf_op jit(solution)/shard_map/ppermute | solution.py:540
  70.5 5.7 %collective-permute-start.16 = (f32[128,128]{1,0:T(8,128)S(1)}, f32[128,128]{1,0:T(8,128)S(1)}, u32[]{:S(2)}, u32[]{:S(2)}) collective-permute-start(f32[128,128]{1,0:T(8,128)S(1)} %get-tuple-element.44), channel_id=1, source_target_pairs={{0,8},{4,12},{8,0},{12,4},{1,9},{5,13},{9,1},{13,5},{2,10},{6,14},... | collective-permute-start | bytes 196616 | tf_op jit(solution)/shard_map/ppermute | solution.py:540
  70.5 5.7 %collective-permute-start.15 = (f32[128,128]{1,0:T(8,128)S(1)}, f32[128,128]{1,0:T(8,128)S(1)}, u32[]{:S(2)}, u32[]{:S(2)}) collective-permute-start(f32[128,128]{1,0:T(8,128)S(1)} %get-tuple-element.44), channel_id=1, source_target_pairs={{0,4},{4,0},{8,12},{12,8},{1,5},{5,1},{9,13},{13,9},{2,6},{6,2},{1... | collective-permute-start | bytes 196616 | tf_op jit(solution)/shard_map/ppermute | solution.py:540
  76.3 7.7 %collective-permute-start.19 = (f32[4,128,128]{2,1,0:T(8,128)S(1)}, f32[4,128,128]{2,1,0:T(8,128)S(1)}, u32[]{:S(2)}, u32[]{:S(2)}) collective-permute-start(f32[4,128,128]{2,1,0:T(8,128)S(1)} %pad_maximum_fusion.3.patch_ref), channel_id=1, source_target_pairs={{1,2},{2,1},{5,6},{6,5},{9,10},{10,9},{13,14},{14,13},{17,18},{18,... | collective-permute-start | bytes 786440 | tf_op jit(solution)/shard_map/ppermute | solution.py:549
  79.6 4.4 %collective-permute-start.18 = (f32[4,128,128]{2,1,0:T(8,128)S(1)}, f32[4,128,128]{2,1,0:T(8,128)S(1)}, u32[]{:S(2)}, u32[]{:S(2)}) collective-permute-start(f32[4,128,128]{2,1,0:T(8,128)S(1)} %pad_maximum_fusion.3.patch_ref), channel_id=1, source_target_pairs={{0,1},{1,0},{2,3},{3,2},{4,5},{5,4},{6,7},{7,6},{8,9},{9,8},{10,11... | collective-permute-start | bytes 786440 | tf_op jit(solution)/shard_map/ppermute | solution.py:549
